TPU v7x, 32 devices: a whole 2x2x4 slice. The times are simulated.
32 devices in a mesh: dom: 4 (over y, core), head: 8 (over z, x).
Axes of the slice: x: 2, y: 2, z: 4, core: 2. Of those that a mesh axis runs over, the one named last changes fastest.
Arguments:
- atoms: bfloat16 [4, 8192, 1024], P('dom', 'head'), may hold values from -6 to 6
- bonds: int32 [4, 4, 8192], P('dom', None, 'head'), may hold values from 0 to 1279
- triplets: int32 [4, 4, 8192], P('dom', None, 'head'), may hold values from 0 to 1279
- halo_ids: int32 [4, 1024], P('dom', 'head'), may hold values from 0 to 1023
- counts: int32 [4, 64], P('dom', 'head'), may hold values from 0 to 256, as said below
- enc_weight: bfloat16 [1024, 1024], replicated, may hold values from -0.1875 to 0.1875
- gate_gain: float32 [1024], replicated, may hold values from -8 to 8
- head_weight: bfloat16 [8, 2, 1024, 1024], P('head', None, 'dom'), may hold values from -0.1875 to 0.1875
Outputs:
- row_grads: bfloat16 [4, 8192, 1024], P('dom', 'head')
- head_grads: float32 [8, 2, 1024, 1024], P('head', None, 'dom')
Inputs may be any that keep to these rules, and one draw needn't show every extreme that they name: `counts`: each entry is a multiple of 128 and at most 256, reached on some device in every draw; the 8 entries of one device sum to 1024; within one partition the entries of one dataset sum to at most 2048, and some dataset reaches that in every partition. `bonds`: entry (b, i) names a row of atom i's device's extended rows: its own 1024 rows, then the cut-bond rows of the previous partition, then those of the next. `triplets`: indexed like bonds. `halo_ids`: rows of the device itself.
All inputs are finite; a program needn't handle non-finite values.
Results may differ from a plain program's by a relative error of at most 0.0095.
Values may be sent and summed in bfloat16 or wider, within the bound.
No kernel may reach another device: no remote copies, remote signals or barrier semaphores. Data moves between devices by JAX's collectives and lax.ppermute only.
A program may use at most 128 MiB of HBM per device.

v0:
```python
import math

import jax
import jax.numpy as jnp
from jax import lax
from jax.sharding import PartitionSpec as P

BLOCK = 128
SLOTS = 2
MOST_BLOCKS = 16


def padded(block, sides, width):
    for axis, dim in sides:
        count = lax.axis_size(axis)
        forward = [(i, i + 1) for i in range(count - 1)]
        backward = [(target, source) for source, target in forward]
        low = lax.ppermute(
            lax.slice_in_dim(block, block.shape[dim] - width, None, axis=dim), axis, forward
        )
        high = lax.ppermute(lax.slice_in_dim(block, 0, width, axis=dim), axis, backward)
        block = jnp.concatenate([low, block, high], axis=dim)
    return block


def encode_rows(extended, atom_rows, bond_ids, partner_ids, enc_weight, gate_gain):
    bonded = jnp.take(extended, bond_ids, axis=0)
    partner = jnp.take(extended, partner_ids, axis=0)
    logits = jnp.sum(
        bonded.astype(jnp.float32) * partner.astype(jnp.float32) * gate_gain, axis=-1
    ) / math.sqrt(extended.shape[1])
    gates = jax.nn.sigmoid(logits)
    message = jnp.sum(gates[..., None] * bonded.astype(jnp.float32), axis=0).astype(jnp.bfloat16)
    update = jnp.dot(message, enc_weight, preferred_element_type=jnp.float32)
    return (atom_rows.astype(jnp.float32) + jax.nn.silu(update)).astype(jnp.bfloat16)


def silu_slope(preact):
    sigma = jax.nn.sigmoid(preact)
    return sigma * (1.0 + preact * (1.0 - sigma))


def body(atoms, bonds, triplets, halo_ids, counts, enc_weight, gate_gain, head_weight):
    atom_rows = atoms[0]
    row_count = atom_rows.shape[0]
    width = atom_rows.shape[1]
    cut_rows = jnp.take(atom_rows, halo_ids[0], axis=0)
    depth = cut_rows.shape[0]
    edged = padded(cut_rows, (("dom", 0),), depth)
    extended = jnp.concatenate([atom_rows, edged[:depth], edged[2 * depth :]], axis=0)
    features = encode_rows(extended, atom_rows, bonds[0], triplets[0], enc_weight, gate_gain)
    block_total = row_count // BLOCK
    set_count = counts.shape[1]
    own_blocks = counts[0] // BLOCK
    own_incl = jnp.cumsum(own_blocks)
    own_excl = own_incl - own_blocks
    slot_ids = jnp.arange(set_count * SLOTS, dtype=jnp.int32)
    slot_rank = slot_ids % SLOTS
    source_block = jnp.repeat(own_excl, SLOTS) + slot_rank
    slot_live = slot_rank < jnp.repeat(own_blocks, SLOTS)
    feature_blocks = features.reshape(block_total, BLOCK, width)
    picked = jnp.take(feature_blocks, jnp.clip(source_block, 0, block_total - 1), axis=0)
    packed = jnp.where(slot_live[:, None, None], picked, jnp.zeros_like(picked)).reshape(
        set_count, SLOTS * BLOCK, width
    )
    all_counts = lax.all_gather(counts, "head", axis=0, tiled=True)
    arrived = lax.all_to_all(packed, "head", split_axis=0, concat_axis=0, tiled=True)
    group_size = arrived.shape[0]
    my_set = lax.axis_index("head")
    from_each = (
        jnp.sum(
            jnp.where(jnp.arange(set_count, dtype=jnp.int32)[None, :] == my_set, all_counts, 0),
            axis=1,
        )
        // BLOCK
    )
    src_incl = jnp.cumsum(from_each)
    src_excl = src_incl - from_each
    targets = jnp.arange(MOST_BLOCKS, dtype=jnp.int32)
    source_of = jnp.clip(
        jnp.sum((src_incl[None, :] <= targets[:, None]).astype(jnp.int32), axis=1),
        0,
        group_size - 1,
    )
    rank_of = targets - jnp.take(src_excl, source_of)
    target_used = targets < src_incl[-1]
    arrived_blocks = arrived.reshape(group_size * SLOTS, BLOCK, width)
    gathered = jnp.take(
        arrived_blocks, jnp.clip(source_of * SLOTS + rank_of, 0, group_size * SLOTS - 1), axis=0
    )
    compact = jnp.where(target_used[:, None, None], gathered, jnp.zeros_like(gathered)).reshape(
        MOST_BLOCKS * BLOCK, width
    )
    weight_shard = head_weight[0]
    layers = weight_shard.shape[0]
    scale = 1.0 / math.sqrt(lax.axis_size("dom") * row_count)
    whole_weights = lax.all_gather(weight_shard, "dom", axis=1, tiled=True)
    activations = [compact]
    preacts = []
    current = compact
    for layer_id in range(layers):
        preact = jnp.dot(current, whole_weights[layer_id], preferred_element_type=jnp.float32)
        preacts.append(preact)
        if layer_id < layers - 1:
            current = jax.nn.silu(preact).astype(jnp.bfloat16)
            activations.append(current)
    residue = preacts[-1] - compact.astype(jnp.float32)
    gradient = residue.astype(jnp.bfloat16)
    shares = [None] * layers
    upward = residue
    for layer_id in reversed(range(layers)):
        activation = activations[layer_id]
        shares[layer_id] = lax.psum_scatter(
            (
                lax.dot_general(
                    activation,
                    gradient,
                    (((0,), (0,)), ((), ())),
                    preferred_element_type=jnp.float32,
                )
                * scale
            ).astype(jnp.bfloat16),
            "dom",
            scatter_dimension=0,
            tiled=True,
        ).astype(jnp.float32)
        upward = lax.dot_general(
            gradient,
            whole_weights[layer_id],
            (((1,), (1,)), ((), ())),
            preferred_element_type=jnp.float32,
        )
        if layer_id > 0:
            gradient = (upward * silu_slope(preacts[layer_id - 1])).astype(jnp.bfloat16)
    head_part = jnp.stack(shares)
    compact_grads = (upward - residue).astype(jnp.bfloat16).reshape(MOST_BLOCKS, BLOCK, width)
    return_ids = jnp.arange(group_size * SLOTS, dtype=jnp.int32)
    return_source = return_ids // SLOTS
    return_rank = return_ids % SLOTS
    return_target = jnp.take(src_excl, return_source) + return_rank
    return_live = return_rank < jnp.take(from_each, return_source)
    sending = jnp.take(compact_grads, jnp.clip(return_target, 0, MOST_BLOCKS - 1), axis=0)
    sending = jnp.where(return_live[:, None, None], sending, jnp.zeros_like(sending)).reshape(
        group_size, SLOTS * BLOCK, width
    )
    returned = lax.all_to_all(sending, "head", split_axis=0, concat_axis=0, tiled=True)
    returned_blocks = returned.reshape(set_count * SLOTS, BLOCK, width)
    block_ids = jnp.arange(block_total, dtype=jnp.int32)
    block_sets = jnp.sum((own_incl[None, :] <= block_ids[:, None]).astype(jnp.int32), axis=1)
    block_rank = block_ids - jnp.take(own_excl, block_sets)
    row_part = jnp.take(returned_blocks, block_sets * SLOTS + block_rank, axis=0).reshape(
        1, row_count, width
    )
    return (row_part, head_part[None])


def solution(mesh):
    return jax.shard_map(
        body,
        mesh=mesh,
        in_specs=(
            P("dom", "head", None),
            P("dom", None, "head"),
            P("dom", None, "head"),
            P("dom", "head"),
            P("dom", "head"),
            P(),
            P(),
            P("head", None, "dom", None),
        ),
        out_specs=(P("dom", "head", None), P("head", None, "dom", None)),
        check_vma=False,
    )
```

profile of v0, /device:TPU:0, one launch (start us, length us, event | category | flops | bytes accessed | tf_op | source)
XLA Modules:
  0.0 382.6 jit_solution(3333866704831230591)
XLA Ops:
  20.5 3.3 pad_maximum_fusion
  23.8 22.9 %gather_fusion.6 = bf16[4096,1024]{1,0:T(8,128)(2,1)} fusion(bf16[1280,1024]{1,0:T(8,128)(2,1)} %pad_maximum_fusion, s32[4096]{0:T(1024)S(1)} %bitcast_clamp_fusion), kind=kCustom, calls=%fused_computation.5.clone | custom fusion | bytes 16793600 | tf_op jit(solution)/shard_map/jit(_take)/gather | solution.py:28
  46.8 22.9 %gather_fusion.5 = bf16[4096,1024]{1,0:T(8,128)(2,1)} fusion(bf16[1280,1024]{1,0:T(8,128)(2,1)} %pad_maximum_fusion, s32[4096]{0:T(1024)S(1)} %bitcast_clamp_fusion.1), kind=kCustom, calls=%fused_computation.1.clone | custom fusion | bytes 16793600 | tf_op jit(solution)/shard_map/jit(_take)/gather | solution.py:27
  69.7 9.0 %fusion.1 = f32[4,1024]{1,0:T(4,128)S(1)} fusion(bf16[4,1024,1024]{2,1,0:T(8,128)(2,1)} %bitcast.131, f32[1024]{0:T(1024)S(1)} %copy-done.7, pred[4,1024]{1,0:T(4,128)(4,1)S(1)} %get-tuple-element.15, bf16[4,1024,1024]{2,1,0:T(8,128)(2,1)} %bitcast.129, pred[4,1024]{1,0:T(4,128)(4,1)S(1)} %get-tuple-element.16), kind=kLoop, calls=%fused_computation.14 | loop fusion | flops 29356032 | bytes 16805888 | tf_op jit(solution)/shard_map/reduce_sum | solution.py:29
  81.8 4.1 %add_convert_fusion = bf16[1024,1024]{1,0:T(8,128)(2,1)} fusion(bf16[1024,1024]{1,0:T(8,128)(2,1)S(1)} %copy-done, bf16[1024,1024]{1,0:T(8,128)(2,1)S(1)} %fusion.2, bf16[1,1024,1024]{2,1,0:T(8,128)(2,1)S(1)} %copy-done.5), kind=kOutput, calls=%fused_computation.29 | convolution fusion | flops 2154823680 | bytes 8388608 | tf_op jit(solution)/shard_map/dot_general | solution.py:34
  86.0 4.4 %gather_fusion.2 = bf16[16,128,1024]{2,1,0:T(8,128)(2,1)} fusion(bf16[8,128,1024]{2,1,0:T(8,128)(2,1)} %bitcast.137, s32[1024]{0:T(1024)S(1)} %pad_clamp_fusion.3), kind=kCustom, calls=%fused_computation.9 | custom fusion | bytes 8388672 | tf_op jit(solution)/shard_map/jit(_take)/gather | solution.py:62
  90.3 4.0 %fusion.4 = bf16[8,256,1024]{2,1,0:T(8,128)(2,1)} fusion(pred[8,256]{1,0:T(8,128)(4,1)S(1)} %broadcast_bitcast_fusion, pred[8,256]{1,0:T(8,128)(4,1)S(1)} %broadcast_bitcast_fusion.1, bf16[8,256,1024]{2,1,0:T(8,128)(2,1)} %bitcast.133), kind=kLoop, calls=%fused_computation.24 | loop fusion | flops 4194304 | bytes 8392704 | tf_op jit(solution)/shard_map/jit(_where)/select_n | solution.py:63
  94.3 7.4 %all-to-all-start = ((bf16[8,256,1024]{2,1,0:T(8,128)(2,1)}), bf16[8,256,1024]{2,1,0:T(8,128)(2,1)}, u32[]{:S(2)}, u32[]{:S(2)}) async-start(bf16[8,256,1024]{2,1,0:T(8,128)(2,1)} %fusion.4), calls=%async_computation | async-start | bytes 8388608 | tf_op jit(solution)/shard_map/all_to_all | solution.py:67
  102.5 83.7 %all-gather.1 = s32[8,1,8]{2,1,0:T(1,128)S(1)} all-gather(s32[1,1,8]{2,1,0:T(1,128)S(1)} %bitcast.145), channel_id=1, replica_groups=mesh['dom'=4,'head'=8] {'head'}, dimensions={0}, use_global_device_ids=true | all-gather | bytes 288 | tf_op jit(solution)/shard_map/all_gather | solution.py:66
  190.0 6.5 %all-to-all-done = bf16[8,256,1024]{2,1,0:T(8,128)(2,1)} async-done(((bf16[8,256,1024]{2,1,0:T(8,128)(2,1)}), bf16[8,256,1024]{2,1,0:T(8,128)(2,1)}, u32[]{:S(2)}, u32[]{:S(2)}) %all-to-all-start) | async-done | bytes 4194336 | tf_op jit(solution)/shard_map/all_to_all | solution.py:67
  196.5 5.1 %gather_fusion.8 = bf16[16,128,1024]{2,1,0:T(8,128)(2,1)} fusion(bf16[16,128,1024]{2,1,0:T(8,128)(2,1)} %bitcast.24, s32[1024]{0:T(1024)S(1)} %pad_clamp_fusion.2), kind=kCustom, calls=%fused_computation.2.clone | custom fusion | bytes 8388672 | tf_op jit(solution)/shard_map/jit(_take)/gather | solution.py:88
  201.6 4.8 %select_select_fusion.1 = bf16[16,128,1024]{2,1,0:T(8,128)(2,1)} fusion(bf16[16,128,1024]{2,1,0:T(8,128)(2,1)} %gather_fusion.8, pred[16]{0:T(512)(128)(4,1)S(1)} %get-tuple-element.7, pred[16]{0:T(512)(128)(4,1)S(1)} %iota_compare_fusion.2), kind=kLoop, calls=%fused_computation.26 | loop fusion | flops 4194304 | bytes 8388640 | tf_op jit(solution)/shard_map/jit(_where)/select_n | solution.py:91
  206.4 7.1 %fusion.9 = f32[2048,1024]{1,0:T(8,128)S(1)} fusion(bf16[2048,1024]{1,0:T(8,128)(2,1)} %bitcast.138, bf16[1,2,1024,1024]{3,2,1,0:T(8,128)(2,1)} %all-gather.4.cloned.1.call-done), kind=kOutput, calls=%fused_computation.36 | convolution fusion | flops 4294967296 | bytes 14680064 | tf_op jit(solution)/shard_map/dot_general | solution.py:102
  213.5 7.9 %fusion.3 = (bf16[2048,1024]{1,0:T(8,128)(2,1)}, f32[2048,1024]{1,0:T(8,128)}) fusion(bf16[16,128,1024]{2,1,0:T(8,128)(2,1)S(1)} %copy-done.6, bf16[1,2,1024,1024]{3,2,1,0:T(8,128)(2,1)S(1)} %copy-done.11, f32[2048,1024]{1,0:T(8,128)S(1)} %fusion.9), kind=kOutput, calls=%fused_computation.22 | convolution fusion | flops 4311744512 | bytes 27262976 | tf_op jit(solution)/shard_map/dot_general | solution.py:102
  221.4 9.4 %multiply_convert_fusion = bf16[2048,1024]{1,0:T(8,128)(2,1)S(1)} fusion(f32[2048,1024]{1,0:T(8,128)S(1)} %fusion.9, bf16[2048,1024]{1,0:T(8,128)(2,1)} %get-tuple-element.13, bf16[1,2,1024,1024]{3,2,1,0:T(8,128)(2,1)S(1)} %copy-done.11), kind=kOutput, calls=%fused_computation.17 | convolution fusion | flops 4313841664 | bytes 18874368 | tf_op jit(solution)/shard_map/dot_general | solution.py:127
  232.8 5.7 %multiply_convert_fusion.3 = bf16[1024,1024]{1,0:T(8,128)(2,1)} fusion(bf16[2048,1024]{1,0:T(8,128)(2,1)S(1)} %bitcast.140, bf16[2048,1024]{1,0:T(8,128)(2,1)S(1)} %multiply_convert_fusion), kind=kOutput, calls=%fused_computation.28 | convolution fusion | flops 4297064448 | bytes 10485760 | tf_op jit(solution)/shard_map/dot_general | solution.py:115
  238.5 13.1 %subtract_convert_fusion = bf16[2048,1024]{1,0:T(8,128)(2,1)} fusion(f32[2048,1024]{1,0:T(8,128)} %get-tuple-element.14, bf16[2048,1024]{1,0:T(8,128)(2,1)} %bitcast.139, bf16[2048,1024]{1,0:T(8,128)(2,1)} %copy-done.12, bf16[1,2,1024,1024]{3,2,1,0:T(8,128)(2,1)} %all-gather.4.cloned.1.call-done), kind=kOutput, calls=%fused_computation.16 | convolution fusion | flops 4303355904 | bytes 23068672 | tf_op jit(solution)/shard_map/dot_general | solution.py:127
  251.6 5.0 %gather_fusion.10 = bf16[16,128,1024]{2,1,0:T(8,128)(2,1)} fusion(bf16[16,128,1024]{2,1,0:T(8,128)(2,1)} %bitcast.141, s32[1024]{0:T(1024)S(1)} %pad_clamp_fusion.1), kind=kCustom, calls=%fused_computation.6.clone | custom fusion | bytes 8388672 | tf_op jit(solution)/shard_map/jit(_take)/gather | solution.py:142
  256.6 4.8 %select_select_fusion = bf16[16,128,1024]{2,1,0:T(8,128)(2,1)} fusion(bf16[16,128,1024]{2,1,0:T(8,128)(2,1)} %gather_fusion.10, pred[16]{0:T(512)(128)(4,1)S(1)} %get-tuple-element.4, pred[16]{0:T(512)(128)(4,1)S(1)} %select_compare_fusion), kind=kLoop, calls=%fused_computation.25 | loop fusion | flops 4194304 | bytes 8388640 | tf_op jit(solution)/shard_map/jit(_where)/select_n | solution.py:143
  261.4 16.2 %all-to-all-start.1 = ((bf16[8,256,1024]{2,1,0:T(8,128)(2,1)}), bf16[8,256,1024]{2,1,0:T(8,128)(2,1)}, u32[]{:S(2)}, u32[]{:S(2)}) async-start(bf16[8,256,1024]{2,1,0:T(8,128)(2,1)} %bitcast.132), calls=%async_computation.1 | async-start | bytes 8388608 | tf_op jit(solution)/shard_map/all_to_all | solution.py:146
  277.6 10.6 %multiply_convert_fusion.2 = bf16[1024,1024]{1,0:T(8,128)(2,1)} fusion(bf16[2048,1024]{1,0:T(8,128)(2,1)} %get-tuple-element.13, f32[2048,1024]{1,0:T(8,128)} %copy-done.13), kind=kOutput, calls=%fused_computation.27 | convolution fusion | flops 4307550208 | bytes 14680064 | tf_op jit(solution)/shard_map/dot_general | solution.py:115
  289.2 31.1 %reduce-scatter.5.cloned.1.call-done = bf16[256,1024]{1,0:T(8,128)(2,1)} async-done(((bf16[1024,1024]{1,0:T(8,128)(2,1)}), bf16[256,1024]{1,0:T(8,128)(2,1)}) %reduce-scatter.5.cloned.1.call-update) | async-done | bytes 524304 | tf_op jit(solution)/shard_map/reduce_scatter | solution.py:113
  323.0 45.5 %all-to-all-done.1 = bf16[8,256,1024]{2,1,0:T(8,128)(2,1)} async-done(((bf16[8,256,1024]{2,1,0:T(8,128)(2,1)}), bf16[8,256,1024]{2,1,0:T(8,128)(2,1)}, u32[]{:S(2)}, u32[]{:S(2)}) %all-to-all-start.1) | async-done | bytes 4194336 | tf_op jit(solution)/shard_map/all_to_all | solution.py:146
  368.5 4.3 %gather_fusion.3 = bf16[8,128,1024]{2,1,0:T(8,128)(2,1)} fusion(bf16[16,128,1024]{2,1,0:T(8,128)(2,1)} %bitcast.30, s32[1024]{0:T(1024)S(1)} %pad_clamp_fusion), kind=kCustom, calls=%fused_computation.10 | custom fusion | bytes 4194336 | tf_op jit(solution)/shard_map/jit(_take)/gather | solution.py:151
  (92 shorter events, 29.6 us)
Async XLA Ops:
  7.2 74.7 %copy-start = (bf16[1024,1024]{1,0:T(8,128)(2,1)S(1)}, bf16[1024,1024]{1,0:T(8,128)(2,1)}, u32[]{:S(2)}) copy-start(bf16[1024,1024]{1,0:T(8,128)(2,1)} %param.19) | copy-start | bytes 6291460
  11.7 8.8 %collective-permute-start.1 = (bf16[128,1024]{1,0:T(8,128)(2,1)S(1)}, bf16[128,1024]{1,0:T(8,128)(2,1)S(1)}, u32[]{:S(2)}, u32[]{:S(2)}) collective-permute-start(bf16[128,1024]{1,0:T(8,128)(2,1)S(1)} %broadcast_select_fusion.1), channel_id=1, source_target_pairs={{8,0},{16,8},{24,16},{9,1},{17,9},{25,17},{10,2},{18,10},{26,18},{... | collective-permute-start | bytes 786440 | tf_op jit(solution)/shard_map/ppermute | solution.py:21
  13.0 7.5 %collective-permute-start = (bf16[128,1024]{1,0:T(8,128)(2,1)S(1)}, bf16[128,1024]{1,0:T(8,128)(2,1)S(1)}, u32[]{:S(2)}, u32[]{:S(2)}) collective-permute-start(bf16[128,1024]{1,0:T(8,128)(2,1)S(1)} %broadcast_select_fusion.1), channel_id=1, source_target_pairs={{0,8},{8,16},{16,24},{1,9},{9,17},{17,25},{2,10},{10,18},{18,26},{... | collective-permute-start | bytes 786440 | tf_op jit(solution)/shard_map/ppermute | solution.py:18
  16.9 0.7 copy-start.9
  17.5 0.5 copy-start.2
  46.8 22.9 %copy-start.7 = (f32[1024]{0:T(1024)S(1)}, f32[1024]{0:T(1024)}, u32[]{:S(2)}) copy-start(f32[1024]{0:T(1024)} %param.20) | copy-start | bytes 12292
  69.7 9.0 %copy-start.4 = (bf16[4096,1024]{1,0:T(8,128)(2,1)S(1)}, bf16[4096,1024]{1,0:T(8,128)(2,1)}, u32[]{:S(2)}) copy-start(bf16[4096,1024]{1,0:T(8,128)(2,1)} %gather_fusion.5) | copy-start | bytes 25165828
  78.7 3.1 copy-start.5
  94.3 8.2 %copy-start.8 = (s32[1,8]{1,0:T(1,128)S(1)}, s32[1,8]{1,0:T(1,128)}, u32[]{:S(2)}) copy-start(s32[1,8]{1,0:T(1,128)} %param.18) | copy-start | bytes 100
  94.3 102.2 %all-to-all-start = ((bf16[8,256,1024]{2,1,0:T(8,128)(2,1)}), bf16[8,256,1024]{2,1,0:T(8,128)(2,1)}, u32[]{:S(2)}, u32[]{:S(2)}) async-start(bf16[8,256,1024]{2,1,0:T(8,128)(2,1)} %fusion.4), calls=%async_computation | async-start | bytes 8388608 | tf_op jit(solution)/shard_map/all_to_all | solution.py:67
  101.7 104.7 %all-gather.4.cloned.1.call-start = ((), (), s32[]{:S(2)}) async-start(), calls=%async_computation.6 | async-start | bytes 5242880 | tf_op jit(solution)/shard_map/all_gather | solution.py:97
  102.4 186.8 %reduce-scatter.3.cloned.1.call-start = ((), (), s32[]{:S(2)}) async-start(), calls=%async_computation.4 | async-start | bytes 2621440 | tf_op jit(solution)/shard_map/reduce_scatter | solution.py:113
  206.4 7.1 %copy-start.6 = (bf16[16,128,1024]{2,1,0:T(8,128)(2,1)S(1)}, bf16[16,128,1024]{2,1,0:T(8,128)(2,1)}, u32[]{:S(2)}) copy-start(bf16[16,128,1024]{2,1,0:T(8,128)(2,1)} %select_select_fusion.1) | copy-start | bytes 12582916
  206.4 7.1 %copy-start.11 = (bf16[1,2,1024,1024]{3,2,1,0:T(8,128)(2,1)S(1)}, bf16[1,2,1024,1024]{3,2,1,0:T(8,128)(2,1)}, u32[]{:S(2)}) copy-start(bf16[1,2,1024,1024]{3,2,1,0:T(8,128)(2,1)} %all-gather.4.cloned.1.call-done) | copy-start | bytes 12582916
  213.5 7.9 %copy-start.13 = (f32[2048,1024]{1,0:T(8,128)}, f32[2048,1024]{1,0:T(8,128)S(1)}, u32[]{:S(2)}) copy-start(f32[2048,1024]{1,0:T(8,128)S(1)} %fusion.9) | copy-start | bytes 25165828
  230.8 2.0 copy-start.12
  261.4 107.1 %all-to-all-start.1 = ((bf16[8,256,1024]{2,1,0:T(8,128)(2,1)}), bf16[8,256,1024]{2,1,0:T(8,128)(2,1)}, u32[]{:S(2)}, u32[]{:S(2)}) async-start(bf16[8,256,1024]{2,1,0:T(8,128)(2,1)} %bitcast.132), calls=%async_computation.1 | async-start | bytes 8388608 | tf_op jit(solution)/shard_map/all_to_all | solution.py:146
  277.6 10.7 %copy-start.10 = (s32[8,1]{0,1:T(1,128)S(1)}, s32[8,1]{0,1:T(1,128)}, u32[]{:S(2)}) copy-start(s32[8,1]{0,1:T(1,128)} %copy-done.9) | copy-start | bytes 100
  277.6 10.9 %copy-start.3 = (s32[8]{0:T(128)S(1)}, s32[8]{0:T(128)}, u32[]{:S(2)}) copy-start(s32[8]{0:T(128)} %copy-done.2) | copy-start | bytes 100
  277.6 42.8 %reduce-scatter.5.cloned.1.call-start = ((), (), s32[]{:S(2)}) async-start(), calls=%async_computation.5 | async-start | bytes 2621440 | tf_op jit(solution)/shard_map/reduce_scatter | solution.py:113
  368.5 7.5 %copy-start.1 = (bf16[1024,1024]{1,0:T(8,128)(2,1)S(1)}, bf16[1024,1024]{1,0:T(8,128)(2,1)}, u32[]{:S(2)}) copy-start(bf16[1024,1024]{1,0:T(8,128)(2,1)} %param.19) | copy-start | bytes 6291460
Sparse Core Ops, SparseCore 0:
  104.1 36.6 all-gather.3
  238.6 41.2 reduce-scatter.2
  288.4 31.8 reduce-scatter.4
where the time goes:
time: 384 us; the launch traced here: 383 us
  waiting for transfers between devices  83.9 us (22%)
  blocking collectives  83.7 us (22%)
  local copies, waits for them, and re-layouts  73.4 us (19%)
  matrix products  58 us (15%)
  other arithmetic  41.5 us (11%)
  starting transfers between devices  28 us (7%)
  between operations  14.1 us (4%)
    all_gather x1, blocking collectives, body(): all_counts = lax.all_gather(counts, 'head', axis=0, tiled=True)  83.7 us
    all_to_all x1, waiting for transfers between devices, body(): lax.all_to_all(sending, 'head', split_axis=0, concat_axis=0, tiled=True)  45.5 us
    reduce_scatter x2, waiting for transfers between devices, body(): lax.psum_scatter((lax.dot_general(activation, gradient, (((0,), (0,)), ((...  31.1 us
    gather x1, local copies, waits for them, and re-layouts, encode_rows(): bonded = jnp.take(extended, bond_ids, axis=0)  22.9 us
    gather x1, local copies, waits for them, and re-layouts, encode_rows(): partner = jnp.take(extended, partner_ids, axis=0)  22.9 us
    dot_general x2, matrix products, body(): lax.dot_general(gradient, whole_weights[layer_id], (((1,), (1,)), ((), ()...  22.5 us
    dot_general x2, matrix products, body(): lax.dot_general(activation, gradient, (((0,), (0,)), ((), ())), preferred...  16.4 us
    all_to_all x1, starting transfers between devices, body(): lax.all_to_all(sending, 'head', split_axis=0, concat_axis=0, tiled=True)  16.2 us
  transfers between devices with their start and end apart: 7, of which 3 were waited for; matrix products, arithmetic and copies ran while one was open for 14% of the time, Pallas kernels for 0%

commit v1 on v0

v1 whole, which is shorter than its diff:
```python
import functools
import math

import jax
import jax.numpy as jnp
from jax import lax
from jax.experimental import pallas as pl
from jax.experimental.pallas import tpu as pltpu
from jax.sharding import PartitionSpec as P

BLOCK = 128
PAIR = 2 * BLOCK
LANES = 128
MB = 1 << 20
F32 = jnp.float32
BF16 = jnp.bfloat16


def sigmoid(x):
    return 1.0 / (1.0 + jnp.exp(-x))


def resident(shape):
    return pl.BlockSpec(shape, lambda *_: (0,) * len(shape))


def pick_kernel(ids_ref, rows_ref, out_ref):
    count, total = out_ref.shape[0], rows_ref.shape[0]
    places = lax.broadcasted_iota(jnp.int32, (count, total), 1)
    ones = jnp.where(places == ids_ref[...], 1.0, 0.0).astype(BF16)
    out_ref[...] = jnp.dot(ones, rows_ref[...], preferred_element_type=F32).astype(BF16)


def pick_rows(rows, ids):
    return pl.pallas_call(
        pick_kernel,
        out_shape=jax.ShapeDtypeStruct((ids.shape[0], rows.shape[1]), rows.dtype),
        compiler_params=pltpu.CompilerParams(vmem_limit_bytes=24 * MB),
        name="pick_rows",
    )(ids[:, None], rows)


def step_source(counts_ref, step, extra, sets):
    zero = jnp.int32(0)

    def scan(dataset, carry):
        start, seen, source, live = carry
        blocks = counts_ref[0, dataset] // BLOCK
        double = blocks > 1
        is_second = jnp.logical_and(double, seen == step)
        is_first = jnp.logical_and(blocks > 0, dataset + extra == step)
        source = jnp.where(is_second, start + 1, jnp.where(is_first, start, source))
        live = jnp.where(jnp.logical_or(is_second, is_first), 1, live)
        return start + blocks, seen + jnp.where(double, 1, 0), source, live

    carry = (zero, zero, zero, zero)
    for dataset in range(sets):
        carry = scan(dataset, carry)
    return carry[2], carry[3]


def encode_kernel(
    extra, bond_count, unroll, counts_ref, codes_ref, atoms_ref, low_ref, high_ref, weight_ref,
    gain_ref, second_ref, first_ref, plain, gained, products, gates, mixed, message,
):
    step = pl.program_id(0)
    rows, width = atoms_ref.shape
    depth = low_ref.shape[0]
    tall = width // LANES
    sets = first_ref.shape[0] if False else counts_ref.shape[1]

    @pl.when(step == 0)
    def _():
        def spread(ref, at, base):
            for k in range(tall):
                lanes = slice(k * LANES, (k + 1) * LANES)
                value = ref[pl.ds(at, BLOCK), lanes].astype(F32)
                place = pl.ds(base * tall + k, BLOCK, stride=tall)
                plain[place, :] = value
                gained[place, :] = value * gain_ref[:, lanes]

        for at in range(0, rows, BLOCK):
            spread(atoms_ref, at, at)
        for at in range(0, depth, BLOCK):
            spread(low_ref, at, rows + at)
            spread(high_ref, at, rows + depth + at)

    source, live = step_source(counts_ref, step, extra, sets)
    base = pl.multiple_of(source * BLOCK, BLOCK)

    def row_of(ref, place):
        return ref[pl.ds(pl.multiple_of(place, tall), tall), :]

    def encode():
        def score(outer, carry):
            for inner in range(unroll):
                atom = outer * unroll + inner
                for bond in range(bond_count):
                    code = codes_ref[bond * rows + base + atom]
                    bonded = row_of(plain, code >> 16)
                    partner = row_of(gained, code & 0xFFFF)
                    place = pl.multiple_of((atom * bond_count + bond) * tall, tall)
                    products[pl.ds(place, tall), :] = bonded * partner
            return carry

        lax.fori_loop(0, BLOCK // unroll, score, 0)
        pairs = BLOCK * bond_count
        total = products[pl.ds(0, pairs, stride=tall), :]
        for k in range(1, tall):
            total = total + products[pl.ds(k, pairs, stride=tall), :]
        logits = jnp.sum(total, axis=1, keepdims=True) * (1.0 / math.sqrt(width))
        gates[...] = jnp.broadcast_to(sigmoid(logits), gates.shape)

        def mix(outer, carry):
            for inner in range(unroll):
                atom = outer * unroll + inner
                acc = None
                for bond in range(bond_count):
                    code = codes_ref[bond * rows + base + atom]
                    gate = gates[pl.ds(atom * bond_count + bond, 1), :]
                    term = row_of(plain, code >> 16) * gate
                    acc = term if acc is None else acc + term
                mixed[pl.ds(pl.multiple_of(atom * tall, tall), tall), :] = acc
            return carry

        lax.fori_loop(0, BLOCK // unroll, mix, 0)
        for k in range(tall):
            part = mixed[pl.ds(k, BLOCK, stride=tall), :]
            message[:, k * LANES : (k + 1) * LANES] = part.astype(BF16)
        update = jnp.dot(message[...], weight_ref[...], preferred_element_type=F32)
        own = atoms_ref[pl.ds(base, BLOCK), :].astype(F32)
        return (own + update * sigmoid(update)).astype(BF16)

    def emit(out_ref):
        @pl.when(live == 1)
        def _():
            out_ref[0] = encode()

        @pl.when(live == 0)
        def _():
            out_ref[...] = jnp.zeros_like(out_ref)

    pl.when(step < extra)(lambda: emit(second_ref))
    pl.when(step >= extra)(lambda: emit(first_ref))


def encode(counts, codes, atoms, low, high, weight, gain, bond_count):
    rows, width = atoms.shape
    depth = low.shape[0]
    sets = counts.shape[1]
    extra = rows // PAIR
    tall = width // LANES
    extended = rows + 2 * depth
    kernel = functools.partial(encode_kernel, extra, bond_count, 4)
    block = (1, BLOCK, width)
    return pl.pallas_call(
        kernel,
        grid_spec=pltpu.PrefetchScalarGridSpec(
            num_scalar_prefetch=2,
            grid=(extra + sets,),
            in_specs=[
                resident((rows, width)),
                resident((depth, width)),
                resident((depth, width)),
                resident((width, width)),
                resident((1, width)),
            ],
            out_specs=[
                pl.BlockSpec(block, lambda t, *_: (jnp.minimum(t, extra - 1), 0, 0)),
                pl.BlockSpec(block, lambda t, *_: (jnp.maximum(t - extra, 0), 0, 0)),
            ],
            scratch_shapes=[
                pltpu.VMEM((extended * tall, LANES), F32),
                pltpu.VMEM((extended * tall, LANES), F32),
                pltpu.VMEM((BLOCK * bond_count * tall, LANES), F32),
                pltpu.VMEM((BLOCK * bond_count, LANES), F32),
                pltpu.VMEM((BLOCK * tall, LANES), F32),
                pltpu.VMEM((BLOCK, width), BF16),
            ],
        ),
        out_shape=[
            jax.ShapeDtypeStruct((extra, BLOCK, width), BF16),
            jax.ShapeDtypeStruct((sets, BLOCK, width), BF16),
        ],
        compiler_params=pltpu.CompilerParams(vmem_limit_bytes=48 * MB),
        name="encode_rows",
    )(counts, codes, atoms, low, high, weight, gain)


def head_kernel(masked, keep_ref, rows_ref, weight_ref, *outs):
    step = pl.program_id(0)
    blocks, _, width = rows_ref.shape
    if masked:
        x_ref, back_ref, sent_ref, act_ref, low_grad_ref, high_grad_ref = outs
        for b in range(blocks):
            live = keep_ref[0, step * blocks + b] == 1
            x_ref[b] = jnp.where(live, rows_ref[b], jnp.zeros_like(rows_ref[b]))
    else:
        back_ref, act_ref, low_grad_ref, high_grad_ref = outs
        x_ref = rows_ref
    x = x_ref[...].reshape(blocks * BLOCK, width)
    shape = x_ref.shape
    low = weight_ref[:, 0].reshape(width, width)
    high = weight_ref[:, 1].reshape(width, width)
    transposed = (((1,), (1,)), ((), ()))
    z = jnp.dot(x, low, preferred_element_type=F32)
    s = sigmoid(z)
    act = (z * s).astype(BF16)
    act_ref[...] = act.reshape(shape)
    slope = s * (1.0 + z * (1.0 - s))
    err = jnp.dot(act, high, preferred_element_type=F32) - x.astype(F32)
    grad = err.astype(BF16)
    high_grad_ref[...] = grad.reshape(shape)
    up = lax.dot_general(grad, high, transposed, preferred_element_type=F32)
    grad = (up * slope).astype(BF16)
    low_grad_ref[...] = grad.reshape(shape)
    up = lax.dot_general(grad, low, transposed, preferred_element_type=F32)
    back = (up - err).astype(BF16).reshape(shape)
    back_ref[...] = back
    if masked:
        for b in range(blocks):
            live = keep_ref[1, step * blocks + b] == 1
            sent_ref[b] = jnp.where(live, back[b], jnp.zeros_like(back[b]))


def run_head(rows, weights, keep):
    count, _, width = rows.shape
    tile = 2 if count % 2 == 0 else 1
    masked = keep is not None
    if keep is None:
        keep = jnp.zeros((2, count), jnp.int32)
    block = pl.BlockSpec((tile, BLOCK, width), lambda t, *_: (t, 0, 0))
    total = count * BLOCK
    outs = 6 if masked else 4
    return pl.pallas_call(
        functools.partial(head_kernel, masked),
        grid_spec=pltpu.PrefetchScalarGridSpec(
            num_scalar_prefetch=1,
            grid=(count // tile,),
            in_specs=[block, resident(weights.shape)],
            out_specs=[block] * outs,
        ),
        out_shape=[jax.ShapeDtypeStruct(rows.shape, BF16)] * outs,
        compiler_params=pltpu.CompilerParams(vmem_limit_bytes=48 * MB),
        cost_estimate=pl.CostEstimate(
            flops=8 * total * width * width,
            bytes_accessed=(outs + 1) * total * width * 2 + weights.size * 2,
            transcendentals=total * width,
        ),
        name="head_rows",
    )(keep, rows, weights)


def place_kernel(counts_ref, first_ref, second_ref, others_ref, out_ref):
    sets = counts_ref.shape[1]
    dataset, rank, order = block_place(counts_ref, pl.program_id(0), sets)
    from_first = rank == 0
    from_second = order == 0
    rest = jnp.where(from_second, second_ref[0], others_ref[0])
    out_ref[0] = jnp.where(from_first, first_ref[0], rest)


def block_place(counts_ref, block, sets):
    zero = jnp.int32(0)
    start, seen, dataset, rank, order = zero, zero, zero, zero, zero
    for candidate in range(sets):
        blocks = counts_ref[0, candidate] // BLOCK
        inside = jnp.logical_and(block >= start, block < start + blocks)
        dataset = jnp.where(inside, candidate, dataset)
        rank = jnp.where(inside, block - start, rank)
        order = jnp.where(inside, seen, order)
        start = start + blocks
        seen = seen + jnp.where(blocks > 1, 1, 0)
    return dataset, rank, order


def place_rows(counts, first, second, others, row_blocks):
    sets, _, width = first.shape
    shape = (1, BLOCK, width)

    def first_index(block, counts_ref):
        return block_place(counts_ref, block, sets)[0], 0, 0

    def other_index(block, counts_ref):
        dataset, rank, order = block_place(counts_ref, block, sets)
        return jnp.where(jnp.logical_and(rank > 0, order > 0), dataset, 0), 0, 0

    return pl.pallas_call(
        place_kernel,
        grid_spec=pltpu.PrefetchScalarGridSpec(
            num_scalar_prefetch=1,
            grid=(row_blocks,),
            in_specs=[
                pl.BlockSpec(shape, first_index),
                resident(shape),
                pl.BlockSpec(shape, other_index),
            ],
            out_specs=pl.BlockSpec(shape, lambda block, *_: (block, 0, 0)),
        ),
        out_shape=jax.ShapeDtypeStruct((row_blocks, BLOCK, width), BF16),
        compiler_params=pltpu.CompilerParams(vmem_limit_bytes=24 * MB),
        name="place_rows",
    )(counts, first, second, others)


def halo(cut_rows):
    count = lax.axis_size("dom")
    forward = [(i, i + 1) for i in range(count - 1)]
    backward = [(target, source) for source, target in forward]
    low = lax.ppermute(cut_rows, "dom", forward)
    high = lax.ppermute(cut_rows, "dom", backward)
    return low, high


def exchange(blocks):
    return lax.all_to_all(blocks, "head", split_axis=0, concat_axis=0, tiled=True)


def body(atoms, bonds, triplets, halo_ids, counts, enc_weight, gate_gain, head_weight):
    atom_rows = atoms[0]
    row_count, width = atom_rows.shape
    row_blocks = row_count // BLOCK
    bond_count = bonds.shape[1]
    sets = counts.shape[1]
    group = lax.axis_size("head")
    tall = width // LANES
    layers = head_weight.shape[1]

    every = lax.all_gather(counts, ("dom", "head"), axis=0, tiled=True)
    weights = lax.all_gather(head_weight[0], "dom", axis=0, tiled=False)
    low, high = halo(pick_rows(atom_rows, halo_ids[0]))
    codes = ((bonds[0] * tall) * 65536 + triplets[0] * tall).reshape(-1)
    second, first = encode(
        counts, codes, atom_rows, low, high, enc_weight, gate_gain[None, :], bond_count
    )

    doubled = every == PAIR
    order = jnp.cumsum(doubled.astype(jnp.int32), axis=1)
    more = (jnp.max(order) > 1).astype(jnp.int32)
    mine = lax.dynamic_slice_in_dim(doubled, lax.axis_index("dom") * group, group, 0)
    mine_order = lax.dynamic_slice_in_dim(order, lax.axis_index("dom") * group, group, 0)
    here = jnp.arange(sets, dtype=jnp.int32)[None, :] == lax.axis_index("head")
    has_second = jnp.any(jnp.logical_and(mine, here), axis=1)
    is_lead = jnp.any(jnp.logical_and(jnp.logical_and(mine, here), mine_order == 1), axis=1)
    keep = jnp.stack([has_second, is_lead]).astype(jnp.int32)
    own_doubled = counts[0] == PAIR
    own_order = jnp.cumsum(own_doubled.astype(jnp.int32)) - 1

    lead = lax.all_gather(second[0], "head", axis=0, tiled=False)
    arrived = exchange(first)

    def send_rest(_, held):
        picked = jnp.take(second, jnp.clip(own_order, 0, second.shape[0] - 1), axis=0)
        rest = exchange(jnp.where(own_doubled[:, None, None], picked, jnp.zeros_like(picked)))
        return jnp.where(is_lead[:, None, None], held, rest)

    seconds = lax.fori_loop(0, more, send_rest, lead)

    x_b, back_b, sent_b, act_b, low_b, high_b = run_head(seconds, weights, keep)
    returned_second = lax.psum_scatter(sent_b, "head", scatter_dimension=0, tiled=True)
    back_a, act_a, low_a, high_a = run_head(arrived, weights, None)
    returned_first = exchange(back_a)
    returned_rest = lax.fori_loop(0, more, lambda _, held: exchange(held), back_b)

    scale = 1.0 / math.sqrt(lax.axis_size("dom") * row_count)

    def share(first_acts, first_grads, second_acts, second_grads):
        def product(acts, grads):
            return lax.dot_general(
                acts.reshape(-1, width),
                grads.reshape(-1, width),
                (((0,), (0,)), ((), ())),
                preferred_element_type=F32,
            )

        total = product(second_acts, second_grads) + product(first_acts, first_grads)
        return lax.psum_scatter(
            (total * scale).astype(BF16), "dom", scatter_dimension=0, tiled=True
        ).astype(F32)

    shares = [share(act_a, high_a, act_b, high_b), share(arrived, low_a, x_b, low_b)]
    head_part = jnp.stack(shares[::-1])
    row_part = place_rows(counts, returned_first, returned_second, returned_rest, row_blocks)
    return row_part.reshape(1, row_count, width), head_part[None]


def solution(mesh):
    return jax.shard_map(
        body,
        mesh=mesh,
        in_specs=(
            P("dom", "head", None),
            P("dom", None, "head"),
            P("dom", None, "head"),
            P("dom", "head"),
            P("dom", "head"),
            P(),
            P(),
            P("head", None, "dom", None),
        ),
        out_specs=(P("dom", "head", None), P("head", None, "dom", None)),
        check_vma=False,
    )
```

time: 384 us -> 342 us (0.89)
  waiting for transfers between devices: 83.9 us -> 155 us
  local copies, waits for them, and re-layouts: 73.4 us -> 5.39 us
  Pallas kernels: 0 us -> 62.1 us
  other arithmetic: 41.5 us -> 3.82 us
  matrix products: 58 us -> 20.7 us
  blocking collectives: 83.7 us -> 67.4 us
  starting transfers between devices: 28 us -> 12.5 us
    reduce_scatter x2 -> x3, waiting for transfers between devices: 31.1 us -> 119 us  [the longest x1 68.5 us: body(): lax.psum_scatter(sent_b, 'head', scatter_dimension=0, tiled=True)]
    gather x11 -> x0, local copies, waits for them, and re-layouts: 70.1 us -> none  [the longest x1 22.9 us: encode_rows(): bonded = jnp.take(extended, bond_ids, axis=0)]
    pallas_call x0 -> x5, Pallas kernels: none -> 62.1 us  [the longest x1 29.7 us: encode(): pl.pallas_call(kernel, grid_spec=pltpu.PrefetchScalarGridSpec(num_scalar_...]
    dot_general x7 -> x4, matrix products: 58 us -> 20.7 us  [product(): lax.dot_general(acts.reshape(-1, width), grads.reshape(-1, width), (((0,)...]
    all_to_all x2, waiting for transfers between devices: 52.1 us -> 16.4 us  [exchange(): lax.all_to_all(blocks, 'head', split_axis=0, concat_axis=0, tiled=True)]
    select_n x13 -> x0, other arithmetic: 18.4 us -> none  [the longest x1 4.8 us: body(): jnp.where(return_live[:, None, None], sending, jnp.zeros_like(sending))]
    all_gather x1, blocking collectives: 83.7 us -> 67.4 us  [body(): every = lax.all_gather(counts, ('dom', 'head'), axis=0, tiled=True)]
    all_to_all x2, starting transfers between devices: 23.5 us -> 8.13 us  [exchange(): lax.all_to_all(blocks, 'head', split_axis=0, concat_axis=0, tiled=True)]
  transfers between devices with their start and end apart: 7 -> 9, of which waited for: 3 -> 6; matrix products, arithmetic and copies ran while one was open for 14% -> 5% of each run, Pallas kernels for 0% -> 4%
where the time goes in v1:
time: 342 us; the launch traced here: 341 us
  waiting for transfers between devices  155 us (45%)
  blocking collectives  67.4 us (20%)
  Pallas kernels  62.1 us (18%)
  matrix products  20.7 us (6%)
  between operations  14.6 us (4%)
  starting transfers between devices  12.5 us (4%)
  local copies, waits for them, and re-layouts  5.39 us (2%)
  other arithmetic  3.82 us (1%)
    reduce_scatter x1, waiting for transfers between devices, body(): lax.psum_scatter(sent_b, 'head', scatter_dimension=0, tiled=True)  68.5 us
    all_gather x1, blocking collectives, body(): every = lax.all_gather(counts, ('dom', 'head'), axis=0, tiled=True)  67.4 us
    reduce_scatter x2, waiting for transfers between devices, share(): lax.psum_scatter((total * scale).astype(BF16), 'dom', scatter_dimension=0...  50.7 us
    pallas_call x1, Pallas kernels, encode(): pl.pallas_call(kernel, grid_spec=pltpu.PrefetchScalarGridSpec(num_scalar_...  29.7 us
    pallas_call x2, Pallas kernels, run_head(): pl.pallas_call(functools.partial(head_kernel, masked), grid_spec=pltpu.Pr...  27 us
    dot_general x4, matrix products, product(): lax.dot_general(acts.reshape(-1, width), grads.reshape(-1, width), (((0,)...  20.7 us
    all_to_all x2, waiting for transfers between devices, exchange(): lax.all_to_all(blocks, 'head', split_axis=0, concat_axis=0, tiled=True)  16.4 us
    all_gather x1, waiting for transfers between devices, body(): weights = lax.all_gather(head_weight[0], 'dom', axis=0, tiled=False)  13.6 us
  transfers between devices with their start and end apart: 9, of which 6 were waited for; matrix products, arithmetic and copies ran while one was open for 5% of the time, Pallas kernels for 4%

profile of v1, /device:TPU:0, one launch (start us, length us, event | category | flops | bytes accessed | tf_op | source)
XLA Modules:
  0.0 341.2 jit_solution(2861781771244147482)
XLA Ops:
  7.3 0.8 copy.20.ids_ref
  8.0 1.6 copy-done
  10.1 2.5 collective-permute-start
  12.6 1.3 collective-permute-start.1
  14.0 4.2 %collective-permute-done.1.high_ref = bf16[128,1024]{1,0:T(8,128)(2,1)S(1)} collective-permute-done((bf16[128,1024]{1,0:T(8,128)(2,1)S(1)}, bf16[128,1024]{1,0:T(8,128)(2,1)S(1)}, u32[]{:S(2)}, u32[]{:S(2)}) %collective-permute-start.1) | collective-permute-done | bytes 262176 | tf_op jit(solution)/shard_map/ppermute | solution.py:311
  18.2 29.7 %encode_rows.1 = (bf16[4,128,1024]{2,1,0:T(8,128)(2,1)S(1)}, bf16[8,128,1024]{2,1,0:T(8,128)(2,1)}) custom-call(s32[1,8]{1,0:T(1,128)S(1)} %copy-done.4, s32[4096]{0:T(1024)S(1)} %bitcast.68, bf16[1024,1024]{1,0:T(8,128)(2,1)S(1)} %bitcast.67, bf16[128,1024]{1,0:T(8,128)(2,1)S(1)} %collective-permute-done.low_ref, ...), custom_call_target="tpu_custom_call" | custom-call | tf_op jit(solution)/shard_map/encode_rows/pallas_call | solution.py:156
  49.4 67.4 %all-gather = s32[32,1,8]{2,1,0:T(1,128)S(1)} all-gather(s32[1,1,8]{2,1,0:T(1,128)S(1)} %bitcast.69), channel_id=1, replica_groups=mesh['dom'=4,'head'=8] {'dom','head'}, dimensions={0}, use_global_device_ids=true | all-gather | bytes 1056 | tf_op jit(solution)/shard_map/all_gather | solution.py:329
  118.6 4.5 %all-to-all-start.2 = ((bf16[8,128,1024]{2,1,0:T(8,128)(2,1)}), bf16[8,128,1024]{2,1,0:T(8,128)(2,1)}, u32[]{:S(2)}, u32[]{:S(2)}) async-start(bf16[8,128,1024]{2,1,0:T(8,128)(2,1)} %get-tuple-element.70), calls=%async_computation.2 | async-start | bytes 4194304 | tf_op jit(solution)/shard_map/all_to_all | solution.py:316
  123.4 13.6 %all-gather.4.cloned.1.call-done.weight_ref = bf16[4,2,256,1024]{3,2,1,0:T(8,128)(2,1)} async-done(((bf16[1,2,256,1024]{3,2,1,0:T(8,128)(2,1)}), bf16[4,2,256,1024]{3,2,1,0:T(8,128)(2,1)}) %all-gather.4.cloned.1.call-update) | async-done | bytes 4194320 | tf_op jit(solution)/shard_map/all_gather | solution.py:330
  137.0 13.8 %head_rows.3 = (bf16[8,128,1024]{2,1,0:T(8,128)(2,1)S(1)}, bf16[8,128,1024]{2,1,0:T(8,128)(2,1)}, bf16[8,128,1024]{2,1,0:T(8,128)(2,1)}, bf16[8,128,1024]{2,1,0:...) custom-call(s32[2,8]{1,0:T(2,128)S(1)} %add_convert_fusion.keep_ref, ...), custom_call_target="tpu_custom_call" | custom-call | flops 8589934592 | bytes 18874368 | tf_op jit(solution)/shard_map/head_rows/pallas_call | solution.py:235
  150.8 6.0 %fusion.10 = f32[1024,1024,1]{1,0,2:T(8,128)} fusion(bf16[8,128,1024]{2,1,0:T(8,128)(2,1)S(1)} %get-tuple-element.77, bf16[8,128,1024]{2,1,0:T(8,128)(2,1)} %get-tuple-element.78), kind=kOutput, calls=%fused_computation.31 | convolution fusion | flops 2147483648 | bytes 8388608 | tf_op jit(solution)/shard_map/dot_general | solution.py:369
  156.8 16.4 %all-to-all-done.2.rows_ref = bf16[8,128,1024]{2,1,0:T(8,128)(2,1)} async-done(((bf16[8,128,1024]{2,1,0:T(8,128)(2,1)}), bf16[8,128,1024]{2,1,0:T(8,128)(2,1)}, u32[]{:S(2)}, u32[]{:S(2)}) %all-to-all-start.2) | async-done | bytes 2097184 | tf_op jit(solution)/shard_map/all_to_all | solution.py:316
  173.2 13.2 %head_rows.2 = (bf16[8,128,1024]{2,1,0:T(8,128)(2,1)S(1)}, bf16[8,128,1024]{2,1,0:T(8,128)(2,1)S(1)}, bf16[8,128,1024]{2,1,0:T(8,128)(2,1)}, bf16[8,128,1024]{2,1,0:T(8,128)(2,1)}) custom-call(s32[2,8]{1,0:T(2,128)S(1)} %broadcast_16_keep_ref.2.keep_ref, bf16[8,128,1024]{2,1,0:T(8,128)(2,1)} %all-to-all-done.2.rows_ref, ...), custom_call_target="tpu_custom_call" | custom-call | flops 8589934592 | bytes 14680064 | tf_op jit(solution)/shard_map/head_rows/pallas_call | solution.py:235
  186.4 1.3 copy-done.2
  187.7 6.1 %fusion.4 = bf16[1024,1024]{1,0:T(8,128)(2,1)} fusion(f32[1024,1024,1]{1,0,2:T(8,128)S(1)} %copy-done.9, bf16[8,128,1024]{2,1,0:T(8,128)(2,1)} %all-to-all-done.2.rows_ref, bf16[8,128,1024]{2,1,0:T(8,128)(2,1)} %get-tuple-element.79), kind=kOutput, calls=%fused_computation.13 | convolution fusion | flops 2150629376 | bytes 10485760 | tf_op jit(solution)/shard_map/dot_general | solution.py:369
  194.1 4.8 %fusion.11 = f32[1024,1024,1]{1,0,2:T(8,128)S(1)} fusion(bf16[8,128,1024]{2,1,0:T(8,128)(2,1)} %get-tuple-element.80, bf16[8,128,1024]{2,1,0:T(8,128)(2,1)} %get-tuple-element.81), kind=kOutput, calls=%fused_computation.32 | convolution fusion | flops 2147483648 | bytes 8388608 | tf_op jit(solution)/shard_map/dot_general | solution.py:369
  198.9 3.9 %fusion.2 = bf16[1024,1024]{1,0:T(8,128)(2,1)} fusion(f32[1024,1024,1]{1,0,2:T(8,128)S(1)} %fusion.11, bf16[8,128,1024]{2,1,0:T(8,128)(2,1)S(1)} %get-tuple-element.82, bf16[8,128,1024]{2,1,0:T(8,128)(2,1)S(1)} %copy-done.10), kind=kOutput, calls=%fused_computation.10 | convolution fusion | flops 2150629376 | bytes 10485760 | tf_op jit(solution)/shard_map/dot_general | solution.py:369
  203.4 3.6 %all-to-all-start.3 = ((bf16[8,128,1024]{2,1,0:T(8,128)(2,1)}), bf16[8,128,1024]{2,1,0:T(8,128)(2,1)S(1)}, u32[]{:S(2)}, u32[]{:S(2)}) async-start(bf16[8,128,1024]{2,1,0:T(8,128)(2,1)} %copy-done.2), calls=%async_computation.3 | async-start | bytes 4194304 | tf_op jit(solution)/shard_map/all_to_all | solution.py:316
  207.0 16.1 %reduce-scatter.6.cloned.1.call-done = bf16[256,1024]{1,0:T(8,128)(2,1)} async-done(((bf16[1024,1024]{1,0:T(8,128)(2,1)}), bf16[256,1024]{1,0:T(8,128)(2,1)}) %reduce-scatter.6.cloned.1.call-update) | async-done | bytes 524304 | tf_op jit(solution)/shard_map/reduce_scatter | solution.py:377
  223.1 34.6 %reduce-scatter.8.cloned.1.call-done = bf16[256,1024]{1,0:T(8,128)(2,1)} async-done(((bf16[1024,1024]{1,0:T(8,128)(2,1)}), bf16[256,1024]{1,0:T(8,128)(2,1)}) %reduce-scatter.8.cloned.1.call-update) | async-done | bytes 524304 | tf_op jit(solution)/shard_map/reduce_scatter | solution.py:377
  257.7 2.7 fusion.5
  260.4 68.5 %reduce-scatter.4.cloned.1.call-done.second_ref = bf16[1,128,1024]{2,1,0:T(8,128)(2,1)} async-done(((bf16[8,128,1024]{2,1,0:T(8,128)(2,1)}), bf16[1,128,1024]{2,1,0:T(8,128)(2,1)}) %reduce-scatter.4.cloned.1.call-update) | async-done | bytes 262160 | tf_op jit(solution)/shard_map/reduce_scatter | solution.py:360
  328.8 0.9 copy-done.3
  329.8 4.8 %place_rows.1 = bf16[8,128,1024]{2,1,0:T(8,128)(2,1)} custom-call(s32[1,8]{1,0:T(1,128)S(1)} %copy-done.4, bf16[8,128,1024]{2,1,0:T(8,128)(2,1)S(1)} %all-to-all-done.3.first_ref, bf16[1,128,1024]{2,1,0:T(8,128)(2,1)S(1)} %copy-done.3, bf16[8,128,1024]{2,1,0:T(8,128)(2,1)} %get-tuple-element.76.others_ref), custom_call_target="tpu_custom_call" | custom-call | tf_op jit(solution)/shard_map/place_rows/pallas_call | solution.py:288
  (48 shorter events, 4.4 us)
Async XLA Ops:
  7.2 6.8 %copy-start.8 = (s32[1,4,1024]{2,1,0:T(4,128)S(1)}, s32[1,4,1024]{2,1,0:T(4,128)}, u32[]{:S(2)}) copy-start(s32[1,4,1024]{2,1,0:T(4,128)} %param.13) | copy-start | bytes 49156
  7.2 6.8 %copy-start.7 = (s32[1,4,1024]{2,1,0:T(4,128)S(1)}, s32[1,4,1024]{2,1,0:T(4,128)}, u32[]{:S(2)}) copy-start(s32[1,4,1024]{2,1,0:T(4,128)} %param.14) | copy-start | bytes 49156
  7.2 11.0 %copy-start.4 = (s32[1,8]{1,0:T(1,128)S(1)}, s32[1,8]{1,0:T(1,128)}, u32[]{:S(2)}) copy-start(s32[1,8]{1,0:T(1,128)} %counts_ref.3) | copy-start | bytes 100
  7.2 11.0 %copy-start.5 = (f32[1024]{0:T(1024)S(1)}, f32[1024]{0:T(1024)}, u32[]{:S(2)}) copy-start(f32[1024]{0:T(1024)} %param.18) | copy-start | bytes 12292
  7.2 111.4 %all-gather.6.cloned.1.call-start = ((), (), s32[]{:S(2)}) async-start(), calls=%async_computation.8 | async-start | bytes 2359296 | tf_op jit(solution)/shard_map/all_gather | solution.py:349
  8.0 1.6 copy-start
  9.6 8.6 %copy-start.1 = (bf16[1,1024,1024]{2,1,0:T(8,128)(2,1)S(1)}, bf16[1,1024,1024]{2,1,0:T(8,128)(2,1)}, u32[]{:S(2)}) copy-start(bf16[1,1024,1024]{2,1,0:T(8,128)(2,1)} %param.12) | copy-start | bytes 6291460
  10.1 3.9 %collective-permute-start = (bf16[128,1024]{1,0:T(8,128)(2,1)S(1)}, bf16[128,1024]{1,0:T(8,128)(2,1)S(1)}, u32[]{:S(2)}, u32[]{:S(2)}) collective-permute-start(bf16[128,1024]{1,0:T(8,128)(2,1)S(1)} %pick_rows.1), channel_id=1, source_target_pairs={{0,8},{8,16},{16,24},{1,9},{9,17},{17,25},{2,10},{10,18},{18,26},{... | collective-permute-start | bytes 786440 | tf_op jit(solution)/shard_map/ppermute | solution.py:310
  12.6 5.5 %collective-permute-start.1 = (bf16[128,1024]{1,0:T(8,128)(2,1)S(1)}, bf16[128,1024]{1,0:T(8,128)(2,1)S(1)}, u32[]{:S(2)}, u32[]{:S(2)}) collective-permute-start(bf16[128,1024]{1,0:T(8,128)(2,1)S(1)} %pick_rows.1), channel_id=1, source_target_pairs={{8,0},{16,8},{24,16},{9,1},{17,9},{25,17},{10,2},{18,10},{26,18},{... | collective-permute-start | bytes 786440 | tf_op jit(solution)/shard_map/ppermute | solution.py:311
  48.7 88.3 %all-gather.4.cloned.1.call-start = ((), (), s32[]{:S(2)}) async-start(), calls=%async_computation.7 | async-start | bytes 5242880 | tf_op jit(solution)/shard_map/all_gather | solution.py:330
  118.6 18.4 %copy-start.6 = (bf16[8,128,1024]{2,1,0:T(8,128)(2,1)S(1)}, bf16[8,128,1024]{2,1,0:T(8,128)(2,1)}, u32[]{:S(2)}) copy-start(bf16[8,128,1024]{2,1,0:T(8,128)(2,1)} %get-tuple-element.73.rows_ref) | copy-start | bytes 6291460
  118.6 54.5 %all-to-all-start.2 = ((bf16[8,128,1024]{2,1,0:T(8,128)(2,1)}), bf16[8,128,1024]{2,1,0:T(8,128)(2,1)}, u32[]{:S(2)}, u32[]{:S(2)}) async-start(bf16[8,128,1024]{2,1,0:T(8,128)(2,1)} %get-tuple-element.70), calls=%async_computation.2 | async-start | bytes 4194304 | tf_op jit(solution)/shard_map/all_to_all | solution.py:316
  123.2 100.0 %reduce-scatter.6.cloned.1.call-start = ((), (), s32[]{:S(2)}) async-start(), calls=%async_computation.10 | async-start | bytes 2621440 | tf_op jit(solution)/shard_map/reduce_scatter | solution.py:377
  173.2 14.5 %copy-start.9 = (f32[1024,1024,1]{1,0,2:T(8,128)S(1)}, f32[1024,1024,1]{1,0,2:T(8,128)}, u32[]{:S(2)}) copy-start(f32[1024,1024,1]{1,0,2:T(8,128)} %fusion.10) | copy-start | bytes 12582916
  186.4 1.3 copy-start.2
  193.8 63.9 %reduce-scatter.8.cloned.1.call-start = ((), (), s32[]{:S(2)}) async-start(), calls=%async_computation.11 | async-start | bytes 2621440 | tf_op jit(solution)/shard_map/reduce_scatter | solution.py:377
  194.1 4.8 %copy-start.10 = (bf16[8,128,1024]{2,1,0:T(8,128)(2,1)S(1)}, bf16[8,128,1024]{2,1,0:T(8,128)(2,1)}, u32[]{:S(2)}) copy-start(bf16[8,128,1024]{2,1,0:T(8,128)(2,1)} %get-tuple-element.83) | copy-start | bytes 6291460
  202.8 126.1 %reduce-scatter.4.cloned.1.call-start = ((), (), s32[]{:S(2)}) async-start(), calls=%async_computation.9 | async-start | bytes 2359296 | tf_op jit(solution)/shard_map/reduce_scatter | solution.py:360
  203.4 57.0 %all-to-all-start.3 = ((bf16[8,128,1024]{2,1,0:T(8,128)(2,1)}), bf16[8,128,1024]{2,1,0:T(8,128)(2,1)S(1)}, u32[]{:S(2)}, u32[]{:S(2)}) async-start(bf16[8,128,1024]{2,1,0:T(8,128)(2,1)} %copy-done.2), calls=%async_computation.3 | async-start | bytes 4194304 | tf_op jit(solution)/shard_map/all_to_all | solution.py:316
  328.8 0.9 copy-start.3
Sparse Core Ops, SparseCore 0:
  48.8 53.5 all-gather.5
  104.0 32.9 all-gather.3
  193.9 29.1 reduce-scatter.5
  226.2 31.4 reduce-scatter.7
  261.1 67.7 reduce-scatter.3

commit v2 on v1

v2 whole, which is shorter than its diff:
```python
import functools
import math

import jax
import jax.numpy as jnp
from jax import lax
from jax.experimental import pallas as pl
from jax.experimental.pallas import tpu as pltpu
from jax.sharding import PartitionSpec as P

BLOCK = 128
LANES = 128
MB = 1 << 20
F32 = jnp.float32
BF16 = jnp.bfloat16


def sigmoid(x):
    return 1.0 / (1.0 + jnp.exp(-x))


def resident(shape):
    return pl.BlockSpec(shape, lambda *_: (0,) * len(shape))


def pick_kernel(ids_ref, rows_ref, out_ref):
    count, total = out_ref.shape[0], rows_ref.shape[0]
    places = lax.broadcasted_iota(jnp.int32, (count, total), 1)
    ones = jnp.where(places == ids_ref[...], 1.0, 0.0).astype(BF16)
    out_ref[...] = jnp.dot(ones, rows_ref[...], preferred_element_type=F32).astype(BF16)


def pick_rows(rows, ids):
    return pl.pallas_call(
        pick_kernel,
        out_shape=jax.ShapeDtypeStruct((ids.shape[0], rows.shape[1]), rows.dtype),
        compiler_params=pltpu.CompilerParams(vmem_limit_bytes=24 * MB),
        name="pick_rows",
    )(ids[:, None], rows)


def step_source(info_ref, step, half, mirror):
    sets = info_ref.shape[1] - 1
    base = info_ref[0, sets] // half * half
    dataset = lax.rem(base + (half if mirror else 0) + step // 2, sets)
    rank = lax.rem(step, 2)
    start = jnp.int32(0)
    blocks = jnp.int32(0)
    for candidate in range(sets):
        here = info_ref[0, candidate] // BLOCK
        start = start + jnp.where(candidate < dataset, here, 0)
        blocks = jnp.where(candidate == dataset, here, blocks)
    live = rank < blocks
    return jnp.where(live, start + rank, 0), live


def encode_kernel(
    half, mirror, bond_count, unroll, info_ref, codes_ref, atoms_ref, low_ref, high_ref,
    weight_ref, gain_ref, out_ref, plain, gained, products, gates, mixed, message,
):
    step = pl.program_id(0)
    rows, width = atoms_ref.shape
    depth = low_ref.shape[0]
    tall = width // LANES
    @pl.when(step == 0)
    def _():
        def spread(ref, at, base):
            for k in range(tall):
                lanes = slice(k * LANES, (k + 1) * LANES)
                value = ref[pl.ds(at, BLOCK), lanes].astype(F32)
                place = pl.ds(base * tall + k, BLOCK, stride=tall)
                plain[place, :] = value
                gained[place, :] = value * gain_ref[:, lanes]

        for at in range(0, rows, BLOCK):
            spread(atoms_ref, at, at)
        for at in range(0, depth, BLOCK):
            spread(low_ref, at, rows + at)
            spread(high_ref, at, rows + depth + at)

    source, live = step_source(info_ref, step, half, mirror)
    base = pl.multiple_of(source * BLOCK, BLOCK)

    def row_of(ref, place):
        return ref[pl.ds(pl.multiple_of(place, tall), tall), :]

    def encode():
        def score(outer, carry):
            for inner in range(unroll):
                atom = outer * unroll + inner
                for bond in range(bond_count):
                    code = codes_ref[bond * rows + base + atom]
                    bonded = row_of(plain, code >> 16)
                    partner = row_of(gained, code & 0xFFFF)
                    place = pl.multiple_of((atom * bond_count + bond) * tall, tall)
                    products[pl.ds(place, tall), :] = bonded * partner
            return carry

        lax.fori_loop(0, BLOCK // unroll, score, 0)
        pairs = BLOCK * bond_count
        total = products[pl.ds(0, pairs, stride=tall), :]
        for k in range(1, tall):
            total = total + products[pl.ds(k, pairs, stride=tall), :]
        logits = jnp.sum(total, axis=1, keepdims=True) * (1.0 / math.sqrt(width))
        gates[...] = jnp.broadcast_to(sigmoid(logits), gates.shape)

        def mix(outer, carry):
            for inner in range(unroll):
                atom = outer * unroll + inner
                acc = None
                for bond in range(bond_count):
                    code = codes_ref[bond * rows + base + atom]
                    gate = gates[pl.ds(atom * bond_count + bond, 1), :]
                    term = row_of(plain, code >> 16) * gate
                    acc = term if acc is None else acc + term
                mixed[pl.ds(pl.multiple_of(atom * tall, tall), tall), :] = acc
            return carry

        lax.fori_loop(0, BLOCK // unroll, mix, 0)
        for k in range(tall):
            part = mixed[pl.ds(k, BLOCK, stride=tall), :]
            message[:, k * LANES : (k + 1) * LANES] = part.astype(BF16)
        update = jnp.dot(message[...], weight_ref[...], preferred_element_type=F32)
        own = atoms_ref[pl.ds(base, BLOCK), :].astype(F32)
        return (own + update * sigmoid(update)).astype(BF16)

    @pl.when(live)
    def _():
        out_ref[0] = encode()

    @pl.when(jnp.logical_not(live))
    def _():
        out_ref[...] = jnp.zeros_like(out_ref)


def encode(info, codes, atoms, low, high, weight, gain, bond_count, half, mirror):
    rows, width = atoms.shape
    depth = low.shape[0]
    tall = width // LANES
    extended = rows + 2 * depth
    blocks = pl.pallas_call(
        functools.partial(encode_kernel, half, mirror, bond_count, 4),
        grid_spec=pltpu.PrefetchScalarGridSpec(
            num_scalar_prefetch=2,
            grid=(2 * half,),
            in_specs=[
                resident((rows, width)),
                resident((depth, width)),
                resident((depth, width)),
                resident((width, width)),
                resident((1, width)),
            ],
            out_specs=pl.BlockSpec((1, BLOCK, width), lambda t, *_: (t, 0, 0)),
            scratch_shapes=[
                pltpu.VMEM((extended * tall, LANES), F32),
                pltpu.VMEM((extended * tall, LANES), F32),
                pltpu.VMEM((BLOCK * bond_count * tall, LANES), F32),
                pltpu.VMEM((BLOCK * bond_count, LANES), F32),
                pltpu.VMEM((BLOCK * tall, LANES), F32),
                pltpu.VMEM((BLOCK, width), BF16),
            ],
        ),
        out_shape=jax.ShapeDtypeStruct((2 * half, BLOCK, width), BF16),
        compiler_params=pltpu.CompilerParams(vmem_limit_bytes=48 * MB),
        cost_estimate=pl.CostEstimate(
            flops=rows * width * width,
            bytes_accessed=30 * MB,
            transcendentals=rows * width,
        ),
        name="encode_mirror" if mirror else "encode_own",
    )(info, codes, atoms, low, high, weight, gain)
    return blocks.reshape(half, 2, BLOCK, width)


def head_kernel(rows_ref, weight_ref, back_ref, act_ref, low_grad_ref, high_grad_ref):
    width = rows_ref.shape[-1]
    shape = rows_ref.shape
    x = rows_ref[...].reshape(-1, width)
    some = jnp.max(jnp.abs(x.astype(F32))) > 0

    @pl.when(some)
    def _():
        low = weight_ref[:, 0].reshape(width, width)
        high = weight_ref[:, 1].reshape(width, width)
        transposed = (((1,), (1,)), ((), ()))
        z = jnp.dot(x, low, preferred_element_type=F32)
        s = sigmoid(z)
        act = (z * s).astype(BF16)
        act_ref[...] = act.reshape(shape)
        slope = s * (1.0 + z * (1.0 - s))
        err = jnp.dot(act, high, preferred_element_type=F32) - x.astype(F32)
        grad = err.astype(BF16)
        high_grad_ref[...] = grad.reshape(shape)
        up = lax.dot_general(grad, high, transposed, preferred_element_type=F32)
        grad = (up * slope).astype(BF16)
        low_grad_ref[...] = grad.reshape(shape)
        up = lax.dot_general(grad, low, transposed, preferred_element_type=F32)
        back_ref[...] = (up - err).astype(BF16).reshape(shape)

    @pl.when(jnp.logical_not(some))
    def _():
        for ref in (back_ref, act_ref, low_grad_ref, high_grad_ref):
            ref[...] = jnp.zeros_like(ref)


def run_head(rows, weights, name):
    sources, ranks, _, width = rows.shape
    tile = 4 if sources % 4 == 0 else 1
    block = pl.BlockSpec((tile, 1, BLOCK, width), lambda r, t: (t, r, 0, 0))
    total = sources * ranks * BLOCK
    return pl.pallas_call(
        head_kernel,
        grid=(ranks, sources // tile),
        in_specs=[block, resident(weights.shape)],
        out_specs=[block] * 4,
        out_shape=[jax.ShapeDtypeStruct(rows.shape, BF16)] * 4,
        compiler_params=pltpu.CompilerParams(vmem_limit_bytes=48 * MB),
        cost_estimate=pl.CostEstimate(
            flops=8 * total * width * width,
            bytes_accessed=5 * total * width * 2 + weights.size * 2,
            transcendentals=total * width,
        ),
        name=name,
    )(rows, weights)


def block_place(info_ref, block):
    sets = info_ref.shape[1] - 1
    start, dataset, rank = jnp.int32(0), jnp.int32(0), jnp.int32(0)
    for candidate in range(sets):
        blocks = info_ref[0, candidate] // BLOCK
        inside = jnp.logical_and(block >= start, block < start + blocks)
        dataset = jnp.where(inside, candidate, dataset)
        rank = jnp.where(inside, block - start, rank)
        start = start + blocks
    return dataset, rank, info_ref[0, sets]


def place_kernel(half, info_ref, own_ref, mirror_ref, out_ref):
    dataset, _, place = block_place(info_ref, pl.program_id(0))
    is_own = dataset // half == place // half
    out_ref[0] = jnp.where(is_own, own_ref[0, 0], mirror_ref[0, 0])


def place_rows(info, own, mirror, row_blocks):
    half, _, _, width = own.shape
    shape = (1, 1, BLOCK, width)

    def index(of_own, block, info_ref):
        dataset, rank, place = block_place(info_ref, block)
        wanted = (dataset // half == place // half) == of_own
        return jnp.where(wanted, lax.rem(dataset, half), 0), jnp.where(wanted, rank, 0), 0, 0

    return pl.pallas_call(
        functools.partial(place_kernel, half),
        grid_spec=pltpu.PrefetchScalarGridSpec(
            num_scalar_prefetch=1,
            grid=(row_blocks,),
            in_specs=[
                pl.BlockSpec(shape, functools.partial(index, True)),
                pl.BlockSpec(shape, functools.partial(index, False)),
            ],
            out_specs=pl.BlockSpec((1, BLOCK, width), lambda block, *_: (block, 0, 0)),
        ),
        out_shape=jax.ShapeDtypeStruct((row_blocks, BLOCK, width), BF16),
        compiler_params=pltpu.CompilerParams(vmem_limit_bytes=24 * MB),
        name="place_rows",
    )(info, own, mirror)


def halo(cut_rows):
    count = lax.axis_size("dom")
    forward = [(i, i + 1) for i in range(count - 1)]
    backward = [(target, source) for source, target in forward]
    low = lax.ppermute(cut_rows, "dom", forward)
    high = lax.ppermute(cut_rows, "dom", backward)
    return low, high


def exchange(blocks, half):
    groups = [list(range(half)), list(range(half, 2 * half))]
    return lax.all_to_all(
        blocks, "head", split_axis=0, concat_axis=0, axis_index_groups=groups, tiled=True
    )


def across(array, half):
    return lax.ppermute(array, "head", [(i, (i + half) % (2 * half)) for i in range(2 * half)])


def sum_over_dom(share):
    count = lax.axis_size("dom")
    rows, width = share.shape
    if count & (count - 1):
        return lax.psum_scatter(share, "dom", scatter_dimension=0, tiled=True).astype(F32)
    bits = count.bit_length() - 1
    place = lax.axis_index("dom")
    total = share.reshape((2,) * bits + (rows // count, width))
    for bit in range(bits):
        axis = bits - 1 - bit
        mine = (place >> bit) & 1
        keep = lax.dynamic_index_in_dim(total, mine, axis, keepdims=False)
        send = lax.dynamic_index_in_dim(total, 1 - mine, axis, keepdims=False)
        got = lax.ppermute(send, "dom", [(i, i ^ (1 << bit)) for i in range(count)])
        total = keep.astype(F32) + got.astype(F32)
        if bit < bits - 1:
            total = total.astype(BF16)
    return total


def body(atoms, bonds, triplets, halo_ids, counts, enc_weight, gate_gain, head_weight):
    atom_rows = atoms[0]
    row_count, width = atom_rows.shape
    row_blocks = row_count // BLOCK
    bond_count = bonds.shape[1]
    half = lax.axis_size("head") // 2
    tall = width // LANES

    own_weights = lax.all_gather(head_weight[0], "dom", axis=0, tiled=False)
    mirror_weights = lax.all_gather(across(head_weight[0], half), "dom", axis=0, tiled=False)
    low, high = halo(pick_rows(atom_rows, halo_ids[0]))
    codes = ((bonds[0] * tall) * 65536 + triplets[0] * tall).reshape(-1)
    place = lax.axis_index("head").astype(jnp.int32).reshape(1, 1)
    info = jnp.concatenate([counts, place], axis=1)

    def encoded(mirror):
        return encode(
            info, codes, atom_rows, low, high, enc_weight, gate_gain[None, :], bond_count, half,
            mirror,
        )

    scale = 1.0 / math.sqrt(lax.axis_size("dom") * row_count)

    def share(acts, grads):
        product = lax.dot_general(
            acts.reshape(-1, width),
            grads.reshape(-1, width),
            (((0,), (0,)), ((), ())),
            preferred_element_type=F32,
        )
        return sum_over_dom((product * scale).astype(BF16))

    own_rows = exchange(encoded(False), half)
    mirror_rows = exchange(encoded(True), half)
    own_back, own_act, own_low, own_high = run_head(own_rows, own_weights, "head_own")
    own_back = exchange(own_back, half)
    mirror_back, act, low_grad, high_grad = run_head(mirror_rows, mirror_weights, "head_mirror")
    mirror_back = exchange(mirror_back, half)
    high_part = across(share(act, high_grad).astype(BF16), half)
    low_part = across(share(mirror_rows, low_grad).astype(BF16), half)
    head_part = jnp.stack(
        [
            share(own_rows, own_low) + low_part.astype(F32),
            share(own_act, own_high) + high_part.astype(F32),
        ]
    )
    row_part = place_rows(info, own_back, mirror_back, row_blocks)
    return row_part.reshape(1, row_count, width), head_part[None]


def solution(mesh):
    return jax.shard_map(
        body,
        mesh=mesh,
        in_specs=(
            P("dom", "head", None),
            P("dom", None, "head"),
            P("dom", None, "head"),
            P("dom", "head"),
            P("dom", "head"),
            P(),
            P(),
            P("head", None, "dom", None),
        ),
        out_specs=(P("dom", "head", None), P("head", None, "dom", None)),
        check_vma=False,
    )
```

time: 342 us -> 257 us (0.75)
  blocking collectives: 67.4 us -> 0 us
  waiting for transfers between devices: 155 us -> 96 us
  starting transfers between devices: 12.5 us -> 42.8 us
  local copies, waits for them, and re-layouts: 5.39 us -> 17.7 us
  matrix products: 20.7 us -> 15.5 us
  other arithmetic: 3.82 us -> 7.91 us
    reduce_scatter x3 -> x0, waiting for transfers between devices: 119 us -> none  [the longest x1 68.5 us: body(): lax.psum_scatter(sent_b, 'head', scatter_dimension=0, tiled=True)]
    ppermute x0 -> x11, waiting for transfers between devices: none -> 77.8 us  [the longest x3 54.6 us: across(): lax.ppermute(array, 'head', [(i, (i + half) % (2 * half)) for i in range(...]
    all_gather x1 -> x0, blocking collectives: 67.4 us -> none  [body(): every = lax.all_gather(counts, ('dom', 'head'), axis=0, tiled=True)]
    ppermute x0 -> x11, starting transfers between devices: none -> 20.1 us  [the longest x3 11.4 us: across(): lax.ppermute(array, 'head', [(i, (i + half) % (2 * half)) for i in range(...]
    all_gather x2, waiting for transfers between devices: 13.6 us -> 0.02 us  [the longest x1 0.02 us: body(): own_weights = lax.all_gather(head_weight[0], 'dom', axis=0, tiled=False)]
    all_to_all x2 -> x4, starting transfers between devices: 8.13 us -> 18.2 us  [exchange(): lax.all_to_all(blocks, 'head', split_axis=0, concat_axis=0, axis_index_gr...]
    unnamed x23 -> x47, local copies, waits for them, and re-layouts: 3.91 us -> 12.1 us
    convert_element_type x3 -> x6, other arithmetic: 0.02 us -> 5.86 us  [the longest x4 5.46 us: sum_over_dom(): total = total.astype(BF16)]
  transfers between devices with their start and end apart: 9 -> 19, of which waited for: 6 -> 7; matrix products, arithmetic and copies ran while one was open for 5% -> 11% of each run, Pallas kernels for 4% -> 21%
where the time goes in v2:
time: 257 us; the launch traced here: 255 us
  waiting for transfers between devices  96 us (37%)
  Pallas kernels  60.1 us (23%)
  starting transfers between devices  42.8 us (17%)
  local copies, waits for them, and re-layouts  17.7 us (7%)
  matrix products  15.5 us (6%)
  between operations  14.4 us (6%)
  other arithmetic  7.91 us (3%)
    ppermute x3, waiting for transfers between devices, across(): lax.ppermute(array, 'head', [(i, (i + half) % (2 * half)) for i in range(...  54.6 us
    pallas_call x2, Pallas kernels, encode(): pl.pallas_call(functools.partial(encode_kernel, half, mirror, bond_count,...  34 us
    ppermute x8, waiting for transfers between devices, sum_over_dom(): got = lax.ppermute(send, 'dom', [(i, i ^ 1 << bit) for i in range(count)])  23.3 us
    pallas_call x2, Pallas kernels, run_head(): pl.pallas_call(head_kernel, grid=(ranks, sources // tile), in_specs=[bloc...  19.6 us
    all_to_all x4, starting transfers between devices, exchange(): lax.all_to_all(blocks, 'head', split_axis=0, concat_axis=0, axis_index_gr...  18.2 us
    all_to_all x4, waiting for transfers between devices, exchange(): lax.all_to_all(blocks, 'head', split_axis=0, concat_axis=0, axis_index_gr...  17.5 us
    dot_general x4, matrix products, share(): lax.dot_general(acts.reshape(-1, width), grads.reshape(-1, width), (((0,)...  15.5 us
    unnamed x47, local copies, waits for them, and re-layouts  12.1 us
  transfers between devices with their start and end apart: 19, of which 7 were waited for; matrix products, arithmetic and copies ran while one was open for 11% of the time, Pallas kernels for 21%

profile of v2, /device:TPU:0, one launch (start us, length us, event | category | flops | bytes accessed | tf_op | source)
XLA Modules:
  0.0 254.5 jit_solution(12598410869314177920)
XLA Ops:
  12.2 3.0 %collective-permute-start = (bf16[128,1024]{1,0:T(8,128)(2,1)S(1)}, bf16[128,1024]{1,0:T(8,128)(2,1)S(1)}, u32[]{:S(2)}, u32[]{:S(2)}) collective-permute-start(bf16[128,1024]{1,0:T(8,128)(2,1)S(1)} %pick_rows.1), channel_id=1, source_target_pairs={{0,8},{8,16},{16,24},{1,9},{9,17},{17,25},{2,10},{10,18},{18,26},{... | collective-permute-start | bytes 786440 | tf_op jit(solution)/shard_map/ppermute | solution.py:275
  15.3 4.1 %collective-permute-start.2 = (bf16[2,256,1024]{2,1,0:T(8,128)(2,1)}, bf16[2,256,1024]{2,1,0:T(8,128)(2,1)}, u32[]{:S(2)}, u32[]{:S(2)}) collective-permute-start(bf16[2,256,1024]{2,1,0:T(8,128)(2,1)} %bitcast.122), channel_id=1, source_target_pairs={{0,4},{1,5},{2,6},{3,7},{4,0},{5,1},{6,2},{7,3},{8,12},{9,13},{10,... | collective-permute-start | bytes 3145736 | tf_op jit(solution)/shard_map/ppermute | solution.py:288
  19.5 17.3 %encode_own.1 = bf16[8,128,1024]{2,1,0:T(8,128)(2,1)S(1)} custom-call(s32[1,9]{1,0:T(1,128)S(1)} %pad_add_fusion.info_ref, s32[4096]{0:T(1024)S(1)} %bitcast.109, bf16[1024,1024]{1,0:T(8,128)(2,1)S(1)} %bitcast.105, bf16[128,1024]{1,0:T(8,128)(2,1)S(1)} %collective-permute-done.low_ref, bf16[128,1024]{1,0:T(8,128)(2,1)S(1)} %collective-permute-done.1.high_ref, ...), custom_call_target="tpu_custom_call" | custom-call | flops 1073741824 | bytes 31457280 | tf_op jit(solution)/shard_map/encode_own/pallas_call | solution.py:141
  38.1 6.4 %all-to-all-start = ((bf16[4,2,128,1024]{3,2,1,0:T(8,128)(2,1)}), bf16[4,2,128,1024]{3,2,1,0:T(8,128)(2,1)}, u32[]{:S(2)}, u32[]{:S(2)}) async-start(bf16[4,2,128,1024]{3,2,1,0:T(8,128)(2,1)} %bitcast.108), calls=%async_computation | async-start | bytes 4194304 | tf_op jit(solution)/shard_map/all_to_all | solution.py:282
  44.5 21.4 %collective-permute-done.2 = bf16[2,256,1024]{2,1,0:T(8,128)(2,1)} collective-permute-done((bf16[2,256,1024]{2,1,0:T(8,128)(2,1)}, bf16[2,256,1024]{2,1,0:T(8,128)(2,1)}, u32[]{:S(2)}, u32[]{:S(2)}) %collective-permute-start.2) | collective-permute-done | bytes 1048608 | tf_op jit(solution)/shard_map/ppermute | solution.py:288
  65.9 16.8 %encode_mirror.1 = bf16[8,128,1024]{2,1,0:T(8,128)(2,1)S(1)} custom-call(s32[1,9]{1,0:T(1,128)S(1)} %pad_add_fusion.info_ref, s32[4096]{0:T(1024)S(1)} %bitcast.110, bf16[1024,1024]{1,0:T(8,128)(2,1)S(1)} %bitcast.106, bf16[128,1024]{1,0:T(8,128)(2,1)S(1)} %collective-permute-done.low_ref, bf16[128,1024]{1,0:T(8,128)(2,1)S(1)} %collective-permute-done.1.high_ref, ...), custom_call_target="tpu_custom_call" | custom-call | flops 1073741824 | bytes 31457280 | tf_op jit(solution)/shard_map/encode_mirror/pallas_call | solution.py:141
  84.1 4.5 %all-to-all-done.rows_ref = bf16[4,2,128,1024]{3,2,1,0:T(8,128)(2,1)} async-done(((bf16[4,2,128,1024]{3,2,1,0:T(8,128)(2,1)}), bf16[4,2,128,1024]{3,2,1,0:T(8,128)(2,1)}, u32[]{:S(2)}, u32[]{:S(2)}) %all-to-all-start) | async-done | bytes 2097184 | tf_op jit(solution)/shard_map/all_to_all | solution.py:282
  88.6 3.6 %all-to-all-start.2 = ((bf16[4,2,128,1024]{3,2,1,0:T(8,128)(2,1)}), bf16[4,2,128,1024]{3,2,1,0:T(8,128)(2,1)S(1)}, u32[]{:S(2)}, u32[]{:S(2)}) async-start(bf16[4,2,128,1024]{3,2,1,0:T(8,128)(2,1)} %bitcast.107), calls=%async_computation.2 | async-start | bytes 4194304 | tf_op jit(solution)/shard_map/all_to_all | solution.py:282
  92.2 9.7 %head_own.1 = (bf16[4,2,128,1024]{3,2,1,0:T(8,128)(2,1)S(1)}, bf16[4,2,128,1024]{3,2,1,0:T(8,128)(2,1)S(1)}, bf16[4,2,128,1024]{3,2,1,0:T(8,128)(2,1)}, bf16[4,2,128,1024]{3,2,1,0:T(8,128)(2,1)}) custom-call(bf16[4,2,128,1024]{3,2,1,0:T(8,128)(2,1)} %all-to-all-done.rows_ref, bf16[4,2,256,1024]{3,2,1,0:T(8,128)(2,1)} %all-gather.4.cloned.1.call-done.weight_ref), custom_call_target="tpu_custom_call" | custom-call | flops 8589934592 | bytes 14680064 | tf_op jit(solution)/shard_map/head_own/pallas_call | solution.py:211
  104.7 13.0 %all-to-all-done.2.rows_ref = bf16[4,2,128,1024]{3,2,1,0:T(8,128)(2,1)S(1)} async-done(((bf16[4,2,128,1024]{3,2,1,0:T(8,128)(2,1)}), bf16[4,2,128,1024]{3,2,1,0:T(8,128)(2,1)S(1)}, u32[]{:S(2)}, u32[]{:S(2)}) %all-to-all-start.2) | async-done | bytes 2097184 | tf_op jit(solution)/shard_map/all_to_all | solution.py:282
  119.1 3.8 %all-to-all-start.1 = ((bf16[4,2,128,1024]{3,2,1,0:T(8,128)(2,1)}), bf16[4,2,128,1024]{3,2,1,0:T(8,128)(2,1)S(1)}, u32[]{:S(2)}, u32[]{:S(2)}) async-start(bf16[4,2,128,1024]{3,2,1,0:T(8,128)(2,1)} %copy-done.5), calls=%async_computation.1 | async-start | bytes 4194304 | tf_op jit(solution)/shard_map/all_to_all | solution.py:282
  122.9 4.6 %fusion.3 = bf16[1024,1024]{1,0:T(8,128)(2,1)S(1)} fusion(bf16[4,2,128,1024]{3,2,1,0:T(8,128)(2,1)} %all-to-all-done.rows_ref, bf16[4,2,128,1024]{3,2,1,0:T(8,128)(2,1)} %get-tuple-element.12), kind=kOutput, calls=%fused_computation.7 | convolution fusion | flops 2149580800 | bytes 6291456 | tf_op jit(solution)/shard_map/dot_general | solution.py:335
  129.9 9.9 %head_mirror.1 = (bf16[4,2,128,1024]{3,2,1,0:T(8,128)(2,1)S(1)}, bf16[4,2,128,1024]{3,2,1,0:T(8,128)(2,1)S(1)}, bf16[4,2,128,1024]{3,2,1,0:T(8,128)(2,1)}, bf16[4,2,128,1024]{3,2,1,0:T(8,128)(2,1)}) custom-call(bf16[4,2,128,1024]{3,2,1,0:T(8,128)(2,1)} %copy-done.16, bf16[4,2,256,1024]{3,2,1,0:T(8,128)(2,1)} %bitcast.124), custom_call_target="tpu_custom_call" | custom-call | flops 8589934592 | bytes 14680064 | tf_op jit(solution)/shard_map/head_mirror/pallas_call | solution.py:211
  139.8 4.7 %fusion.2 = bf16[1024,1024]{1,0:T(8,128)(2,1)S(1)} fusion(bf16[4,2,128,1024]{3,2,1,0:T(8,128)(2,1)S(1)} %copy-done.17, bf16[4,2,128,1024]{3,2,1,0:T(8,128)(2,1)} %get-tuple-element.13), kind=kOutput, calls=%fused_computation.5 | convolution fusion | flops 2149580800 | bytes 6291456 | tf_op jit(solution)/shard_map/dot_general | solution.py:335
  152.4 3.7 %fusion.1 = bf16[1024,1024]{1,0:T(8,128)(2,1)} fusion(bf16[4,2,128,1024]{3,2,1,0:T(8,128)(2,1)S(1)} %copy-done.8, bf16[4,2,128,1024]{3,2,1,0:T(8,128)(2,1)S(1)} %copy-done.21), kind=kOutput, calls=%fused_computation.3 | convolution fusion | flops 2149580800 | bytes 6291456 | tf_op jit(solution)/shard_map/dot_general | solution.py:335
  156.2 4.5 %all-to-all-start.3 = ((bf16[4,2,128,1024]{3,2,1,0:T(8,128)(2,1)}), bf16[4,2,128,1024]{3,2,1,0:T(8,128)(2,1)}, u32[]{:S(2)}, u32[]{:S(2)}) async-start(bf16[4,2,128,1024]{3,2,1,0:T(8,128)(2,1)} %copy-done.4), calls=%async_computation.3 | async-start | bytes 4194304 | tf_op jit(solution)/shard_map/all_to_all | solution.py:282
  164.4 3.0 %collective-permute-start.4 = (bf16[256,1024]{1,0:T(8,128)(2,1)S(1)}, bf16[256,1024]{1,0:T(8,128)(2,1)S(1)}, u32[]{:S(2)}, u32[]{:S(2)}) collective-permute-start(bf16[256,1024]{1,0:T(8,128)(2,1)S(1)} %dynamic-slice_bitcast_fusion.7), channel_id=1, source_target_pairs={{0,16},{8,24},{16,0},{24,8},{1,17},{9,25},{17,1},{25,9},{2,18},{10... | collective-permute-start | bytes 1572872 | tf_op jit(solution)/shard_map/ppermute | solution.py:304
  173.4 18.0 %collective-permute-done.6 = bf16[256,1024]{1,0:T(8,128)(2,1)S(1)} collective-permute-done((bf16[256,1024]{1,0:T(8,128)(2,1)S(1)}, bf16[256,1024]{1,0:T(8,128)(2,1)S(1)}, u32[]{:S(2)}, u32[]{:S(2)}) %collective-permute-start.6) | collective-permute-done | bytes 524320 | tf_op jit(solution)/shard_map/ppermute | solution.py:304
  191.6 3.6 %collective-permute-start.7 = (bf16[256,1024]{1,0:T(8,128)(2,1)S(1)}, bf16[256,1024]{1,0:T(8,128)(2,1)S(1)}, u32[]{:S(2)}, u32[]{:S(2)}) collective-permute-start(bf16[256,1024]{1,0:T(8,128)(2,1)S(1)} %fusion.11), channel_id=1, source_target_pairs={{0,4},{1,5},{2,6},{3,7},{4,0},{5,1},{6,2},{7,3},{8,12},{9,13},{10,... | collective-permute-start | bytes 1572872 | tf_op jit(solution)/shard_map/ppermute | solution.py:288
  197.4 5.2 %collective-permute-done.11 = bf16[256,1024]{1,0:T(8,128)(2,1)S(1)} collective-permute-done((bf16[256,1024]{1,0:T(8,128)(2,1)S(1)}, bf16[256,1024]{1,0:T(8,128)(2,1)S(1)}, u32[]{:S(2)}, u32[]{:S(2)}) %collective-permute-start.11) | collective-permute-done | bytes 524320 | tf_op jit(solution)/shard_map/ppermute | solution.py:304
  202.9 3.6 %collective-permute-start.12 = (bf16[256,1024]{1,0:T(8,128)(2,1)S(1)}, bf16[256,1024]{1,0:T(8,128)(2,1)S(1)}, u32[]{:S(2)}, u32[]{:S(2)}) collective-permute-start(bf16[256,1024]{1,0:T(8,128)(2,1)S(1)} %fusion.8), channel_id=1, source_target_pairs={{0,4},{1,5},{2,6},{3,7},{4,0},{5,1},{6,2},{7,3},{8,12},{9,13},{10,... | collective-permute-start | bytes 1572872 | tf_op jit(solution)/shard_map/ppermute | solution.py:288
  206.5 24.1 %collective-permute-done.7 = bf16[256,1024]{1,0:T(8,128)(2,1)S(1)} collective-permute-done((bf16[256,1024]{1,0:T(8,128)(2,1)S(1)}, bf16[256,1024]{1,0:T(8,128)(2,1)S(1)}, u32[]{:S(2)}, u32[]{:S(2)}) %collective-permute-start.7) | collective-permute-done | bytes 524320 | tf_op jit(solution)/shard_map/ppermute | solution.py:288
  230.9 9.1 %collective-permute-done.12 = bf16[256,1024]{1,0:T(8,128)(2,1)S(1)} collective-permute-done((bf16[256,1024]{1,0:T(8,128)(2,1)S(1)}, bf16[256,1024]{1,0:T(8,128)(2,1)S(1)}, u32[]{:S(2)}, u32[]{:S(2)}) %collective-permute-start.12) | collective-permute-done | bytes 524320 | tf_op jit(solution)/shard_map/ppermute | solution.py:288
  241.7 6.0 %place_rows.1 = bf16[8,128,1024]{2,1,0:T(8,128)(2,1)} custom-call(s32[1,9]{1,0:T(1,128)S(1)} %pad_add_fusion.info_ref, bf16[4,2,128,1024]{3,2,1,0:T(8,128)(2,1)S(1)} %all-to-all-done.1.own_ref, bf16[4,2,128,1024]{3,2,1,0:T(8,128)(2,1)} %all-to-all-done.3.mirror_ref), custom_call_target="tpu_custom_call" | custom-call | tf_op jit(solution)/shard_map/place_rows/pallas_call | solution.py:254
  (93 shorter events, 36.4 us)
Async XLA Ops:
  7.2 12.2 %copy-start.18 = (s32[1,4,1024]{2,1,0:T(4,128)S(1)}, s32[1,4,1024]{2,1,0:T(4,128)}, u32[]{:S(2)}) copy-start(s32[1,4,1024]{2,1,0:T(4,128)} %param.10) | copy-start | bytes 49156
  7.2 12.2 %copy-start.19 = (s32[1,4,1024]{2,1,0:T(4,128)S(1)}, s32[1,4,1024]{2,1,0:T(4,128)}, u32[]{:S(2)}) copy-start(s32[1,4,1024]{2,1,0:T(4,128)} %param.9) | copy-start | bytes 49156
  7.2 12.2 %copy-start.20 = (s32[1,8]{1,0:T(1,128)S(1)}, s32[1,8]{1,0:T(1,128)}, u32[]{:S(2)}) copy-start(s32[1,8]{1,0:T(1,128)} %param.12) | copy-start | bytes 100
  7.2 12.3 %copy-start.6 = (f32[1024]{0:T(1024)S(1)}, f32[1024]{0:T(1024)}, u32[]{:S(2)}) copy-start(f32[1024]{0:T(1024)} %param.14) | copy-start | bytes 12292
  7.2 85.0 %all-gather.4.cloned.1.call-start = ((), (), s32[]{:S(2)}) async-start(), calls=%async_computation.4 | async-start | bytes 5242880 | tf_op jit(solution)/shard_map/all_gather | solution.py:319
  10.8 8.7 %collective-permute-start.1 = (bf16[128,1024]{1,0:T(8,128)(2,1)S(1)}, bf16[128,1024]{1,0:T(8,128)(2,1)S(1)}, u32[]{:S(2)}, u32[]{:S(2)}) collective-permute-start(bf16[128,1024]{1,0:T(8,128)(2,1)S(1)} %pick_rows.1), channel_id=1, source_target_pairs={{8,0},{16,8},{24,16},{9,1},{17,9},{25,17},{10,2},{18,10},{26,18},{... | collective-permute-start | bytes 786440 | tf_op jit(solution)/shard_map/ppermute | solution.py:276
  12.2 7.3 %collective-permute-start = (bf16[128,1024]{1,0:T(8,128)(2,1)S(1)}, bf16[128,1024]{1,0:T(8,128)(2,1)S(1)}, u32[]{:S(2)}, u32[]{:S(2)}) collective-permute-start(bf16[128,1024]{1,0:T(8,128)(2,1)S(1)} %pick_rows.1), channel_id=1, source_target_pairs={{0,8},{8,16},{16,24},{1,9},{9,17},{17,25},{2,10},{10,18},{18,26},{... | collective-permute-start | bytes 786440 | tf_op jit(solution)/shard_map/ppermute | solution.py:275
  15.3 50.6 %collective-permute-start.2 = (bf16[2,256,1024]{2,1,0:T(8,128)(2,1)}, bf16[2,256,1024]{2,1,0:T(8,128)(2,1)}, u32[]{:S(2)}, u32[]{:S(2)}) collective-permute-start(bf16[2,256,1024]{2,1,0:T(8,128)(2,1)} %bitcast.122), channel_id=1, source_target_pairs={{0,4},{1,5},{2,6},{3,7},{4,0},{5,1},{6,2},{7,3},{8,12},{9,13},{10,... | collective-permute-start | bytes 3145736 | tf_op jit(solution)/shard_map/ppermute | solution.py:288
  38.1 50.4 %all-to-all-start = ((bf16[4,2,128,1024]{3,2,1,0:T(8,128)(2,1)}), bf16[4,2,128,1024]{3,2,1,0:T(8,128)(2,1)}, u32[]{:S(2)}, u32[]{:S(2)}) async-start(bf16[4,2,128,1024]{3,2,1,0:T(8,128)(2,1)} %bitcast.108), calls=%async_computation | async-start | bytes 4194304 | tf_op jit(solution)/shard_map/all_to_all | solution.py:282
  44.5 85.4 %all-gather.6.cloned.1.call-start = ((), (), s32[]{:S(2)}) async-start(), calls=%async_computation.5 | async-start | bytes 5242880 | tf_op jit(solution)/shard_map/all_gather | solution.py:320
  88.6 29.1 %all-to-all-start.2 = ((bf16[4,2,128,1024]{3,2,1,0:T(8,128)(2,1)}), bf16[4,2,128,1024]{3,2,1,0:T(8,128)(2,1)S(1)}, u32[]{:S(2)}, u32[]{:S(2)}) async-start(bf16[4,2,128,1024]{3,2,1,0:T(8,128)(2,1)} %bitcast.107), calls=%async_computation.2 | async-start | bytes 4194304 | tf_op jit(solution)/shard_map/all_to_all | solution.py:282
  119.1 37.1 %all-to-all-start.1 = ((bf16[4,2,128,1024]{3,2,1,0:T(8,128)(2,1)}), bf16[4,2,128,1024]{3,2,1,0:T(8,128)(2,1)S(1)}, u32[]{:S(2)}, u32[]{:S(2)}) async-start(bf16[4,2,128,1024]{3,2,1,0:T(8,128)(2,1)} %copy-done.5), calls=%async_computation.1 | async-start | bytes 4194304 | tf_op jit(solution)/shard_map/all_to_all | solution.py:282
  129.9 32.8 %collective-permute-start.3 = (bf16[2,256,1024]{2,1,0:T(8,128)(2,1)}, bf16[2,256,1024]{2,1,0:T(8,128)(2,1)}, u32[]{:S(2)}, u32[]{:S(2)}) collective-permute-start(bf16[2,256,1024]{2,1,0:T(8,128)(2,1)} %dynamic-slice_bitcast_fusion.3), channel_id=1, source_target_pairs={{0,8},{8,0},{16,24},{24,16},{1,9},{9,1},{17,25},{25,17},{2,10},{10... | collective-permute-start | bytes 3145736 | tf_op jit(solution)/shard_map/ppermute | solution.py:304
  129.9 9.9 %copy-start.17 = (bf16[4,2,128,1024]{3,2,1,0:T(8,128)(2,1)S(1)}, bf16[4,2,128,1024]{3,2,1,0:T(8,128)(2,1)}, u32[]{:S(2)}) copy-start(bf16[4,2,128,1024]{3,2,1,0:T(8,128)(2,1)} %copy-done.16) | copy-start | bytes 6291460
  145.6 21.8 %collective-permute-start.5 = (bf16[2,256,1024]{2,1,0:T(8,128)(2,1)}, bf16[2,256,1024]{2,1,0:T(8,128)(2,1)}, u32[]{:S(2)}, u32[]{:S(2)}) collective-permute-start(bf16[2,256,1024]{2,1,0:T(8,128)(2,1)} %dynamic-slice_bitcast_fusion.2), channel_id=1, source_target_pairs={{0,8},{8,0},{16,24},{24,16},{1,9},{9,1},{17,25},{25,17},{2,10},{10... | collective-permute-start | bytes 3145736 | tf_op jit(solution)/shard_map/ppermute | solution.py:304
  150.8 18.5 %collective-permute-start.10 = (bf16[2,256,1024]{2,1,0:T(8,128)(2,1)}, bf16[2,256,1024]{2,1,0:T(8,128)(2,1)}, u32[]{:S(2)}, u32[]{:S(2)}) collective-permute-start(bf16[2,256,1024]{2,1,0:T(8,128)(2,1)} %dynamic-slice_bitcast_fusion), channel_id=1, source_target_pairs={{0,8},{8,0},{16,24},{24,16},{1,9},{9,1},{17,25},{25,17},{2,10},{10... | collective-permute-start | bytes 3145736 | tf_op jit(solution)/shard_map/ppermute | solution.py:304
  156.2 85.5 %all-to-all-start.3 = ((bf16[4,2,128,1024]{3,2,1,0:T(8,128)(2,1)}), bf16[4,2,128,1024]{3,2,1,0:T(8,128)(2,1)}, u32[]{:S(2)}, u32[]{:S(2)}) async-start(bf16[4,2,128,1024]{3,2,1,0:T(8,128)(2,1)} %copy-done.4), calls=%async_computation.3 | async-start | bytes 4194304 | tf_op jit(solution)/shard_map/all_to_all | solution.py:282
  162.1 10.8 %collective-permute-start.8 = (bf16[2,256,1024]{2,1,0:T(8,128)(2,1)S(1)}, bf16[2,256,1024]{2,1,0:T(8,128)(2,1)S(1)}, u32[]{:S(2)}, u32[]{:S(2)}) collective-permute-start(bf16[2,256,1024]{2,1,0:T(8,128)(2,1)S(1)} %dynamic-slice_bitcast_fusion.1), channel_id=1, source_target_pairs={{0,8},{8,0},{16,24},{24,16},{1,9},{9,1},{17,25},{25,17},{2,10},{10... | collective-permute-start | bytes 3145736 | tf_op jit(solution)/shard_map/ppermute | solution.py:304
  164.4 42.1 %collective-permute-start.4 = (bf16[256,1024]{1,0:T(8,128)(2,1)S(1)}, bf16[256,1024]{1,0:T(8,128)(2,1)S(1)}, u32[]{:S(2)}, u32[]{:S(2)}) collective-permute-start(bf16[256,1024]{1,0:T(8,128)(2,1)S(1)} %dynamic-slice_bitcast_fusion.7), channel_id=1, source_target_pairs={{0,16},{8,24},{16,0},{24,8},{1,17},{9,25},{17,1},{25,9},{2,18},{10... | collective-permute-start | bytes 1572872 | tf_op jit(solution)/shard_map/ppermute | solution.py:304
  169.1 22.3 %collective-permute-start.6 = (bf16[256,1024]{1,0:T(8,128)(2,1)S(1)}, bf16[256,1024]{1,0:T(8,128)(2,1)S(1)}, u32[]{:S(2)}, u32[]{:S(2)}) collective-permute-start(bf16[256,1024]{1,0:T(8,128)(2,1)S(1)} %dynamic-slice_bitcast_fusion.6), channel_id=1, source_target_pairs={{0,16},{8,24},{16,0},{24,8},{1,17},{9,25},{17,1},{25,9},{2,18},{10... | collective-permute-start | bytes 1572872 | tf_op jit(solution)/shard_map/ppermute | solution.py:304
  171.1 31.5 %collective-permute-start.11 = (bf16[256,1024]{1,0:T(8,128)(2,1)S(1)}, bf16[256,1024]{1,0:T(8,128)(2,1)S(1)}, u32[]{:S(2)}, u32[]{:S(2)}) collective-permute-start(bf16[256,1024]{1,0:T(8,128)(2,1)S(1)} %dynamic-slice_bitcast_fusion.4), channel_id=1, source_target_pairs={{0,16},{8,24},{16,0},{24,8},{1,17},{9,25},{17,1},{25,9},{2,18},{10... | collective-permute-start | bytes 1572872 | tf_op jit(solution)/shard_map/ppermute | solution.py:304
  191.6 39.0 %collective-permute-start.7 = (bf16[256,1024]{1,0:T(8,128)(2,1)S(1)}, bf16[256,1024]{1,0:T(8,128)(2,1)S(1)}, u32[]{:S(2)}, u32[]{:S(2)}) collective-permute-start(bf16[256,1024]{1,0:T(8,128)(2,1)S(1)} %fusion.11), channel_id=1, source_target_pairs={{0,4},{1,5},{2,6},{3,7},{4,0},{5,1},{6,2},{7,3},{8,12},{9,13},{10,... | collective-permute-start | bytes 1572872 | tf_op jit(solution)/shard_map/ppermute | solution.py:288
  195.3 35.5 %collective-permute-start.9 = (bf16[256,1024]{1,0:T(8,128)(2,1)S(1)}, bf16[256,1024]{1,0:T(8,128)(2,1)S(1)}, u32[]{:S(2)}, u32[]{:S(2)}) collective-permute-start(bf16[256,1024]{1,0:T(8,128)(2,1)S(1)} %dynamic-slice_bitcast_fusion.5), channel_id=1, source_target_pairs={{0,16},{8,24},{16,0},{24,8},{1,17},{9,25},{17,1},{25,9},{2,18},{10... | collective-permute-start | bytes 1572872 | tf_op jit(solution)/shard_map/ppermute | solution.py:304
  202.9 37.1 %collective-permute-start.12 = (bf16[256,1024]{1,0:T(8,128)(2,1)S(1)}, bf16[256,1024]{1,0:T(8,128)(2,1)S(1)}, u32[]{:S(2)}, u32[]{:S(2)}) collective-permute-start(bf16[256,1024]{1,0:T(8,128)(2,1)S(1)} %fusion.8), channel_id=1, source_target_pairs={{0,4},{1,5},{2,6},{3,7},{4,0},{5,1},{6,2},{7,3},{8,12},{9,13},{10,... | collective-permute-start | bytes 1572872 | tf_op jit(solution)/shard_map/ppermute | solution.py:288
  (18 other events, 52.8 us)
Sparse Core Ops, SparseCore 0:
  9.6 37.1 all-gather.3
  66.0 35.3 all-gather.5

commit v3 on v2

v3 whole, which is shorter than its diff:
```python
import functools
import math

import jax
import jax.numpy as jnp
from jax import lax
from jax.experimental import pallas as pl
from jax.experimental.pallas import tpu as pltpu
from jax.sharding import PartitionSpec as P

BLOCK = 128
LANES = 128
MB = 1 << 20
VMEM = 58 * MB
F32 = jnp.float32
BF16 = jnp.bfloat16


def sigmoid(x):
    return 1.0 / (1.0 + jnp.exp(-x))


def resident(shape):
    return pl.BlockSpec(shape, lambda *_: (0,) * len(shape))


def pick_kernel(ids_ref, rows_ref, out_ref):
    count, total = out_ref.shape[0], rows_ref.shape[0]
    places = lax.broadcasted_iota(jnp.int32, (count, total), 1)
    ones = jnp.where(places == ids_ref[...], 1.0, 0.0).astype(BF16)
    out_ref[...] = jnp.dot(ones, rows_ref[...], preferred_element_type=F32).astype(BF16)


def pick_rows(rows, ids):
    return pl.pallas_call(
        pick_kernel,
        out_shape=jax.ShapeDtypeStruct((ids.shape[0], rows.shape[1]), rows.dtype),
        compiler_params=pltpu.CompilerParams(vmem_limit_bytes=VMEM),
        name="pick_rows",
    )(ids[:, None], rows)


def step_source(info_ref, step, half, mirror):
    sets = info_ref.shape[1] - 1
    base = info_ref[0, sets] // half * half
    dataset = lax.rem(base + (half if mirror else 0) + step // 2, sets)
    rank = lax.rem(step, 2)
    start = jnp.int32(0)
    blocks = jnp.int32(0)
    for candidate in range(sets):
        here = info_ref[0, candidate] // BLOCK
        start = start + jnp.where(candidate < dataset, here, 0)
        blocks = jnp.where(candidate == dataset, here, blocks)
    live = rank < blocks
    return jnp.where(live, start + rank, 0), live


def fold(arrays):
    rows = lax.broadcasted_iota(jnp.int32, arrays[0].shape, 0)
    for shift in (1, 2, 4):
        first = (rows & shift) == 0
        arrays = [
            jnp.where(first, a, b) + pltpu.roll(jnp.where(first, b, a), 8 - shift, 0)
            for a, b in zip(arrays[::2], arrays[1::2])
        ]
    return arrays[0]


def encode_kernel(
    half, mirror, bond_count, info_ref, codes_ref, atoms_ref, low_ref, high_ref,
    weight_ref, gain_ref, ids_ref, out_ref, plain, gained, partial, gate_rows,
):
    step = pl.program_id(0)
    rows, width = atoms_ref.shape
    depth = low_ref.shape[0]
    tall = width // LANES

    @pl.when(step == 0)
    def _():
        def spread(ref, at, base):
            for k in range(tall):
                lanes = slice(k * LANES, (k + 1) * LANES)
                value = ref[pl.ds(at, BLOCK), lanes].astype(F32)
                place = pl.ds(base * tall + k, BLOCK, stride=tall)
                plain[place, :] = value
                gained[place, :] = value * gain_ref[:, lanes]

        for at in range(0, rows, BLOCK):
            spread(atoms_ref, at, at)
        for at in range(0, depth, BLOCK):
            spread(low_ref, at, rows + at)
            spread(high_ref, at, rows + depth + at)

    source, live = step_source(info_ref, step, half, mirror)
    base = pl.multiple_of(source * BLOCK, BLOCK)

    def row_of(ref, place):
        return ref[pl.ds(pl.multiple_of(place, tall), tall), :]

    def product(code):
        value = row_of(plain, code >> 16) * row_of(gained, code & 0xFFFF)
        return sum(value[k : k + 8] for k in range(0, tall, 8))

    @pl.when(live)
    def _():
        def score(group, carry):
            for bond in range(bond_count):
                at = bond * rows + base + group * 8
                place = pl.multiple_of(bond * BLOCK + group * 8, 8)
                partial[pl.ds(place, 8), :] = fold([product(codes_ref[at + j]) for j in range(8)])
            return carry

        lax.fori_loop(0, BLOCK // 8, score, 0)
        logits = jnp.sum(partial[...], axis=1, keepdims=True) * (1.0 / math.sqrt(width))
        gates = sigmoid(logits)
        ids = ids_ref[pl.ds(base, BLOCK), :]
        total = gate_rows.shape[1]
        for at in range(0, total, LANES):
            places = lax.broadcasted_iota(jnp.int32, (BLOCK, LANES), 1) + at
            acc = jnp.zeros((BLOCK, LANES), F32)
            for bond in range(bond_count):
                gate = gates[bond * BLOCK : (bond + 1) * BLOCK]
                acc = acc + jnp.where(places == ids[:, bond : bond + 1], gate, 0.0)
            gate_rows[:, at : at + LANES] = acc.astype(BF16)
        message = jnp.dot(gate_rows[:, :rows], atoms_ref[...], preferred_element_type=F32)
        for ref, at in ((low_ref, rows), (high_ref, rows + depth)):
            message += jnp.dot(
                gate_rows[:, at : at + depth], ref[...], preferred_element_type=F32
            )
        update = jnp.dot(message.astype(BF16), weight_ref[...], preferred_element_type=F32)
        own = atoms_ref[pl.ds(base, BLOCK), :].astype(F32)
        out_ref[0] = (own + update * sigmoid(update)).astype(BF16)

    @pl.when(jnp.logical_not(live))
    def _():
        out_ref[...] = jnp.zeros_like(out_ref)


def encode(info, codes, atoms, low, high, weight, gain, ids, half, mirror):
    rows, width = atoms.shape
    depth = low.shape[0]
    tall = width // LANES
    extended = rows + 2 * depth
    bond_count = ids.shape[1]
    blocks = pl.pallas_call(
        functools.partial(encode_kernel, half, mirror, bond_count),
        grid_spec=pltpu.PrefetchScalarGridSpec(
            num_scalar_prefetch=2,
            grid=(2 * half,),
            in_specs=[
                resident((rows, width)),
                resident((depth, width)),
                resident((depth, width)),
                resident((width, width)),
                resident((1, width)),
                resident((rows, bond_count)),
            ],
            out_specs=pl.BlockSpec((1, BLOCK, width), lambda t, *_: (t, 0, 0)),
            scratch_shapes=[
                pltpu.VMEM((extended * tall, LANES), F32),
                pltpu.VMEM((extended * tall, LANES), F32),
                pltpu.VMEM((BLOCK * bond_count, LANES), F32),
                pltpu.VMEM((BLOCK, extended), BF16),
            ],
        ),
        out_shape=jax.ShapeDtypeStruct((2 * half, BLOCK, width), BF16),
        compiler_params=pltpu.CompilerParams(vmem_limit_bytes=VMEM),
        cost_estimate=pl.CostEstimate(
            flops=rows * width * width,
            bytes_accessed=30 * MB,
            transcendentals=rows * width,
        ),
        name="encode_mirror" if mirror else "encode_own",
    )(info, codes, atoms, low, high, weight, gain, ids)
    return blocks.reshape(half, 2, BLOCK, width)


def head_kernel(rows_ref, low_ref, high_ref, back_ref, act_ref, low_grad_ref, high_grad_ref):
    width = rows_ref.shape[-1]
    shape = rows_ref.shape
    x = rows_ref[...].reshape(-1, width)
    some = jnp.max(jnp.abs(x.astype(F32))) > 0

    @pl.when(some)
    def _():
        low = low_ref[...].reshape(width, width)
        high = high_ref[...].reshape(width, width)
        transposed = (((1,), (1,)), ((), ()))
        z = jnp.dot(x, low, preferred_element_type=F32)
        s = sigmoid(z)
        act = (z * s).astype(BF16)
        act_ref[...] = act.reshape(shape)
        slope = s * (1.0 + z * (1.0 - s))
        err = jnp.dot(act, high, preferred_element_type=F32) - x.astype(F32)
        grad = err.astype(BF16)
        high_grad_ref[...] = grad.reshape(shape)
        up = lax.dot_general(grad, high, transposed, preferred_element_type=F32)
        grad = (up * slope).astype(BF16)
        low_grad_ref[...] = grad.reshape(shape)
        up = lax.dot_general(grad, low, transposed, preferred_element_type=F32)
        back_ref[...] = (up - err).astype(BF16).reshape(shape)

    @pl.when(jnp.logical_not(some))
    def _():
        for ref in (back_ref, act_ref, low_grad_ref, high_grad_ref):
            ref[...] = jnp.zeros_like(ref)


def run_head(rows, weights, name):
    sources, ranks, _, width = rows.shape
    tile = 4 if sources % 4 == 0 else 1
    block = pl.BlockSpec((tile, 1, BLOCK, width), lambda r, t: (t, r, 0, 0))
    total = sources * ranks * BLOCK
    return pl.pallas_call(
        head_kernel,
        grid=(ranks, sources // tile),
        in_specs=[block] + [resident(w.shape) for w in weights],
        out_specs=[block] * 4,
        out_shape=[jax.ShapeDtypeStruct(rows.shape, BF16)] * 4,
        compiler_params=pltpu.CompilerParams(vmem_limit_bytes=VMEM),
        cost_estimate=pl.CostEstimate(
            flops=8 * total * width * width,
            bytes_accessed=5 * total * width * 2 + width * width * 4,
            transcendentals=total * width,
        ),
        name=name,
    )(rows, *weights)


def block_place(info_ref, block):
    sets = info_ref.shape[1] - 1
    start, dataset, rank = jnp.int32(0), jnp.int32(0), jnp.int32(0)
    for candidate in range(sets):
        blocks = info_ref[0, candidate] // BLOCK
        inside = jnp.logical_and(block >= start, block < start + blocks)
        dataset = jnp.where(inside, candidate, dataset)
        rank = jnp.where(inside, block - start, rank)
        start = start + blocks
    return dataset, rank, info_ref[0, sets]


def place_kernel(half, info_ref, own_ref, mirror_ref, out_ref, sems):
    def moves(block, act):
        dataset, rank, place = block_place(info_ref, block)
        is_own = dataset // half == place // half

        def one(ref):
            source = ref.at[lax.rem(dataset, half), rank]
            act(pltpu.make_async_copy(source, out_ref.at[block], sems.at[block]))

        pl.when(is_own)(lambda: one(own_ref))
        pl.when(jnp.logical_not(is_own))(lambda: one(mirror_ref))

    for block in range(out_ref.shape[0]):
        moves(block, lambda copy: copy.start())
    for block in range(out_ref.shape[0]):
        moves(block, lambda copy: copy.wait())


def place_rows(info, own, mirror, row_blocks):
    half, _, _, width = own.shape
    anywhere = pl.BlockSpec(memory_space=pl.ANY)
    return pl.pallas_call(
        functools.partial(place_kernel, half),
        grid_spec=pltpu.PrefetchScalarGridSpec(
            num_scalar_prefetch=1,
            grid=(1,),
            in_specs=[anywhere, anywhere],
            out_specs=anywhere,
            scratch_shapes=[pltpu.SemaphoreType.DMA((row_blocks,))],
        ),
        out_shape=jax.ShapeDtypeStruct((row_blocks, BLOCK, width), BF16),
        compiler_params=pltpu.CompilerParams(vmem_limit_bytes=VMEM),
        name="place_rows",
    )(info, own, mirror)


def halo(cut_rows):
    count = lax.axis_size("dom")
    forward = [(i, i + 1) for i in range(count - 1)]
    backward = [(target, source) for source, target in forward]
    low = lax.ppermute(cut_rows, "dom", forward)
    high = lax.ppermute(cut_rows, "dom", backward)
    return low, high


def exchange(blocks, half):
    groups = [list(range(half)), list(range(half, 2 * half))]
    return lax.all_to_all(
        blocks, "head", split_axis=0, concat_axis=0, axis_index_groups=groups, tiled=True
    )


def across(array, half):
    return lax.ppermute(array, "head", [(i, (i + half) % (2 * half)) for i in range(2 * half)])


def after(value, *others):
    return lax.optimization_barrier((value,) + others)[0]


def sum_steps(share):
    count = lax.axis_size("dom")
    rows, width = share.shape
    bits = count.bit_length() - 1
    place = lax.axis_index("dom")
    total = share.reshape((2,) * bits + (rows // count, width))
    for bit in range(bits):
        axis = bits - 1 - bit
        mine = (place >> bit) & 1
        keep = lax.dynamic_index_in_dim(total, mine, axis, keepdims=False)
        send = lax.dynamic_index_in_dim(total, 1 - mine, axis, keepdims=False)
        yield send
        got = lax.ppermute(send, "dom", [(i, i ^ (1 << bit)) for i in range(count)])
        total = keep.astype(F32) + got.astype(F32)
        if bit < bits - 1:
            total = total.astype(BF16)
    yield total


def sum_over_dom(share):
    return list(sum_steps(share))


def body(atoms, bonds, triplets, halo_ids, counts, enc_weight, gate_gain, head_weight):
    atom_rows = atoms[0]
    row_count, width = atom_rows.shape
    row_blocks = row_count // BLOCK
    half = lax.axis_size("head") // 2
    tall = width // LANES

    def gather(shard):
        return lax.all_gather(shard, "dom", axis=0, tiled=False)

    shard = head_weight[0]
    own_weights = [gather(shard[0]), gather(shard[1])]
    low, high = halo(pick_rows(atom_rows, halo_ids[0]))
    far_low = across(shard[0], half)
    codes = ((bonds[0] * tall) * 65536 + triplets[0] * tall).reshape(-1)
    ids = bonds[0].T
    place = lax.axis_index("head").astype(jnp.int32).reshape(1, 1)
    info = jnp.concatenate([counts, place], axis=1)
    gain = gate_gain[None, :]

    def encoded(info, mirror):
        return encode(info, codes, atom_rows, low, high, enc_weight, gain, ids, half, mirror)

    scale = 1.0 / math.sqrt(lax.axis_size("dom") * row_count)

    def share(acts, grads):
        product = lax.dot_general(
            acts.reshape(-1, width),
            grads.reshape(-1, width),
            (((0,), (0,)), ((), ())),
            preferred_element_type=F32,
        )
        return (product * scale).astype(BF16)

    own_blocks = encoded(info, False)
    own_rows = exchange(own_blocks, half)
    far_high = across(after(shard[1], far_low, own_blocks), half)
    mirror_low = gather(after(far_low, own_blocks))
    mirror_blocks = encoded(after(info, own_blocks), True)
    mirror_rows = exchange(mirror_blocks, half)
    mirror_high = gather(after(far_high, mirror_blocks))

    back, act, low_grad, high_grad = run_head(own_rows, own_weights, "head_own")
    own_back = exchange(back, half)
    own_high_sum = sum_over_dom(share(act, high_grad))
    own_low_sum = sum_over_dom(share(own_rows, low_grad))

    mirror_rows = after(mirror_rows, own_high_sum[-2], own_low_sum[-2])
    back, act, low_grad, high_grad = run_head(
        mirror_rows, [mirror_low, mirror_high], "head_mirror"
    )
    high_share = share(act, high_grad)
    low_share = share(mirror_rows, low_grad)
    high_part = across(sum_over_dom(high_share)[-1].astype(BF16), half)
    low_part = across(sum_over_dom(low_share)[-1].astype(BF16), half)
    mirror_back = exchange(after(back, high_share), half)
    row_part = place_rows(info, own_back, mirror_back, row_blocks)
    low_part, high_part, row_part = lax.optimization_barrier((low_part, high_part, row_part))
    head_part = jnp.stack(
        [own_low_sum[-1] + low_part.astype(F32), own_high_sum[-1] + high_part.astype(F32)]
    )
    return row_part.reshape(1, row_count, width), head_part[None]


def solution(mesh):
    return jax.shard_map(
        body,
        mesh=mesh,
        in_specs=(
            P("dom", "head", None),
            P("dom", None, "head"),
            P("dom", None, "head"),
            P("dom", "head"),
            P("dom", "head"),
            P(),
            P(),
            P("head", None, "dom", None),
        ),
        out_specs=(P("dom", "head", None), P("head", None, "dom", None)),
        check_vma=False,
    )
```

time: 257 us -> 319 us (1.24)
  Pallas kernels: 60.1 us -> 128 us
  waiting for transfers between devices: 96 us -> 65.3 us
  starting transfers between devices: 42.8 us -> 52.7 us
  local copies, waits for them, and re-layouts: 17.7 us -> 23.4 us
  other arithmetic: 7.91 us -> 12.8 us
    pallas_call x1, Pallas kernels: 6 us -> 65.4 us  [place_rows(): pl.pallas_call(functools.partial(place_kernel, half), grid_spec=pltpu.Pre...]
    all_to_all x4, waiting for transfers between devices: 17.5 us -> 0.01 us  [exchange(): lax.all_to_all(blocks, 'head', split_axis=0, concat_axis=0, axis_index_gr...]
    ppermute x3 -> x4, waiting for transfers between devices: 54.6 us -> 44.5 us  [across(): lax.ppermute(array, 'head', [(i, (i + half) % (2 * half)) for i in range(...]
    ppermute x8, starting transfers between devices: 8.71 us -> 17 us  [sum_steps(): got = lax.ppermute(send, 'dom', [(i, i ^ 1 << bit) for i in range(count)])]
    ppermute x8, waiting for transfers between devices: 23.3 us -> 17.8 us  [sum_steps(): got = lax.ppermute(send, 'dom', [(i, i ^ 1 << bit) for i in range(count)])]
    squeeze x8 -> x9, local copies, waits for them, and re-layouts: 4.84 us -> 9.25 us  [the longest x8 6.73 us: sum_steps(): send = lax.dynamic_index_in_dim(total, 1 - mine, axis, keepdims=False)]
    pallas_call x2, Pallas kernels: 34 us -> 38.1 us  [encode(): pl.pallas_call(functools.partial(encode_kernel, half, mirror, bond_count)...]
    all_to_all x4, starting transfers between devices: 18.2 us -> 21.8 us  [exchange(): lax.all_to_all(blocks, 'head', split_axis=0, concat_axis=0, axis_index_gr...]
  transfers between devices with their start and end apart: 19 -> 22, of which waited for: 7 -> 5; matrix products, arithmetic and copies ran while one was open for 11% -> 12% of each run, Pallas kernels for 21% -> 41%
where the time goes in v3:
time: 319 us; the launch traced here: 314 us
  Pallas kernels  128 us (40%)
  waiting for transfers between devices  65.3 us (20%)
  starting transfers between devices  52.7 us (17%)
  local copies, waits for them, and re-layouts  23.4 us (7%)
  matrix products  17.8 us (6%)
  between operations  14 us (4%)
  other arithmetic  12.8 us (4%)
    pallas_call x1, Pallas kernels, place_rows(): pl.pallas_call(functools.partial(place_kernel, half), grid_spec=pltpu.Pre...  65.4 us
    ppermute x4, waiting for transfers between devices, across(): lax.ppermute(array, 'head', [(i, (i + half) % (2 * half)) for i in range(...  44.5 us
    pallas_call x2, Pallas kernels, encode(): pl.pallas_call(functools.partial(encode_kernel, half, mirror, bond_count)...  38.1 us
    pallas_call x2, Pallas kernels, run_head(): pl.pallas_call(head_kernel, grid=(ranks, sources // tile), in_specs=[bloc...  22 us
    all_to_all x4, starting transfers between devices, exchange(): lax.all_to_all(blocks, 'head', split_axis=0, concat_axis=0, axis_index_gr...  21.8 us
    ppermute x8, waiting for transfers between devices, sum_steps(): got = lax.ppermute(send, 'dom', [(i, i ^ 1 << bit) for i in range(count)])  17.8 us
    dot_general x4, matrix products, share(): lax.dot_general(acts.reshape(-1, width), grads.reshape(-1, width), (((0,)...  17.8 us
    ppermute x8, starting transfers between devices, sum_steps(): got = lax.ppermute(send, 'dom', [(i, i ^ 1 << bit) for i in range(count)])  17 us
  transfers between devices with their start and end apart: 22, of which 5 were waited for; matrix products, arithmetic and copies ran while one was open for 12% of the time, Pallas kernels for 41%

profile of v3, /device:TPU:0, one launch (start us, length us, event | category | flops | bytes accessed | tf_op | source)
XLA Modules:
  0.0 314.4 jit_solution(12619622917051807292)
XLA Ops:
  7.2 2.5 slice_bitcast_fusion
  11.3 2.8 pick_rows.1
  22.9 21.3 %encode_own.1 = bf16[8,128,1024]{2,1,0:T(8,128)(2,1)} custom-call(s32[1,9]{1,0:T(1,128)} %pad_add_fusion.info_ref, s32[4096]{0:T(1024)} %bitcast.129, bf16[1024,1024]{1,0:T(8,128)(2,1)} %bitcast.114, bf16[128,1024]{1,0:T(8,128)(2,1)} %copy-done.11, bf16[128,1024]{1,0:T(8,128)(2,1)} %copy-done.12, bf16[1024,1024]{1,0:T(8,128)(2,1)} %weight_ref.3, ...), custom_call_target="tpu_custom_call" | custom-call | flops 1073741824 | bytes 31457280 | tf_op jit(solution)/shard_map/encode_own/pallas_call | solution.py:145
  44.3 3.8 %all-to-all-start.1 = ((bf16[4,2,128,1024]{3,2,1,0:T(8,128)(2,1)}), bf16[4,2,128,1024]{3,2,1,0:T(8,128)(2,1)S(1)}, u32[]{:S(2)}, u32[]{:S(2)}) async-start(bf16[4,2,128,1024]{3,2,1,0:T(8,128)(2,1)} %bitcast.117), calls=%async_computation.1 | async-start | bytes 4194304 | tf_op jit(solution)/shard_map/all_to_all | solution.py:289
  48.5 24.8 %collective-permute-done.4 = bf16[256,1024]{1,0:T(8,128)(2,1)S(1)} collective-permute-done((bf16[256,1024]{1,0:T(8,128)(2,1)}, bf16[256,1024]{1,0:T(8,128)(2,1)S(1)}, u32[]{:S(2)}, u32[]{:S(2)}) %collective-permute-start.4) | collective-permute-done | bytes 524320 | tf_op jit(solution)/shard_map/ppermute | solution.py:295
  74.2 16.8 %encode_mirror.1 = bf16[8,128,1024]{2,1,0:T(8,128)(2,1)} custom-call(s32[1,9]{1,0:T(1,128)} %pad_add_fusion.info_ref, s32[4096]{0:T(1024)} %bitcast.130, bf16[1024,1024]{1,0:T(8,128)(2,1)} %bitcast.115, bf16[128,1024]{1,0:T(8,128)(2,1)} %copy-done.11, bf16[128,1024]{1,0:T(8,128)(2,1)} %copy-done.12, bf16[1024,1024]{1,0:T(8,128)(2,1)} %weight_ref.3, ...), custom_call_target="tpu_custom_call" | custom-call | flops 1073741824 | bytes 31457280 | tf_op jit(solution)/shard_map/encode_mirror/pallas_call | solution.py:145
  92.2 5.0 %all-to-all-start = ((bf16[4,2,128,1024]{3,2,1,0:T(8,128)(2,1)}), bf16[4,2,128,1024]{3,2,1,0:T(8,128)(2,1)S(1)}, u32[]{:S(2)}, u32[]{:S(2)}) async-start(bf16[4,2,128,1024]{3,2,1,0:T(8,128)(2,1)} %bitcast.116), calls=%async_computation | async-start | bytes 4194304 | tf_op jit(solution)/shard_map/all_to_all | solution.py:289
  97.3 4.2 %collective-permute-start.5 = (bf16[256,1024]{1,0:T(8,128)(2,1)S(1)}, bf16[256,1024]{1,0:T(8,128)(2,1)S(1)}, u32[]{:S(2)}, u32[]{:S(2)}) collective-permute-start(bf16[256,1024]{1,0:T(8,128)(2,1)S(1)} %get-tuple-element.25), channel_id=1, source_target_pairs={{0,4},{1,5},{2,6},{3,7},{4,0},{5,1},{6,2},{7,3},{8,12},{9,13},{10,... | collective-permute-start | bytes 1572872 | tf_op jit(solution)/shard_map/ppermute | solution.py:295
  101.5 19.7 %collective-permute-done.5 = bf16[256,1024]{1,0:T(8,128)(2,1)S(1)} collective-permute-done((bf16[256,1024]{1,0:T(8,128)(2,1)S(1)}, bf16[256,1024]{1,0:T(8,128)(2,1)S(1)}, u32[]{:S(2)}, u32[]{:S(2)}) %collective-permute-start.5) | collective-permute-done | bytes 524320 | tf_op jit(solution)/shard_map/ppermute | solution.py:295
  122.1 11.1 %head_own.1 = (bf16[4,2,128,1024]{3,2,1,0:T(8,128)(2,1)}, bf16[4,2,128,1024]{3,2,1,0:T(8,128)(2,1)}, bf16[4,2,128,1024]{3,2,1,0:T(8,128)(2,1)}, bf16[4,2,128,1024]{3,2,1,0:T(8,128)(2,1)}) custom-call(bf16[4,2,128,1024]{3,2,1,0:T(8,128)(2,1)} %copy-done.9, bf16[4,256,1024]{2,1,0:T(8,128)(2,1)} %bitcast.135, bf16[4,256,1024]{2,1,0:T(8,128)(2,1)} %bitcast.136), custom_call_target="tpu_custom_call" | custom-call | flops 8589934592 | bytes 14680064 | tf_op jit(solution)/shard_map/head_own/pallas_call | solution.py:214
  133.2 4.0 %fusion.2 = bf16[1024,1024]{1,0:T(8,128)(2,1)S(1)} fusion(bf16[4,2,128,1024]{3,2,1,0:T(8,128)(2,1)S(1)} %copy-done.10, bf16[4,2,128,1024]{3,2,1,0:T(8,128)(2,1)} %get-tuple-element.22), kind=kOutput, calls=%fused_computation.5 | convolution fusion | flops 2149580800 | bytes 6291456 | tf_op jit(solution)/shard_map/dot_general | solution.py:351
  139.6 11.6 %collective-permute-start.3 = (bf16[2,256,1024]{2,1,0:T(8,128)(2,1)}, bf16[2,256,1024]{2,1,0:T(8,128)(2,1)}, u32[]{:S(2)}, u32[]{:S(2)}) collective-permute-start(bf16[2,256,1024]{2,1,0:T(8,128)(2,1)} %dynamic-slice_bitcast_fusion.2), channel_id=1, source_target_pairs={{0,8},{8,0},{16,24},{24,16},{1,9},{9,1},{17,25},{25,17},{2,10},{10... | collective-permute-start | bytes 3145736 | tf_op jit(solution)/shard_map/ppermute | solution.py:314
  152.5 8.3 %all-to-all-start.2 = ((bf16[4,2,128,1024]{3,2,1,0:T(8,128)(2,1)}), bf16[4,2,128,1024]{3,2,1,0:T(8,128)(2,1)S(1)}, u32[]{:S(2)}, u32[]{:S(2)}) async-start(bf16[4,2,128,1024]{3,2,1,0:T(8,128)(2,1)} %get-tuple-element.30), calls=%async_computation.2 | async-start | bytes 4194304 | tf_op jit(solution)/shard_map/all_to_all | solution.py:289
  160.8 4.6 %fusion.3 = bf16[1024,1024]{1,0:T(8,128)(2,1)S(1)} fusion(bf16[4,2,128,1024]{3,2,1,0:T(8,128)(2,1)} %get-tuple-element.20, bf16[4,2,128,1024]{3,2,1,0:T(8,128)(2,1)} %get-tuple-element.21), kind=kOutput, calls=%fused_computation.7 | convolution fusion | flops 2149580800 | bytes 6291456 | tf_op jit(solution)/shard_map/dot_general | solution.py:351
  174.2 10.9 %head_mirror.1 = (bf16[4,2,128,1024]{3,2,1,0:T(8,128)(2,1)}, bf16[4,2,128,1024]{3,2,1,0:T(8,128)(2,1)}, bf16[4,2,128,1024]{3,2,1,0:T(8,128)(2,1)}, bf16[4,2,128,1024]{3,2,1,0:T(8,128)(2,1)}) custom-call(bf16[4,2,128,1024]{3,2,1,0:T(8,128)(2,1)} %copy-done.8, bf16[4,256,1024]{2,1,0:T(8,128)(2,1)} %bitcast.134, bf16[4,256,1024]{2,1,0:T(8,128)(2,1)} %bitcast.137), custom_call_target="tpu_custom_call" | custom-call | flops 8589934592 | bytes 14680064 | tf_op jit(solution)/shard_map/head_mirror/pallas_call | solution.py:214
  185.2 4.6 %fusion = bf16[1024,1024]{1,0:T(8,128)(2,1)S(1)} fusion(bf16[4,2,128,1024]{3,2,1,0:T(8,128)(2,1)} %get-tuple-element.28, bf16[4,2,128,1024]{3,2,1,0:T(8,128)(2,1)} %get-tuple-element.29), kind=kOutput, calls=%fused_computation.1 | convolution fusion | flops 2149580800 | bytes 6291456 | tf_op jit(solution)/shard_map/dot_general | solution.py:351
  193.2 4.7 %all-to-all-start.3 = ((bf16[4,2,128,1024]{3,2,1,0:T(8,128)(2,1)}), bf16[4,2,128,1024]{3,2,1,0:T(8,128)(2,1)}, u32[]{:S(2)}, u32[]{:S(2)}) async-start(bf16[4,2,128,1024]{3,2,1,0:T(8,128)(2,1)} %get-tuple-element.32), calls=%async_computation.3 | async-start | bytes 4194304 | tf_op jit(solution)/shard_map/all_to_all | solution.py:289
  197.9 4.6 %fusion.1 = bf16[1024,1024]{1,0:T(8,128)(2,1)S(1)} fusion(bf16[4,2,128,1024]{3,2,1,0:T(8,128)(2,1)} %copy-done.8, bf16[4,2,128,1024]{3,2,1,0:T(8,128)(2,1)} %get-tuple-element.27), kind=kOutput, calls=%fused_computation.3 | convolution fusion | flops 2149580800 | bytes 6291456 | tf_op jit(solution)/shard_map/dot_general | solution.py:351
  206.6 2.9 collective-permute-start.10
  210.7 11.8 %collective-permute-done.10 = bf16[256,1024]{1,0:T(8,128)(2,1)} collective-permute-done((bf16[256,1024]{1,0:T(8,128)(2,1)}, bf16[256,1024]{1,0:T(8,128)(2,1)}, u32[]{:S(2)}, u32[]{:S(2)}) %collective-permute-start.10) | collective-permute-done | bytes 524320 | tf_op jit(solution)/shard_map/ppermute | solution.py:314
  224.5 2.6 collective-permute-start.11
  227.1 6.0 %collective-permute-done.7 = bf16[256,1024]{1,0:T(8,128)(2,1)} collective-permute-done((bf16[256,1024]{1,0:T(8,128)(2,1)}, bf16[256,1024]{1,0:T(8,128)(2,1)}, u32[]{:S(2)}, u32[]{:S(2)}) %collective-permute-start.7) | collective-permute-done | bytes 524320 | tf_op jit(solution)/shard_map/ppermute | solution.py:314
  234.3 2.9 collective-permute-start.8
  239.3 65.4 %place_rows.1 = bf16[8,128,1024]{2,1,0:T(8,128)(2,1)} custom-call(s32[1,9]{1,0:T(1,128)} %pad_add_fusion.info_ref, bf16[4,2,128,1024]{3,2,1,0:T(8,128)(2,1)} %copy-done, bf16[4,2,128,1024]{3,2,1,0:T(8,128)(2,1)} %all-to-all-done.3.mirror_ref), custom_call_target="tpu_custom_call" | custom-call | tf_op jit(solution)/shard_map/place_rows/pallas_call | solution.py:263
  (95 shorter events, 43.5 us)
Async XLA Ops:
  7.2 114.9 %all-gather.9.cloned.1.call-start = ((), (), s32[]{:S(2)}) async-start(), calls=%async_computation.4 | async-start | bytes 2621440 | tf_op jit(solution)/shard_map/all_gather | solution.py:333
  9.7 9.7 %copy-start.18 = (s32[1,8]{1,0:T(1,128)S(1)}, s32[1,8]{1,0:T(1,128)}, u32[]{:S(2)}) copy-start(s32[1,8]{1,0:T(1,128)} %param.12) | copy-start | bytes 100
  9.8 112.3 %all-gather.11.cloned.1.call-start = ((), (), s32[]{:S(2)}) async-start(), calls=%async_computation.5 | async-start | bytes 2621440 | tf_op jit(solution)/shard_map/all_gather | solution.py:333
  14.1 6.0 %collective-permute-start = (bf16[128,1024]{1,0:T(8,128)(2,1)}, bf16[128,1024]{1,0:T(8,128)(2,1)S(1)}, u32[]{:S(2)}, u32[]{:S(2)}) collective-permute-start(bf16[128,1024]{1,0:T(8,128)(2,1)} %pick_rows.1), channel_id=1, source_target_pairs={{0,8},{8,16},{16,24},{1,9},{9,17},{17,25},{2,10},{10,18},{18,26},{... | collective-permute-start | bytes 786440 | tf_op jit(solution)/shard_map/ppermute | solution.py:282
  16.5 5.8 %collective-permute-start.1 = (bf16[128,1024]{1,0:T(8,128)(2,1)}, bf16[128,1024]{1,0:T(8,128)(2,1)S(1)}, u32[]{:S(2)}, u32[]{:S(2)}) collective-permute-start(bf16[128,1024]{1,0:T(8,128)(2,1)} %pick_rows.1), channel_id=1, source_target_pairs={{8,0},{16,8},{24,16},{9,1},{17,9},{25,17},{10,2},{18,10},{26,18},{... | collective-permute-start | bytes 786440 | tf_op jit(solution)/shard_map/ppermute | solution.py:283
  44.3 46.6 %all-to-all-start.1 = ((bf16[4,2,128,1024]{3,2,1,0:T(8,128)(2,1)}), bf16[4,2,128,1024]{3,2,1,0:T(8,128)(2,1)S(1)}, u32[]{:S(2)}, u32[]{:S(2)}) async-start(bf16[4,2,128,1024]{3,2,1,0:T(8,128)(2,1)} %bitcast.117), calls=%async_computation.1 | async-start | bytes 4194304 | tf_op jit(solution)/shard_map/all_to_all | solution.py:289
  48.1 126.2 %all-gather.13.cloned.1.call-start = ((), (), s32[]{:S(2)}) async-start(), calls=%async_computation.6 | async-start | bytes 2621440 | tf_op jit(solution)/shard_map/all_gather | solution.py:333
  48.1 25.3 %collective-permute-start.4 = (bf16[256,1024]{1,0:T(8,128)(2,1)}, bf16[256,1024]{1,0:T(8,128)(2,1)S(1)}, u32[]{:S(2)}, u32[]{:S(2)}) collective-permute-start(bf16[256,1024]{1,0:T(8,128)(2,1)} %get-tuple-element.37), channel_id=1, source_target_pairs={{0,4},{1,5},{2,6},{3,7},{4,0},{5,1},{6,2},{7,3},{8,12},{9,13},{10,... | collective-permute-start | bytes 1572872 | tf_op jit(solution)/shard_map/ppermute | solution.py:295
  92.2 58.9 %all-to-all-start = ((bf16[4,2,128,1024]{3,2,1,0:T(8,128)(2,1)}), bf16[4,2,128,1024]{3,2,1,0:T(8,128)(2,1)S(1)}, u32[]{:S(2)}, u32[]{:S(2)}) async-start(bf16[4,2,128,1024]{3,2,1,0:T(8,128)(2,1)} %bitcast.116), calls=%async_computation | async-start | bytes 4194304 | tf_op jit(solution)/shard_map/all_to_all | solution.py:289
  97.3 76.9 %all-gather.15.cloned.1.call-start = ((), (), s32[]{:S(2)}) async-start(), calls=%async_computation.7 | async-start | bytes 2621440 | tf_op jit(solution)/shard_map/all_gather | solution.py:333
  97.3 23.9 %collective-permute-start.5 = (bf16[256,1024]{1,0:T(8,128)(2,1)S(1)}, bf16[256,1024]{1,0:T(8,128)(2,1)S(1)}, u32[]{:S(2)}, u32[]{:S(2)}) collective-permute-start(bf16[256,1024]{1,0:T(8,128)(2,1)S(1)} %get-tuple-element.25), channel_id=1, source_target_pairs={{0,4},{1,5},{2,6},{3,7},{4,0},{5,1},{6,2},{7,3},{8,12},{9,13},{10,... | collective-permute-start | bytes 1572872 | tf_op jit(solution)/shard_map/ppermute | solution.py:295
  122.1 11.1 %copy-start.10 = (bf16[4,2,128,1024]{3,2,1,0:T(8,128)(2,1)S(1)}, bf16[4,2,128,1024]{3,2,1,0:T(8,128)(2,1)}, u32[]{:S(2)}) copy-start(bf16[4,2,128,1024]{3,2,1,0:T(8,128)(2,1)} %copy-done.9) | copy-start | bytes 6291460
  139.6 28.2 %collective-permute-start.3 = (bf16[2,256,1024]{2,1,0:T(8,128)(2,1)}, bf16[2,256,1024]{2,1,0:T(8,128)(2,1)}, u32[]{:S(2)}, u32[]{:S(2)}) collective-permute-start(bf16[2,256,1024]{2,1,0:T(8,128)(2,1)} %dynamic-slice_bitcast_fusion.2), channel_id=1, source_target_pairs={{0,8},{8,0},{16,24},{24,16},{1,9},{9,1},{17,25},{25,17},{2,10},{10... | collective-permute-start | bytes 3145736 | tf_op jit(solution)/shard_map/ppermute | solution.py:314
  152.5 39.4 %all-to-all-start.2 = ((bf16[4,2,128,1024]{3,2,1,0:T(8,128)(2,1)}), bf16[4,2,128,1024]{3,2,1,0:T(8,128)(2,1)S(1)}, u32[]{:S(2)}, u32[]{:S(2)}) async-start(bf16[4,2,128,1024]{3,2,1,0:T(8,128)(2,1)} %get-tuple-element.30), calls=%async_computation.2 | async-start | bytes 4194304 | tf_op jit(solution)/shard_map/all_to_all | solution.py:289
  167.8 3.0 collective-permute-start.2
  191.4 11.3 %collective-permute-start.9 = (bf16[2,256,1024]{2,1,0:T(8,128)(2,1)}, bf16[2,256,1024]{2,1,0:T(8,128)(2,1)}, u32[]{:S(2)}, u32[]{:S(2)}) collective-permute-start(bf16[2,256,1024]{2,1,0:T(8,128)(2,1)} %dynamic-slice_bitcast_fusion), channel_id=1, source_target_pairs={{0,8},{8,0},{16,24},{24,16},{1,9},{9,1},{17,25},{25,17},{2,10},{10... | collective-permute-start | bytes 3145736 | tf_op jit(solution)/shard_map/ppermute | solution.py:314
  193.2 46.0 %all-to-all-start.3 = ((bf16[4,2,128,1024]{3,2,1,0:T(8,128)(2,1)}), bf16[4,2,128,1024]{3,2,1,0:T(8,128)(2,1)}, u32[]{:S(2)}, u32[]{:S(2)}) async-start(bf16[4,2,128,1024]{3,2,1,0:T(8,128)(2,1)} %get-tuple-element.32), calls=%async_computation.3 | async-start | bytes 4194304 | tf_op jit(solution)/shard_map/all_to_all | solution.py:289
  202.6 6.8 %collective-permute-start.6 = (bf16[2,256,1024]{2,1,0:T(8,128)(2,1)S(1)}, bf16[2,256,1024]{2,1,0:T(8,128)(2,1)S(1)}, u32[]{:S(2)}, u32[]{:S(2)}) collective-permute-start(bf16[2,256,1024]{2,1,0:T(8,128)(2,1)S(1)} %dynamic-slice_bitcast_fusion.1), channel_id=1, source_target_pairs={{0,8},{8,0},{16,24},{24,16},{1,9},{9,1},{17,25},{25,17},{2,10},{10... | collective-permute-start | bytes 3145736 | tf_op jit(solution)/shard_map/ppermute | solution.py:314
  206.6 15.9 %collective-permute-start.10 = (bf16[256,1024]{1,0:T(8,128)(2,1)}, bf16[256,1024]{1,0:T(8,128)(2,1)}, u32[]{:S(2)}, u32[]{:S(2)}) collective-permute-start(bf16[256,1024]{1,0:T(8,128)(2,1)} %dynamic-slice_bitcast_fusion.4), channel_id=1, source_target_pairs={{0,16},{8,24},{16,0},{24,8},{1,17},{9,25},{17,1},{25,9},{2,18},{10... | collective-permute-start | bytes 1572872 | tf_op jit(solution)/shard_map/ppermute | solution.py:314
  210.7 22.4 %collective-permute-start.7 = (bf16[256,1024]{1,0:T(8,128)(2,1)}, bf16[256,1024]{1,0:T(8,128)(2,1)}, u32[]{:S(2)}, u32[]{:S(2)}) collective-permute-start(bf16[256,1024]{1,0:T(8,128)(2,1)} %dynamic-slice_bitcast_fusion.5), channel_id=1, source_target_pairs={{0,16},{8,24},{16,0},{24,8},{1,17},{9,25},{17,1},{25,9},{2,18},{10... | collective-permute-start | bytes 1572872 | tf_op jit(solution)/shard_map/ppermute | solution.py:314
  224.5 80.2 %collective-permute-start.11 = (bf16[256,1024]{1,0:T(8,128)(2,1)}, bf16[256,1024]{1,0:T(8,128)(2,1)S(1)}, u32[]{:S(2)}, u32[]{:S(2)}) collective-permute-start(bf16[256,1024]{1,0:T(8,128)(2,1)} %fusion.12), channel_id=1, source_target_pairs={{0,4},{1,5},{2,6},{3,7},{4,0},{5,1},{6,2},{7,3},{8,12},{9,13},{10,... | collective-permute-start | bytes 1572872 | tf_op jit(solution)/shard_map/ppermute | solution.py:295
  234.3 70.4 %collective-permute-start.8 = (bf16[256,1024]{1,0:T(8,128)(2,1)S(1)}, bf16[256,1024]{1,0:T(8,128)(2,1)S(1)}, u32[]{:S(2)}, u32[]{:S(2)}) collective-permute-start(bf16[256,1024]{1,0:T(8,128)(2,1)S(1)} %fusion.13), channel_id=1, source_target_pairs={{0,4},{1,5},{2,6},{3,7},{4,0},{5,1},{6,2},{7,3},{8,12},{9,13},{10,... | collective-permute-start | bytes 1572872 | tf_op jit(solution)/shard_map/ppermute | solution.py:295
  237.2 67.5 %collective-permute-start.12 = (bf16[256,1024]{1,0:T(8,128)(2,1)}, bf16[256,1024]{1,0:T(8,128)(2,1)}, u32[]{:S(2)}, u32[]{:S(2)}) collective-permute-start(bf16[256,1024]{1,0:T(8,128)(2,1)} %dynamic-slice_bitcast_fusion.6), channel_id=1, source_target_pairs={{0,16},{8,24},{16,0},{24,8},{1,17},{9,25},{17,1},{25,9},{2,18},{10... | collective-permute-start | bytes 1572872 | tf_op jit(solution)/shard_map/ppermute | solution.py:314
  239.0 67.1 %collective-permute-start.13 = (bf16[256,1024]{1,0:T(8,128)(2,1)}, bf16[256,1024]{1,0:T(8,128)(2,1)S(1)}, u32[]{:S(2)}, u32[]{:S(2)}) collective-permute-start(bf16[256,1024]{1,0:T(8,128)(2,1)} %dynamic-slice_bitcast_fusion.7), channel_id=1, source_target_pairs={{0,16},{8,24},{16,0},{24,8},{1,17},{9,25},{17,1},{25,9},{2,18},{10... | collective-permute-start | bytes 1572872 | tf_op jit(solution)/shard_map/ppermute | solution.py:314
  (17 other events, 40.3 us)
Sparse Core Ops, SparseCore 0:
  9.9 28.0 all-gather.8
  39.6 22.5 all-gather.10
  74.3 32.8 all-gather.12
  122.2 37.4 all-gather.14

commit v4 on v3

v4 whole, which is shorter than its diff:
```python
import functools
import math

import jax
import jax.numpy as jnp
from jax import lax
from jax.experimental import pallas as pl
from jax.experimental.pallas import tpu as pltpu
from jax.sharding import PartitionSpec as P

BLOCK = 128
LANES = 128
MB = 1 << 20
VMEM = 58 * MB
F32 = jnp.float32
BF16 = jnp.bfloat16


def sigmoid(x):
    return 1.0 / (1.0 + jnp.exp(-x))


def resident(shape):
    return pl.BlockSpec(shape, lambda *_: (0,) * len(shape))


def pick_kernel(ids_ref, rows_ref, out_ref):
    count, total = out_ref.shape[0], rows_ref.shape[0]
    places = lax.broadcasted_iota(jnp.int32, (count, total), 1)
    ones = jnp.where(places == ids_ref[...], 1.0, 0.0).astype(BF16)
    out_ref[...] = jnp.dot(ones, rows_ref[...], preferred_element_type=F32).astype(BF16)


def pick_rows(rows, ids):
    return pl.pallas_call(
        pick_kernel,
        out_shape=jax.ShapeDtypeStruct((ids.shape[0], rows.shape[1]), rows.dtype),
        compiler_params=pltpu.CompilerParams(vmem_limit_bytes=VMEM),
        name="pick_rows",
    )(ids[:, None], rows)


def block_source(info_ref, dataset, rank):
    start = jnp.int32(0)
    blocks = jnp.int32(0)
    for candidate in range(info_ref.shape[1] - 1):
        here = info_ref[0, candidate] // BLOCK
        start = start + jnp.where(candidate < dataset, here, 0)
        blocks = jnp.where(candidate == dataset, here, blocks)
    live = rank < blocks
    return jnp.where(live, start + rank, 0), live


def fold(arrays):
    rows = lax.broadcasted_iota(jnp.int32, arrays[0].shape, 0)
    for shift in (1, 2, 4):
        first = (rows & shift) == 0
        arrays = [
            jnp.where(first, a, b) + pltpu.roll(jnp.where(first, b, a), 8 - shift, 0)
            for a, b in zip(arrays[::2], arrays[1::2])
        ]
    return arrays[0]


def encode_kernel(
    half, info_ref, codes_ref, atoms_ref, low_ref, high_ref, weight_ref, gain_ref, ids_ref,
    own_ref, mirror_ref, plain, gained, partial, gate_rows, staged, sems,
):
    rows, width = atoms_ref.shape
    depth = low_ref.shape[0]
    tall = width // LANES
    bond_count = ids_ref.shape[1]
    sets = 2 * half
    home = info_ref[0, sets] // half * half

    def leave(slot, act):
        def one(ref, at):
            act(pltpu.make_async_copy(staged.at[slot], ref.at[at], sems.at[slot]))

        pl.when(slot < sets)(lambda: one(own_ref, slot))
        pl.when(slot >= sets)(lambda: one(mirror_ref, slot - sets))

    def spread(ref, at, base):
        for k in range(tall):
            lanes = slice(k * LANES, (k + 1) * LANES)
            value = ref[pl.ds(at, BLOCK), lanes].astype(F32)
            place = pl.ds(base * tall + k, BLOCK, stride=tall)
            plain[place, :] = value
            gained[place, :] = value * gain_ref[:, lanes]

    for at in range(0, rows, BLOCK):
        spread(atoms_ref, at, at)
    for at in range(0, depth, BLOCK):
        spread(low_ref, at, rows + at)
        spread(high_ref, at, rows + depth + at)

    def row_of(ref, place):
        return ref[pl.ds(pl.multiple_of(place, tall), tall), :]

    def product(code):
        value = row_of(plain, code >> 16) * row_of(gained, code & 0xFFFF)
        return sum(value[k : k + 8] for k in range(0, tall, 8))

    def encode_block(source, slot):
        base = pl.multiple_of(source * BLOCK, BLOCK)

        def score(group, carry):
            for bond in range(bond_count):
                at = bond * rows + base + group * 8
                place = pl.multiple_of(bond * BLOCK + group * 8, 8)
                partial[pl.ds(place, 8), :] = fold([product(codes_ref[at + j]) for j in range(8)])
            return carry

        lax.fori_loop(0, BLOCK // 8, score, 0)
        logits = jnp.sum(partial[...], axis=1, keepdims=True) * (1.0 / math.sqrt(width))
        gates = sigmoid(logits)
        ids = ids_ref[pl.ds(base, BLOCK), :]
        for at in range(0, gate_rows.shape[1], LANES):
            places = lax.broadcasted_iota(jnp.int32, (BLOCK, LANES), 1) + at
            acc = jnp.zeros((BLOCK, LANES), F32)
            for bond in range(bond_count):
                gate = gates[bond * BLOCK : (bond + 1) * BLOCK]
                acc = acc + jnp.where(places == ids[:, bond : bond + 1], gate, 0.0)
            gate_rows[:, at : at + LANES] = acc.astype(BF16)
        message = jnp.dot(gate_rows[:, :rows], atoms_ref[...], preferred_element_type=F32)
        for ref, at in ((low_ref, rows), (high_ref, rows + depth)):
            message += jnp.dot(
                gate_rows[:, at : at + depth], ref[...], preferred_element_type=F32
            )
        update = jnp.dot(message.astype(BF16), weight_ref[...], preferred_element_type=F32)
        own = atoms_ref[pl.ds(base, BLOCK), :].astype(F32)
        staged[slot] = (own + update * sigmoid(update)).astype(BF16)

    def one(slot, carry):
        dataset = lax.rem(home + slot // 2, sets)
        source, live = block_source(info_ref, dataset, lax.rem(slot, 2))
        pl.when(live)(lambda: encode_block(source, slot))

        @pl.when(jnp.logical_not(live))
        def _():
            staged[slot] = jnp.zeros(staged.shape[1:], BF16)

        leave(slot, lambda copy: copy.start())
        return carry

    def settle(slot, carry):
        leave(slot, lambda copy: copy.wait())
        return carry

    lax.fori_loop(0, 2 * sets, one, 0)
    lax.fori_loop(0, 2 * sets, settle, 0)


def encode(info, codes, atoms, low, high, weight, gain, ids, half):
    rows, width = atoms.shape
    depth = low.shape[0]
    tall = width // LANES
    extended = rows + 2 * depth
    bond_count = ids.shape[1]
    slots = 4 * half
    blocks = pl.pallas_call(
        functools.partial(encode_kernel, half),
        grid_spec=pltpu.PrefetchScalarGridSpec(
            num_scalar_prefetch=2,
            grid=(1,),
            in_specs=[
                resident((rows, width)),
                resident((depth, width)),
                resident((depth, width)),
                resident((width, width)),
                resident((1, width)),
                resident((rows, bond_count)),
            ],
            out_specs=[pl.BlockSpec(memory_space=pltpu.HBM)] * 2,
            scratch_shapes=[
                pltpu.VMEM((extended * tall, LANES), F32),
                pltpu.VMEM((extended * tall, LANES), F32),
                pltpu.VMEM((BLOCK * bond_count, LANES), F32),
                pltpu.VMEM((BLOCK, extended), BF16),
                pltpu.VMEM((slots, BLOCK, width), BF16),
                pltpu.SemaphoreType.DMA((slots,)),
            ],
        ),
        out_shape=[pltpu.HBM((2 * half, BLOCK, width), BF16)] * 2,
        compiler_params=pltpu.CompilerParams(vmem_limit_bytes=40 * MB),
        cost_estimate=pl.CostEstimate(
            flops=40 * rows * width * width,
            bytes_accessed=30 * MB,
            transcendentals=rows * width,
        ),
        name="encode_rows",
    )(info, codes, atoms, low, high, weight, gain, ids)
    return [rows.reshape(half, 2, BLOCK, width) for rows in blocks]


def head_kernel(sizes, scale, table_ref, rows_ref, *refs):
    pieces = refs[: len(sizes)]
    back_ref, send_ref, keep_ref, weights, totals, sems = refs[len(sizes) :]
    width = rows_ref.shape[-1]
    shape = rows_ref.shape
    count = weights.shape[1]
    first = jnp.logical_and(pl.program_id(0) == 0, pl.program_id(1) == 0)
    last = jnp.logical_and(
        pl.program_id(0) == pl.num_programs(0) - 1, pl.program_id(1) == pl.num_programs(1) - 1
    )

    def loads(act):
        shard = 0
        for ref, size in zip(pieces, sizes):
            for i in range(size):
                for layer in range(2):
                    place = weights.at[layer, table_ref[shard]]
                    act(pltpu.make_async_copy(ref.at[i, layer], place, sems.at[layer, shard]))
                shard += 1

    @pl.when(first)
    def _():
        loads(lambda copy: copy.start())
        loads(lambda copy: copy.wait())

    x = rows_ref[...].reshape(-1, width)
    some = jnp.logical_or(first, jnp.max(jnp.abs(x.astype(F32))) > 0)

    @pl.when(some)
    def _():
        low = weights[0].reshape(width, width)
        high = weights[1].reshape(width, width)
        transposed = (((1,), (1,)), ((), ()))
        over_rows = (((0,), (0,)), ((), ()))

        def add(layer, acts, grads):
            value = lax.dot_general(acts, grads, over_rows, preferred_element_type=F32)
            value = value.reshape(totals.shape[1:])

            @pl.when(first)
            def _():
                totals[layer] = value

            @pl.when(jnp.logical_not(first))
            def _():
                totals[layer] += value

        z = jnp.dot(x, low, preferred_element_type=F32)
        s = sigmoid(z)
        act = (z * s).astype(BF16)
        slope = s * (1.0 + z * (1.0 - s))
        err = jnp.dot(act, high, preferred_element_type=F32) - x.astype(F32)
        grad = err.astype(BF16)
        add(1, act, grad)
        up = lax.dot_general(grad, high, transposed, preferred_element_type=F32)
        grad = (up * slope).astype(BF16)
        add(0, x, grad)
        up = lax.dot_general(grad, low, transposed, preferred_element_type=F32)
        back_ref[...] = (up - err).astype(BF16).reshape(shape)

    @pl.when(jnp.logical_not(some))
    def _():
        back_ref[...] = jnp.zeros_like(back_ref)

    @pl.when(last)
    def _():
        bit = table_ref[count]
        for layer in range(2):
            for j in range(count // 2):
                keep_ref[layer, j] = (totals[layer, 2 * j + bit] * scale).astype(BF16)
                send_ref[layer, j] = (totals[layer, 2 * j + 1 - bit] * scale).astype(BF16)


def run_head(rows, pieces, places, scale, name):
    sources, ranks, _, width = rows.shape
    count = lax.axis_size("dom")
    depth = width // count
    tile = 4 if sources % 4 == 0 else 1
    block = pl.BlockSpec((tile, 1, BLOCK, width), lambda r, t, *_: (t, r, 0, 0))
    total = sources * ranks * BLOCK
    sizes = [piece.shape[0] for piece in pieces]
    part = (2, count // 2, depth, width)
    bit = lax.axis_index("dom").astype(jnp.int32) & 1
    return pl.pallas_call(
        functools.partial(head_kernel, sizes, scale),
        grid_spec=pltpu.PrefetchScalarGridSpec(
            num_scalar_prefetch=1,
            grid=(ranks, sources // tile),
            in_specs=[block] + [pl.BlockSpec(memory_space=pltpu.HBM)] * len(pieces),
            out_specs=[block, resident(part), resident(part)],
            scratch_shapes=[
                pltpu.VMEM((2, count, depth, width), BF16),
                pltpu.VMEM((2, count, depth, width), F32),
                pltpu.SemaphoreType.DMA((2, count)),
            ],
        ),
        out_shape=[
            jax.ShapeDtypeStruct(rows.shape, BF16),
            jax.ShapeDtypeStruct(part, BF16),
            jax.ShapeDtypeStruct(part, BF16),
        ],
        compiler_params=pltpu.CompilerParams(vmem_limit_bytes=VMEM),
        cost_estimate=pl.CostEstimate(
            flops=24 * total * width * width,
            bytes_accessed=5 * total * width * 2 + width * width * 4,
            transcendentals=total * width,
        ),
        name=name,
    )(jnp.stack(places + [bit]).astype(jnp.int32), rows, *pieces)


def block_place(info_ref, block):
    sets = info_ref.shape[1] - 1
    start, dataset, rank = jnp.int32(0), jnp.int32(0), jnp.int32(0)
    for candidate in range(sets):
        blocks = info_ref[0, candidate] // BLOCK
        inside = jnp.logical_and(block >= start, block < start + blocks)
        dataset = jnp.where(inside, candidate, dataset)
        rank = jnp.where(inside, block - start, rank)
        start = start + blocks
    return dataset, rank, info_ref[0, sets]


def place_kernel(half, info_ref, own_ref, mirror_ref, out_ref):
    dataset, _, place = block_place(info_ref, pl.program_id(0))
    is_own = dataset // half == place // half
    out_ref[0] = jnp.where(is_own, own_ref[0, 0], mirror_ref[0, 0])


def place_rows(info, own, mirror, row_blocks):
    half, _, _, width = own.shape
    shape = (1, 1, BLOCK, width)

    def index(of_own, block, info_ref):
        dataset, rank, place = block_place(info_ref, block)
        wanted = (dataset // half == place // half) == of_own
        return jnp.where(wanted, lax.rem(dataset, half), 0), jnp.where(wanted, rank, 0), 0, 0

    return pl.pallas_call(
        functools.partial(place_kernel, half),
        grid_spec=pltpu.PrefetchScalarGridSpec(
            num_scalar_prefetch=1,
            grid=(row_blocks,),
            in_specs=[
                pl.BlockSpec(shape, functools.partial(index, True)),
                pl.BlockSpec(shape, functools.partial(index, False)),
            ],
            out_specs=pl.BlockSpec((1, BLOCK, width), lambda block, *_: (block, 0, 0)),
        ),
        out_shape=jax.ShapeDtypeStruct((row_blocks, BLOCK, width), BF16),
        compiler_params=pltpu.CompilerParams(vmem_limit_bytes=16 * MB),
        name="place_rows",
    )(info, own, mirror)


def halo(cut_rows):
    count = lax.axis_size("dom")
    forward = [(i, i + 1) for i in range(count - 1)]
    backward = [(target, source) for source, target in forward]
    low = lax.ppermute(cut_rows, "dom", forward)
    high = lax.ppermute(cut_rows, "dom", backward)
    return low, high


def exchange(blocks, half):
    groups = [list(range(half)), list(range(half, 2 * half))]
    return lax.all_to_all(
        blocks, "head", split_axis=0, concat_axis=0, axis_index_groups=groups, tiled=True
    )


def across(array, half):
    return lax.ppermute(array, "head", [(i, (i + half) % (2 * half)) for i in range(2 * half)])


def after(value, *others):
    return lax.optimization_barrier((value,) + others)[0]


def swap(array, bit):
    count = lax.axis_size("dom")
    return lax.ppermute(array, "dom", [(i, i ^ (1 << bit)) for i in range(count)])


def spread_over_dom(shard):
    place = lax.axis_index("dom").astype(jnp.int32)
    pieces, places = [shard], [place]
    for bit in reversed(range(lax.axis_size("dom").bit_length() - 1)):
        pieces += [swap(piece, bit) for piece in pieces]
        places += [there ^ (1 << bit) for there in places]
    return pieces, places


def merge_kernel(bit_ref, keep_ref, got_ref, send_ref, kept_ref):
    bit = bit_ref[0]
    for layer in range(keep_ref.shape[0]):
        for j in range(kept_ref.shape[1]):
            for out_ref, at in ((kept_ref, 2 * j + bit), (send_ref, 2 * j + 1 - bit)):
                total = keep_ref[layer, at].astype(F32) + got_ref[layer, at].astype(F32)
                out_ref[layer, j] = total.astype(BF16)


def merge(keep, got, bit, first, layers):
    _, count, depth, width = keep.shape
    mine = (lax.axis_index("dom").astype(jnp.int32) >> bit) & 1
    part = pl.BlockSpec((layers, count, depth, width), lambda t, *_: (first // layers, 0, 0, 0))
    shape = (layers, count // 2, depth, width)
    return pl.pallas_call(
        merge_kernel,
        grid_spec=pltpu.PrefetchScalarGridSpec(
            num_scalar_prefetch=1,
            grid=(1,),
            in_specs=[part, part],
            out_specs=[resident(shape)] * 2,
        ),
        out_shape=[jax.ShapeDtypeStruct(shape, BF16)] * 2,
        compiler_params=pltpu.CompilerParams(vmem_limit_bytes=20 * MB),
        name="merge_shares",
    )(mine.reshape(1), keep, got)


def sum_over_dom(send, keep, got, first, layers):
    bits = lax.axis_size("dom").bit_length() - 1
    for bit in range(1, bits):
        send, keep = merge(keep, got, bit, first, layers)
        got = swap(send, bit)
        first = 0
    return keep[:, 0], got[:, 0], send


def total_kernel(*refs):
    *terms, out_ref = refs
    for layer in range(out_ref.shape[0]):
        acc = None
        for ref, at in terms_of(terms, layer):
            value = ref[at].astype(F32)
            acc = value if acc is None else acc + value
        out_ref[layer] = acc


def terms_of(terms, layer):
    keep, got, low, high = terms
    return [(keep, layer), (got, layer), ((low, high)[layer], 0)]


def total(keep, got, low, high):
    return pl.pallas_call(
        total_kernel,
        out_shape=jax.ShapeDtypeStruct(keep.shape, F32),
        compiler_params=pltpu.CompilerParams(vmem_limit_bytes=20 * MB),
        name="total_shares",
    )(keep, got, low, high)


def body(atoms, bonds, triplets, halo_ids, counts, enc_weight, gate_gain, head_weight):
    atom_rows = atoms[0]
    row_count, width = atom_rows.shape
    row_blocks = row_count // BLOCK
    half = lax.axis_size("head") // 2
    tall = width // LANES

    shard = head_weight[0]
    count = lax.axis_size("dom")
    own_weights = lax.all_gather(shard, "dom", axis=0, tiled=False)
    far = across(head_weight, half)
    low, high = halo(pick_rows(atom_rows, halo_ids[0]))
    codes = ((bonds[0] * tall) * 65536 + triplets[0] * tall).reshape(-1)
    place = lax.axis_index("head").astype(jnp.int32).reshape(1, 1)
    info = jnp.concatenate([counts, place], axis=1)
    own_blocks, mirror_blocks = encode(
        info, codes, atom_rows, low, high, enc_weight, gate_gain[None, :], bonds[0].T, half
    )
    own_rows = exchange(own_blocks, half)
    mirror_rows = exchange(mirror_blocks, half)
    far_pieces, far_places = spread_over_dom(far)

    scale = 1.0 / math.sqrt(count * row_count)
    orders = [jnp.int32(i) for i in range(count)]
    back, send, keep = run_head(own_rows, [own_weights], orders, scale, "head_own")
    own_back = exchange(back, half)
    own_keep, own_got, own_sent = sum_over_dom(send, keep, swap(send, 0), 0, 2)

    mirror_rows = after(mirror_rows, own_sent)
    back, send, keep = run_head(mirror_rows, far_pieces, far_places, scale, "head_mirror")
    got = swap(send, 0)
    high_keep, high_got, high_sent = sum_over_dom(send, keep, got, 1, 1)
    low_keep, low_got, low_sent = sum_over_dom(send, keep, got, 0, 1)
    mirror_back = exchange(after(back, high_sent, low_sent), half)
    high_part = across((high_keep.astype(F32) + high_got.astype(F32)).astype(BF16), half)
    low_part = across((low_keep.astype(F32) + low_got.astype(F32)).astype(BF16), half)
    row_part = place_rows(info, own_back, mirror_back, row_blocks)
    head_part = total(own_keep, own_got, low_part, after(high_part, row_part))
    return row_part.reshape(1, row_count, width), head_part[None]


def solution(mesh):
    return jax.shard_map(
        body,
        mesh=mesh,
        in_specs=(
            P("dom", "head", None),
            P("dom", None, "head"),
            P("dom", None, "head"),
            P("dom", "head"),
            P("dom", "head"),
            P(),
            P(),
            P("head", None, "dom", None),
        ),
        out_specs=(P("dom", "head", None), P("head", None, "dom", None)),
        check_vma=False,
    )
```

time: 319 us -> 274 us (0.86); the launches traced: 314 us -> 273 us
  waiting for transfers between devices: 65.3 us -> 129 us
  Pallas kernels: 128 us -> 78.4 us
  starting transfers between devices: 52.7 us -> 33.7 us
  matrix products: 17.8 us -> 0 us
  local copies, waits for them, and re-layouts: 23.4 us -> 13.4 us
  other arithmetic: 12.8 us -> 4.16 us
    pallas_call x1, Pallas kernels: 65.4 us -> 5.53 us  [place_rows(): pl.pallas_call(functools.partial(place_kernel, half), grid_spec=pltpu.Pre...]
    all_to_all x4, waiting for transfers between devices: 0.01 us -> 44.5 us  [exchange(): lax.all_to_all(blocks, 'head', split_axis=0, concat_axis=0, axis_index_gr...]
    ppermute x8, waiting for transfers between devices: 17.8 us -> 49.4 us  [swap(): return lax.ppermute(array, 'dom', [(i, i ^ 1 << bit) for i in range(count)])]
    dot_general x4 -> x0, matrix products: 17.8 us -> none  [share(): lax.dot_general(acts.reshape(-1, width), grads.reshape(-1, width), (((0,)...]
    ppermute x4 -> x3, waiting for transfers between devices: 44.5 us -> 30.8 us  [across(): lax.ppermute(array, 'head', [(i, (i + half) % (2 * half)) for i in range(...]
    pallas_call x4 -> x7, Pallas kernels: 60.1 us -> 70.1 us  [the longest x2 39.8 us: run_head(): pl.pallas_call(functools.partial(head_kernel, sizes, scale), grid_spec=pl...]
    squeeze x9 -> x0, local copies, waits for them, and re-layouts: 9.25 us -> none  [the longest x8 6.73 us: sum_steps(): send = lax.dynamic_index_in_dim(total, 1 - mine, axis, keepdims=False)]
    ppermute x4 -> x3, starting transfers between devices: 10.2 us -> 2.59 us  [across(): lax.ppermute(array, 'head', [(i, (i + half) % (2 * half)) for i in range(...]
  transfers between devices with their start and end apart: 22 -> 18, of which waited for: 5 -> 8; matrix products, arithmetic and copies ran while one was open for 12% -> 2% of each run, Pallas kernels for 41% -> 27%
where the time goes in v4:
time: 274 us; the launch traced here: 273 us
  waiting for transfers between devices  129 us (47%)
  Pallas kernels  78.4 us (29%)
  starting transfers between devices  33.7 us (12%)
  between operations  14.3 us (5%)
  local copies, waits for them, and re-layouts  13.4 us (5%)
  other arithmetic  4.16 us (2%)
    ppermute x8, waiting for transfers between devices, swap(): return lax.ppermute(array, 'dom', [(i, i ^ 1 << bit) for i in range(count)])  49.4 us
    all_to_all x4, waiting for transfers between devices, exchange(): lax.all_to_all(blocks, 'head', split_axis=0, concat_axis=0, axis_index_gr...  44.5 us
    pallas_call x2, Pallas kernels, run_head(): pl.pallas_call(functools.partial(head_kernel, sizes, scale), grid_spec=pl...  39.8 us
    ppermute x3, waiting for transfers between devices, across(): lax.ppermute(array, 'head', [(i, (i + half) % (2 * half)) for i in range(...  30.8 us
    pallas_call x1, Pallas kernels, encode(): pl.pallas_call(functools.partial(encode_kernel, half), grid_spec=pltpu.Pr...  26.1 us
    all_to_all x4, starting transfers between devices, exchange(): lax.all_to_all(blocks, 'head', split_axis=0, concat_axis=0, axis_index_gr...  16.7 us
    ppermute x8, starting transfers between devices, swap(): return lax.ppermute(array, 'dom', [(i, i ^ 1 << bit) for i in range(count)])  10.7 us
    unnamed x30, local copies, waits for them, and re-layouts  10.5 us
  transfers between devices with their start and end apart: 18, of which 8 were waited for; matrix products, arithmetic and copies ran while one was open for 2% of the time, Pallas kernels for 27%

profile of v4, /device:TPU:0, one launch (start us, length us, event | category | flops | bytes accessed | tf_op | source)
XLA Modules:
  0.0 272.7 jit_solution(18364313070408126428)
XLA Ops:
  8.8 2.8 %pick_rows.1 = bf16[128,1024]{1,0:T(8,128)(2,1)} custom-call(s32[128,1]{1,0:T(8,128)} %copy.13.ids_ref, bf16[1024,1024]{1,0:T(8,128)(2,1)} %bitcast.29), custom_call_target="tpu_custom_call" | custom-call | tf_op jit(solution)/shard_map/pick_rows/pallas_call | solution.py:35
  11.6 2.4 collective-permute-start
  15.7 4.1 %collective-permute-done.1.high_ref = bf16[128,1024]{1,0:T(8,128)(2,1)S(1)} collective-permute-done((bf16[128,1024]{1,0:T(8,128)(2,1)}, bf16[128,1024]{1,0:T(8,128)(2,1)S(1)}, u32[]{:S(2)}, u32[]{:S(2)}) %collective-permute-start.1) | collective-permute-done | bytes 262176 | tf_op jit(solution)/shard_map/ppermute | solution.py:356
  21.3 26.1 %encode_rows.1 = (bf16[8,128,1024]{2,1,0:T(8,128)(2,1)}, bf16[8,128,1024]{2,1,0:T(8,128)(2,1)}) custom-call(s32[1,9]{1,0:T(1,128)S(1)} %pad_add_fusion.info_ref, s32[4096]{0:T(1024)S(1)} %bitcast.33, bf16[1024,1024]{1,0:T(8,128)(2,1)S(1)} %bitcast.30, bf16[128,1024]{1,0:T(8,128)(2,1)S(1)} %collective-permute-done.low_ref, ...), custom_call_target="tpu_custom_call" | custom-call | flops 42949672960 | bytes 31457280 | tf_op jit(solution)/shard_map/encode_rows/pallas_call | solution.py:161
  47.5 3.8 %all-to-all-start = ((bf16[4,2,128,1024]{3,2,1,0:T(8,128)(2,1)}), bf16[4,2,128,1024]{3,2,1,0:T(8,128)(2,1)S(1)}, u32[]{:S(2)}, u32[]{:S(2)}) async-start(bf16[4,2,128,1024]{3,2,1,0:T(8,128)(2,1)} %bitcast.37), calls=%async_computation | async-start | bytes 4194304 | tf_op jit(solution)/shard_map/all_to_all | solution.py:362
  51.2 2.6 collective-permute-start.3
  54.4 44.5 %all-to-all-done.rows_ref = bf16[4,2,128,1024]{3,2,1,0:T(8,128)(2,1)S(1)} async-done(((bf16[4,2,128,1024]{3,2,1,0:T(8,128)(2,1)}), bf16[4,2,128,1024]{3,2,1,0:T(8,128)(2,1)S(1)}, u32[]{:S(2)}, u32[]{:S(2)}) %all-to-all-start) | async-done | bytes 2097184 | tf_op jit(solution)/shard_map/all_to_all | solution.py:362
  100.2 4.6 %all-to-all-start.2 = ((bf16[4,2,128,1024]{3,2,1,0:T(8,128)(2,1)}), bf16[4,2,128,1024]{3,2,1,0:T(8,128)(2,1)}, u32[]{:S(2)}, u32[]{:S(2)}) async-start(bf16[4,2,128,1024]{3,2,1,0:T(8,128)(2,1)} %bitcast.12), calls=%async_computation.2 | async-start | bytes 4194304 | tf_op jit(solution)/shard_map/all_to_all | solution.py:362
  104.9 24.0 %head_own.1 = (bf16[4,2,128,1024]{3,2,1,0:T(8,128)(2,1)}, bf16[2,2,256,1024]{3,2,1,0:T(8,128)(2,1)}, bf16[2,2,256,1024]{3,2,1,0:T(8,128)(2,1)}) custom-call(s32[5]{0:T(128)} %stack.23.table_ref, bf16[4,2,128,1024]{3,2,1,0:T(8,128)(2,1)} %copy-done.10, bf16[4,2,256,1024]{3,2,1,0:T(8,128)(2,1)} %all-gather.2.cloned.1.call-done.refs_0_), custom_call_target="tpu_custom_call" | custom-call | flops 25769803776 | bytes 14680064 | tf_op jit(solution)/shard_map/head_own/pallas_call | solution.py:279
  130.0 25.3 %collective-permute-done.4.refs_1_ = bf16[1,2,256,1024]{3,2,1,0:T(8,128)(2,1)} collective-permute-done((bf16[1,2,256,1024]{3,2,1,0:T(8,128)(2,1)}, bf16[1,2,256,1024]{3,2,1,0:T(8,128)(2,1)}, u32[]{:S(2)}, u32[]{:S(2)}) %collective-permute-start.4) | collective-permute-done | bytes 1048608 | tf_op jit(solution)/shard_map/ppermute | solution.py:377
  159.1 3.8 %all-to-all-start.1 = ((bf16[4,2,128,1024]{3,2,1,0:T(8,128)(2,1)}), bf16[4,2,128,1024]{3,2,1,0:T(8,128)(2,1)S(1)}, u32[]{:S(2)}, u32[]{:S(2)}) async-start(bf16[4,2,128,1024]{3,2,1,0:T(8,128)(2,1)} %get-tuple-element.20), calls=%async_computation.1 | async-start | bytes 4194304 | tf_op jit(solution)/shard_map/all_to_all | solution.py:362
  163.0 15.8 %head_mirror.1 = (bf16[4,2,128,1024]{3,2,1,0:T(8,128)(2,1)}, bf16[2,2,256,1024]{3,2,1,0:T(8,128)(2,1)}, bf16[2,2,256,1024]{3,2,1,0:T(8,128)(2,1)}) custom-call(s32[5]{0:T(128)} %stack.28.table_ref, bf16[4,2,128,1024]{3,2,1,0:T(8,128)(2,1)} %all-to-all-done.2.rows_ref, bf16[1,2,256,1024]{3,2,1,0:T(8,128)(2,1)} %collective-permute-done.3.refs_0_, ...), custom_call_target="tpu_custom_call" | custom-call | flops 25769803776 | bytes 14680064 | tf_op jit(solution)/shard_map/head_mirror/pallas_call | solution.py:279
  179.4 4.0 %collective-permute-done.7.got_ref = bf16[2,2,256,1024]{3,2,1,0:T(8,128)(2,1)S(1)} collective-permute-done((bf16[2,2,256,1024]{3,2,1,0:T(8,128)(2,1)}, bf16[2,2,256,1024]{3,2,1,0:T(8,128)(2,1)S(1)}, u32[]{:S(2)}, u32[]{:S(2)}) %collective-permute-start.7) | collective-permute-done | bytes 2097184 | tf_op jit(solution)/shard_map/ppermute | solution.py:377
  188.7 4.4 %all-to-all-start.3 = ((bf16[4,2,128,1024]{3,2,1,0:T(8,128)(2,1)}), bf16[4,2,128,1024]{3,2,1,0:T(8,128)(2,1)}, u32[]{:S(2)}, u32[]{:S(2)}) async-start(bf16[4,2,128,1024]{3,2,1,0:T(8,128)(2,1)} %get-tuple-element.31), calls=%async_computation.3 | async-start | bytes 4194304 | tf_op jit(solution)/shard_map/all_to_all | solution.py:362
  193.1 7.0 %collective-permute-start.11 = (bf16[1,1,256,1024]{3,2,1,0:T(8,128)(2,1)}, bf16[1,1,256,1024]{3,2,1,0:T(8,128)(2,1)S(1)}, u32[]{:S(2)}, u32[]{:S(2)}) collective-permute-start(bf16[1,1,256,1024]{3,2,1,0:T(8,128)(2,1)} %copy-done.8), channel_id=1, source_target_pairs={{0,16},{8,24},{16,0},{24,8},{1,17},{9,25},{17,1},{25,9},{2,18},{10... | collective-permute-start | bytes 1572872 | tf_op jit(solution)/shard_map/ppermute | solution.py:377
  200.2 2.0 collective-permute-start.8
  202.2 10.9 %collective-permute-done.11 = bf16[1,1,256,1024]{3,2,1,0:T(8,128)(2,1)S(1)} collective-permute-done((bf16[1,1,256,1024]{3,2,1,0:T(8,128)(2,1)}, bf16[1,1,256,1024]{3,2,1,0:T(8,128)(2,1)S(1)}, u32[]{:S(2)}, u32[]{:S(2)}) %collective-permute-start.11) | collective-permute-done | bytes 524320 | tf_op jit(solution)/shard_map/ppermute | solution.py:377
  213.1 2.0 fusion.1
  215.1 9.2 %collective-permute-done.9 = bf16[1,1,256,1024]{3,2,1,0:T(8,128)(2,1)S(1)} collective-permute-done((bf16[1,1,256,1024]{3,2,1,0:T(8,128)(2,1)}, bf16[1,1,256,1024]{3,2,1,0:T(8,128)(2,1)S(1)}, u32[]{:S(2)}, u32[]{:S(2)}) %collective-permute-start.9) | collective-permute-done | bytes 524320 | tf_op jit(solution)/shard_map/ppermute | solution.py:377
  224.3 2.1 fusion
  226.4 5.5 %place_rows.1 = bf16[8,128,1024]{2,1,0:T(8,128)(2,1)} custom-call(s32[1,9]{1,0:T(1,128)S(1)} %pad_add_fusion.info_ref, bf16[4,2,128,1024]{3,2,1,0:T(8,128)(2,1)S(1)} %all-to-all-done.1.own_ref, bf16[4,2,128,1024]{3,2,1,0:T(8,128)(2,1)} %all-to-all-done.3.mirror_ref), custom_call_target="tpu_custom_call" | custom-call | tf_op jit(solution)/shard_map/place_rows/pallas_call | solution.py:334
  231.9 21.7 %collective-permute-done.12.refs_3_ = bf16[1,256,1024]{2,1,0:T(8,128)(2,1)} collective-permute-done((bf16[1,256,1024]{2,1,0:T(8,128)(2,1)}, bf16[1,256,1024]{2,1,0:T(8,128)(2,1)}, u32[]{:S(2)}, u32[]{:S(2)}) %collective-permute-start.12) | collective-permute-done | bytes 524320 | tf_op jit(solution)/shard_map/ppermute | solution.py:368
  253.6 9.1 %collective-permute-done.10.refs_2_ = bf16[1,256,1024]{2,1,0:T(8,128)(2,1)} collective-permute-done((bf16[1,256,1024]{2,1,0:T(8,128)(2,1)}, bf16[1,256,1024]{2,1,0:T(8,128)(2,1)}, u32[]{:S(2)}, u32[]{:S(2)}) %collective-permute-start.10) | collective-permute-done | bytes 524320 | tf_op jit(solution)/shard_map/ppermute | solution.py:368
  262.7 3.2 %total_shares.1 = f32[2,256,1024]{2,1,0:T(8,128)} custom-call(bf16[2,256,1024]{2,1,0:T(8,128)(2,1)S(1)} %bitcast.31, bf16[2,256,1024]{2,1,0:T(8,128)(2,1)} %bitcast.17.refs_1_, bf16[1,256,1024]{2,1,0:T(8,128)(2,1)} %collective-permute-done.10.refs_2_, bf16[1,256,1024]{2,1,0:T(8,128)(2,1)} %collective-permute-done.12.refs_3_), custom_call_target="tpu_custom_call" | custom-call | tf_op jit(solution)/shard_map/total_shares/pallas_call | solution.py:442
  (59 shorter events, 17.6 us)
Async XLA Ops:
  7.2 12.6 %copy-start.1 = (bf16[1,1024,1024]{2,1,0:T(8,128)(2,1)S(1)}, bf16[1,1024,1024]{2,1,0:T(8,128)(2,1)}, u32[]{:S(2)}) copy-start(bf16[1,1024,1024]{2,1,0:T(8,128)(2,1)} %param.8) | copy-start | bytes 6291460
  7.2 8.1 %copy-start.11 = (s32[1,4,1024]{2,1,0:T(4,128)S(1)}, s32[1,4,1024]{2,1,0:T(4,128)}, u32[]{:S(2)}) copy-start(s32[1,4,1024]{2,1,0:T(4,128)} %param.9) | copy-start | bytes 49156
  7.2 8.4 %copy-start.12 = (s32[1,4,1024]{2,1,0:T(4,128)S(1)}, s32[1,4,1024]{2,1,0:T(4,128)}, u32[]{:S(2)}) copy-start(s32[1,4,1024]{2,1,0:T(4,128)} %param.10) | copy-start | bytes 49156
  7.2 8.4 %copy-start.13 = (s32[1,8]{1,0:T(1,128)S(1)}, s32[1,8]{1,0:T(1,128)}, u32[]{:S(2)}) copy-start(s32[1,8]{1,0:T(1,128)} %param.12) | copy-start | bytes 100
  7.2 12.5 %copy-start.9 = (f32[1024]{0:T(1024)S(1)}, f32[1024]{0:T(1024)}, u32[]{:S(2)}) copy-start(f32[1024]{0:T(1024)} %param.14) | copy-start | bytes 12292
  7.2 97.7 %all-gather.2.cloned.1.call-start = ((), (), s32[]{:S(2)}) async-start(), calls=%async_computation.4 | async-start | bytes 5242880 | tf_op jit(solution)/shard_map/all_gather | solution.py:459
  11.6 4.1 %collective-permute-start = (bf16[128,1024]{1,0:T(8,128)(2,1)}, bf16[128,1024]{1,0:T(8,128)(2,1)S(1)}, u32[]{:S(2)}, u32[]{:S(2)}) collective-permute-start(bf16[128,1024]{1,0:T(8,128)(2,1)} %pick_rows.1), channel_id=1, source_target_pairs={{0,8},{8,16},{16,24},{1,9},{9,17},{17,25},{2,10},{10,18},{18,26},{... | collective-permute-start | bytes 786440 | tf_op jit(solution)/shard_map/ppermute | solution.py:355
  14.0 5.8 %collective-permute-start.1 = (bf16[128,1024]{1,0:T(8,128)(2,1)}, bf16[128,1024]{1,0:T(8,128)(2,1)S(1)}, u32[]{:S(2)}, u32[]{:S(2)}) collective-permute-start(bf16[128,1024]{1,0:T(8,128)(2,1)} %pick_rows.1), channel_id=1, source_target_pairs={{8,0},{16,8},{24,16},{9,1},{17,9},{25,17},{10,2},{18,10},{26,18},{... | collective-permute-start | bytes 786440 | tf_op jit(solution)/shard_map/ppermute | solution.py:356
  19.8 1.6 copy-start.5
  47.5 51.4 %all-to-all-start = ((bf16[4,2,128,1024]{3,2,1,0:T(8,128)(2,1)}), bf16[4,2,128,1024]{3,2,1,0:T(8,128)(2,1)S(1)}, u32[]{:S(2)}, u32[]{:S(2)}) async-start(bf16[4,2,128,1024]{3,2,1,0:T(8,128)(2,1)} %bitcast.37), calls=%async_computation | async-start | bytes 4194304 | tf_op jit(solution)/shard_map/all_to_all | solution.py:362
  51.2 78.6 %collective-permute-start.3 = (bf16[1,2,256,1024]{3,2,1,0:T(8,128)(2,1)}, bf16[1,2,256,1024]{3,2,1,0:T(8,128)(2,1)}, u32[]{:S(2)}, u32[]{:S(2)}) collective-permute-start(bf16[1,2,256,1024]{3,2,1,0:T(8,128)(2,1)} %param.15), channel_id=1, source_target_pairs={{0,4},{1,5},{2,6},{3,7},{4,0},{5,1},{6,2},{7,3},{8,12},{9,13},{10,... | collective-permute-start | bytes 3145736 | tf_op jit(solution)/shard_map/ppermute | solution.py:368
  100.2 58.9 %all-to-all-start.2 = ((bf16[4,2,128,1024]{3,2,1,0:T(8,128)(2,1)}), bf16[4,2,128,1024]{3,2,1,0:T(8,128)(2,1)}, u32[]{:S(2)}, u32[]{:S(2)}) async-start(bf16[4,2,128,1024]{3,2,1,0:T(8,128)(2,1)} %bitcast.12), calls=%async_computation.2 | async-start | bytes 4194304 | tf_op jit(solution)/shard_map/all_to_all | solution.py:362
  128.9 27.1 %collective-permute-start.2 = (bf16[2,2,256,1024]{3,2,1,0:T(8,128)(2,1)}, bf16[2,2,256,1024]{3,2,1,0:T(8,128)(2,1)S(1)}, u32[]{:S(2)}, u32[]{:S(2)}) collective-permute-start(bf16[2,2,256,1024]{3,2,1,0:T(8,128)(2,1)} %get-tuple-element.23), channel_id=1, source_target_pairs={{0,8},{8,0},{16,24},{24,16},{1,9},{9,1},{17,25},{25,17},{2,10},{10... | collective-permute-start | bytes 6291464 | tf_op jit(solution)/shard_map/ppermute | solution.py:377
  129.8 25.5 %collective-permute-start.4 = (bf16[1,2,256,1024]{3,2,1,0:T(8,128)(2,1)}, bf16[1,2,256,1024]{3,2,1,0:T(8,128)(2,1)}, u32[]{:S(2)}, u32[]{:S(2)}) collective-permute-start(bf16[1,2,256,1024]{3,2,1,0:T(8,128)(2,1)} %collective-permute-done.3.refs_0_), channel_id=1, source_target_pairs={{0,16},{8,24},{16,0},{24,8},{1,17},{9,25},{17,1},{25,9},{2,18},{10... | collective-permute-start | bytes 3145736 | tf_op jit(solution)/shard_map/ppermute | solution.py:377
  129.8 33.1 %collective-permute-start.5 = (bf16[1,2,256,1024]{3,2,1,0:T(8,128)(2,1)}, bf16[1,2,256,1024]{3,2,1,0:T(8,128)(2,1)}, u32[]{:S(2)}, u32[]{:S(2)}) collective-permute-start(bf16[1,2,256,1024]{3,2,1,0:T(8,128)(2,1)} %collective-permute-done.3.refs_0_), channel_id=1, source_target_pairs={{0,8},{8,0},{16,24},{24,16},{1,9},{9,1},{17,25},{25,17},{2,10},{10... | collective-permute-start | bytes 3145736 | tf_op jit(solution)/shard_map/ppermute | solution.py:377
  155.3 7.7 %collective-permute-start.6 = (bf16[1,2,256,1024]{3,2,1,0:T(8,128)(2,1)}, bf16[1,2,256,1024]{3,2,1,0:T(8,128)(2,1)}, u32[]{:S(2)}, u32[]{:S(2)}) collective-permute-start(bf16[1,2,256,1024]{3,2,1,0:T(8,128)(2,1)} %collective-permute-done.4.refs_1_), channel_id=1, source_target_pairs={{0,8},{8,0},{16,24},{24,16},{1,9},{9,1},{17,25},{25,17},{2,10},{10... | collective-permute-start | bytes 3145736 | tf_op jit(solution)/shard_map/ppermute | solution.py:377
  159.1 29.5 %all-to-all-start.1 = ((bf16[4,2,128,1024]{3,2,1,0:T(8,128)(2,1)}), bf16[4,2,128,1024]{3,2,1,0:T(8,128)(2,1)S(1)}, u32[]{:S(2)}, u32[]{:S(2)}) async-start(bf16[4,2,128,1024]{3,2,1,0:T(8,128)(2,1)} %get-tuple-element.20), calls=%async_computation.1 | async-start | bytes 4194304 | tf_op jit(solution)/shard_map/all_to_all | solution.py:362
  178.8 4.6 %collective-permute-start.7 = (bf16[2,2,256,1024]{3,2,1,0:T(8,128)(2,1)}, bf16[2,2,256,1024]{3,2,1,0:T(8,128)(2,1)S(1)}, u32[]{:S(2)}, u32[]{:S(2)}) collective-permute-start(bf16[2,2,256,1024]{3,2,1,0:T(8,128)(2,1)} %get-tuple-element.28), channel_id=1, source_target_pairs={{0,8},{8,0},{16,24},{24,16},{1,9},{9,1},{17,25},{25,17},{2,10},{10... | collective-permute-start | bytes 6291464 | tf_op jit(solution)/shard_map/ppermute | solution.py:377
  188.7 37.7 %all-to-all-start.3 = ((bf16[4,2,128,1024]{3,2,1,0:T(8,128)(2,1)}), bf16[4,2,128,1024]{3,2,1,0:T(8,128)(2,1)}, u32[]{:S(2)}, u32[]{:S(2)}) async-start(bf16[4,2,128,1024]{3,2,1,0:T(8,128)(2,1)} %get-tuple-element.31), calls=%async_computation.3 | async-start | bytes 4194304 | tf_op jit(solution)/shard_map/all_to_all | solution.py:362
  193.1 20.0 %collective-permute-start.11 = (bf16[1,1,256,1024]{3,2,1,0:T(8,128)(2,1)}, bf16[1,1,256,1024]{3,2,1,0:T(8,128)(2,1)S(1)}, u32[]{:S(2)}, u32[]{:S(2)}) collective-permute-start(bf16[1,1,256,1024]{3,2,1,0:T(8,128)(2,1)} %copy-done.8), channel_id=1, source_target_pairs={{0,16},{8,24},{16,0},{24,8},{1,17},{9,25},{17,1},{25,9},{2,18},{10... | collective-permute-start | bytes 1572872 | tf_op jit(solution)/shard_map/ppermute | solution.py:377
  200.1 24.2 %collective-permute-start.9 = (bf16[1,1,256,1024]{3,2,1,0:T(8,128)(2,1)}, bf16[1,1,256,1024]{3,2,1,0:T(8,128)(2,1)S(1)}, u32[]{:S(2)}, u32[]{:S(2)}) collective-permute-start(bf16[1,1,256,1024]{3,2,1,0:T(8,128)(2,1)} %copy-done.7), channel_id=1, source_target_pairs={{0,16},{8,24},{16,0},{24,8},{1,17},{9,25},{17,1},{25,9},{2,18},{10... | collective-permute-start | bytes 1572872 | tf_op jit(solution)/shard_map/ppermute | solution.py:377
  200.2 53.5 %collective-permute-start.8 = (bf16[2,1,256,1024]{3,2,0,1:T(8,128)(2,1)}, bf16[2,1,256,1024]{3,2,0,1:T(8,128)(2,1)}, u32[]{:S(2)}, u32[]{:S(2)}) collective-permute-start(bf16[2,1,256,1024]{3,2,0,1:T(8,128)(2,1)} %bitcast.34), channel_id=1, source_target_pairs={{0,16},{8,24},{16,0},{24,8},{1,17},{9,25},{17,1},{25,9},{2,18},{10... | collective-permute-start | bytes 3145736 | tf_op jit(solution)/shard_map/ppermute | solution.py:377
  215.1 38.5 %collective-permute-start.12 = (bf16[1,256,1024]{2,1,0:T(8,128)(2,1)}, bf16[1,256,1024]{2,1,0:T(8,128)(2,1)}, u32[]{:S(2)}, u32[]{:S(2)}) collective-permute-start(bf16[1,256,1024]{2,1,0:T(8,128)(2,1)} %fusion.1), channel_id=1, source_target_pairs={{0,4},{1,5},{2,6},{3,7},{4,0},{5,1},{6,2},{7,3},{8,12},{9,13},{10,... | collective-permute-start | bytes 1572872 | tf_op jit(solution)/shard_map/ppermute | solution.py:368
  226.4 36.3 %collective-permute-start.10 = (bf16[1,256,1024]{2,1,0:T(8,128)(2,1)}, bf16[1,256,1024]{2,1,0:T(8,128)(2,1)}, u32[]{:S(2)}, u32[]{:S(2)}) collective-permute-start(bf16[1,256,1024]{2,1,0:T(8,128)(2,1)} %fusion), channel_id=1, source_target_pairs={{0,4},{1,5},{2,6},{3,7},{4,0},{5,1},{6,2},{7,3},{8,12},{9,13},{10,... | collective-permute-start | bytes 1572872 | tf_op jit(solution)/shard_map/ppermute | solution.py:368
  (8 other events, 8.7 us)
Sparse Core Ops, SparseCore 0:
  15.4 39.0 all-gather.1

commit v5 on v4

--- a/solution.py
+++ b/solution.py
@@ -294,7 +294,7 @@
             jax.ShapeDtypeStruct(part, BF16),
             jax.ShapeDtypeStruct(part, BF16),
         ],
-        compiler_params=pltpu.CompilerParams(vmem_limit_bytes=VMEM),
+        compiler_params=pltpu.CompilerParams(vmem_limit_bytes=44 * MB),
         cost_estimate=pl.CostEstimate(
             flops=24 * total * width * width,
             bytes_accessed=5 * total * width * 2 + width * width * 4,
@@ -375,15 +375,6 @@
 def swap(array, bit):
     count = lax.axis_size("dom")
     return lax.ppermute(array, "dom", [(i, i ^ (1 << bit)) for i in range(count)])
-
-
-def spread_over_dom(shard):
-    place = lax.axis_index("dom").astype(jnp.int32)
-    pieces, places = [shard], [place]
-    for bit in reversed(range(lax.axis_size("dom").bit_length() - 1)):
-        pieces += [swap(piece, bit) for piece in pieces]
-        places += [there ^ (1 << bit) for there in places]
-    return pieces, places
 
 
 def merge_kernel(bit_ref, keep_ref, got_ref, send_ref, kept_ref):
@@ -467,7 +458,7 @@
     )
     own_rows = exchange(own_blocks, half)
     mirror_rows = exchange(mirror_blocks, half)
-    far_pieces, far_places = spread_over_dom(far)
+    mirror_weights = lax.all_gather(far[0], "dom", axis=0, tiled=False)
 
     scale = 1.0 / math.sqrt(count * row_count)
     orders = [jnp.int32(i) for i in range(count)]
@@ -476,11 +467,11 @@
     own_keep, own_got, own_sent = sum_over_dom(send, keep, swap(send, 0), 0, 2)
 
     mirror_rows = after(mirror_rows, own_sent)
-    back, send, keep = run_head(mirror_rows, far_pieces, far_places, scale, "head_mirror")
+    back, send, keep = run_head(mirror_rows, [mirror_weights], orders, scale, "head_mirror")
     got = swap(send, 0)
     high_keep, high_got, high_sent = sum_over_dom(send, keep, got, 1, 1)
     low_keep, low_got, low_sent = sum_over_dom(send, keep, got, 0, 1)
-    mirror_back = exchange(after(back, high_sent, low_sent), half)
+    mirror_back = exchange(after(back, high_got, low_sent), half)
     high_part = across((high_keep.astype(F32) + high_got.astype(F32)).astype(BF16), half)
     low_part = across((low_keep.astype(F32) + low_got.astype(F32)).astype(BF16), half)
     row_part = place_rows(info, own_back, mirror_back, row_blocks)

time: 274 us -> 252 us (0.920)
  waiting for transfers between devices: 129 us -> 107 us
  Pallas kernels: 78.4 us -> 66.9 us
  starting transfers between devices: 33.7 us -> 44 us
    all_to_all x4, waiting for transfers between devices: 44.5 us -> 12 us  [exchange(): lax.all_to_all(blocks, 'head', split_axis=0, concat_axis=0, axis_index_gr...]
    ppermute x3, waiting for transfers between devices: 30.8 us -> 62.6 us  [across(): lax.ppermute(array, 'head', [(i, (i + half) % (2 * half)) for i in range(...]
    ppermute x8 -> x5, waiting for transfers between devices: 49.4 us -> 25.4 us  [swap(): return lax.ppermute(array, 'dom', [(i, i ^ 1 << bit) for i in range(count)])]
    pallas_call x2, Pallas kernels: 39.8 us -> 26.9 us  [run_head(): pl.pallas_call(functools.partial(head_kernel, sizes, scale), grid_spec=pl...]
    ppermute x3, starting transfers between devices: 2.59 us -> 9.66 us  [across(): lax.ppermute(array, 'head', [(i, (i + half) % (2 * half)) for i in range(...]
    unnamed x30 -> x40, local copies, waits for them, and re-layouts: 10.5 us -> 13.9 us
    ppermute x8 -> x5, starting transfers between devices: 10.7 us -> 13.9 us  [swap(): return lax.ppermute(array, 'dom', [(i, i ^ 1 << bit) for i in range(count)])]
  transfers between devices with their start and end apart: 18 -> 16, of which waited for: 8 -> 11; matrix products, arithmetic and copies ran while one was open for 2% -> 2% of each run, Pallas kernels for 27% -> 25%
where the time goes in v5:
time: 252 us; the launch traced here: 250 us
  waiting for transfers between devices  107 us (42%)
  Pallas kernels  66.9 us (27%)
  starting transfers between devices  44 us (17%)
  local copies, waits for them, and re-layouts  15.4 us (6%)
  between operations  14.3 us (6%)
    ppermute x3, waiting for transfers between devices, across(): lax.ppermute(array, 'head', [(i, (i + half) % (2 * half)) for i in range(...  62.6 us
    pallas_call x2, Pallas kernels, run_head(): pl.pallas_call(functools.partial(head_kernel, sizes, scale), grid_spec=pl...  26.9 us
    pallas_call x1, Pallas kernels, encode(): pl.pallas_call(functools.partial(encode_kernel, half), grid_spec=pltpu.Pr...  26.1 us
    ppermute x5, waiting for transfers between devices, swap(): return lax.ppermute(array, 'dom', [(i, i ^ 1 << bit) for i in range(count)])  25.4 us
    all_to_all x4, starting transfers between devices, exchange(): lax.all_to_all(blocks, 'head', split_axis=0, concat_axis=0, axis_index_gr...  16.7 us
    unnamed x40, local copies, waits for them, and re-layouts  13.9 us
    ppermute x5, starting transfers between devices, swap(): return lax.ppermute(array, 'dom', [(i, i ^ 1 << bit) for i in range(count)])  13.9 us
    all_to_all x4, waiting for transfers between devices, exchange(): lax.all_to_all(blocks, 'head', split_axis=0, concat_axis=0, axis_index_gr...  12 us
  transfers between devices with their start and end apart: 16, of which 11 were waited for; matrix products, arithmetic and copies ran while one was open for 2% of the time, Pallas kernels for 25%

profile of v5, /device:TPU:0, one launch (start us, length us, event | category | flops | bytes accessed | tf_op | source)
XLA Modules:
  0.0 249.9 jit_solution(9129692532662744225)
XLA Ops:
  9.3 2.8 %pick_rows.1 = bf16[128,1024]{1,0:T(8,128)(2,1)} custom-call(s32[128,1]{1,0:T(8,128)} %copy.13.ids_ref, bf16[1024,1024]{1,0:T(8,128)(2,1)} %bitcast.25), custom_call_target="tpu_custom_call" | custom-call | tf_op jit(solution)/shard_map/pick_rows/pallas_call | solution.py:35
  16.2 4.1 %collective-permute-done.1.high_ref = bf16[128,1024]{1,0:T(8,128)(2,1)S(1)} collective-permute-done((bf16[128,1024]{1,0:T(8,128)(2,1)}, bf16[128,1024]{1,0:T(8,128)(2,1)S(1)}, u32[]{:S(2)}, u32[]{:S(2)}) %collective-permute-start.1) | collective-permute-done | bytes 262176 | tf_op jit(solution)/shard_map/ppermute | solution.py:356
  22.4 26.1 %encode_rows.1 = (bf16[8,128,1024]{2,1,0:T(8,128)(2,1)}, bf16[8,128,1024]{2,1,0:T(8,128)(2,1)}) custom-call(s32[1,9]{1,0:T(1,128)S(1)} %pad_add_fusion.info_ref, s32[4096]{0:T(1024)S(1)} %bitcast.29, bf16[1024,1024]{1,0:T(8,128)(2,1)S(1)} %bitcast.26, bf16[128,1024]{1,0:T(8,128)(2,1)S(1)} %collective-permute-done.low_ref, ...), custom_call_target="tpu_custom_call" | custom-call | flops 42949672960 | bytes 31457280 | tf_op jit(solution)/shard_map/encode_rows/pallas_call | solution.py:161
  48.5 3.8 %all-to-all-start = ((bf16[4,2,128,1024]{3,2,1,0:T(8,128)(2,1)}), bf16[4,2,128,1024]{3,2,1,0:T(8,128)(2,1)S(1)}, u32[]{:S(2)}, u32[]{:S(2)}) async-start(bf16[4,2,128,1024]{3,2,1,0:T(8,128)(2,1)} %bitcast.33), calls=%async_computation | async-start | bytes 4194304 | tf_op jit(solution)/shard_map/all_to_all | solution.py:362
  52.3 2.7 %collective-permute-start.3 = (bf16[1,2,256,1024]{3,2,1,0:T(8,128)(2,1)S(1)}, bf16[1,2,256,1024]{3,2,1,0:T(8,128)(2,1)}, u32[]{:S(2)}, u32[]{:S(2)}) collective-permute-start(bf16[1,2,256,1024]{3,2,1,0:T(8,128)(2,1)S(1)} %copy-done.15), channel_id=1, source_target_pairs={{0,4},{1,5},{2,6},{3,7},{4,0},{5,1},{6,2},{7,3},{8,12},{9,13},{10,... | collective-permute-start | bytes 3145736 | tf_op jit(solution)/shard_map/ppermute | solution.py:368
  55.0 34.6 %collective-permute-done.3 = bf16[1,2,256,1024]{3,2,1,0:T(8,128)(2,1)} collective-permute-done((bf16[1,2,256,1024]{3,2,1,0:T(8,128)(2,1)S(1)}, bf16[1,2,256,1024]{3,2,1,0:T(8,128)(2,1)}, u32[]{:S(2)}, u32[]{:S(2)}) %collective-permute-start.3) | collective-permute-done | bytes 1048608 | tf_op jit(solution)/shard_map/ppermute | solution.py:368
  89.7 10.4 %all-to-all-done.rows_ref = bf16[4,2,128,1024]{3,2,1,0:T(8,128)(2,1)S(1)} async-done(((bf16[4,2,128,1024]{3,2,1,0:T(8,128)(2,1)}), bf16[4,2,128,1024]{3,2,1,0:T(8,128)(2,1)S(1)}, u32[]{:S(2)}, u32[]{:S(2)}) %all-to-all-start) | async-done | bytes 2097184 | tf_op jit(solution)/shard_map/all_to_all | solution.py:362
  100.1 4.7 %all-to-all-start.2 = ((bf16[4,2,128,1024]{3,2,1,0:T(8,128)(2,1)}), bf16[4,2,128,1024]{3,2,1,0:T(8,128)(2,1)}, u32[]{:S(2)}, u32[]{:S(2)}) async-start(bf16[4,2,128,1024]{3,2,1,0:T(8,128)(2,1)} %bitcast.32), calls=%async_computation.2 | async-start | bytes 4194304 | tf_op jit(solution)/shard_map/all_to_all | solution.py:362
  104.8 13.6 %head_own.1 = (bf16[4,2,128,1024]{3,2,1,0:T(8,128)(2,1)S(1)}, bf16[2,2,256,1024]{3,2,1,0:T(8,128)(2,1)}, bf16[2,2,256,1024]{3,2,1,0:T(8,128)(2,1)S(1)}) custom-call(s32[5]{0:T(128)S(1)} %stack.9.table_ref, bf16[4,2,128,1024]{3,2,1,0:T(8,128)(2,1)S(1)} %all-to-all-done.rows_ref, bf16[4,2,256,1024]{3,2,1,0:T(8,128)(2,1)} %all-gather.3.cloned.1.call-done.refs_0_), custom_call_target="tpu_custom_call" | custom-call | flops 25769803776 | bytes 14680064 | tf_op jit(solution)/shard_map/head_own/pallas_call | solution.py:279
  122.0 4.2 %collective-permute-done.2.got_ref = bf16[2,2,256,1024]{3,2,1,0:T(8,128)(2,1)S(1)} collective-permute-done((bf16[2,2,256,1024]{3,2,1,0:T(8,128)(2,1)}, bf16[2,2,256,1024]{3,2,1,0:T(8,128)(2,1)S(1)}, u32[]{:S(2)}, u32[]{:S(2)}) %collective-permute-start.2) | collective-permute-done | bytes 2097184 | tf_op jit(solution)/shard_map/ppermute | solution.py:377
  130.7 3.8 %all-to-all-start.1 = ((bf16[4,2,128,1024]{3,2,1,0:T(8,128)(2,1)}), bf16[4,2,128,1024]{3,2,1,0:T(8,128)(2,1)S(1)}, u32[]{:S(2)}, u32[]{:S(2)}) async-start(bf16[4,2,128,1024]{3,2,1,0:T(8,128)(2,1)} %copy-done.6), calls=%async_computation.1 | async-start | bytes 4194304 | tf_op jit(solution)/shard_map/all_to_all | solution.py:362
  134.5 2.5 %all-gather.5.cloned.1.call-done.refs_0_ = bf16[4,2,256,1024]{3,2,1,0:T(8,128)(2,1)} async-done(((bf16[1,2,256,1024]{3,2,1,0:T(8,128)(2,1)}), bf16[4,2,256,1024]{3,2,1,0:T(8,128)(2,1)}) %all-gather.5.cloned.1.call-update) | async-done | bytes 4194320 | tf_op jit(solution)/shard_map/all_gather | solution.py:461
  137.1 13.4 %head_mirror.1 = (bf16[4,2,128,1024]{3,2,1,0:T(8,128)(2,1)S(1)}, bf16[2,2,256,1024]{3,2,1,0:T(8,128)(2,1)S(1)}, bf16[2,2,256,1024]{3,2,1,0:T(8,128)(2,1)S(1)}) custom-call(s32[5]{0:T(128)S(1)} %stack.9.table_ref, bf16[4,2,128,1024]{3,2,1,0:T(8,128)(2,1)} %all-to-all-done.2.rows_ref, bf16[4,2,256,1024]{3,2,1,0:T(8,128)(2,1)} %all-gather.5.cloned.1.call-done.refs_0_), custom_call_target="tpu_custom_call" | custom-call | flops 25769803776 | bytes 14680064 | tf_op jit(solution)/shard_map/head_mirror/pallas_call | solution.py:279
  151.8 8.5 %collective-permute-start.4 = (bf16[2,2,256,1024]{3,2,1,0:T(8,128)(2,1)S(1)}, bf16[2,2,256,1024]{3,2,1,0:T(8,128)(2,1)S(1)}, u32[]{:S(2)}, u32[]{:S(2)}) collective-permute-start(bf16[2,2,256,1024]{3,2,1,0:T(8,128)(2,1)S(1)} %get-tuple-element.28), channel_id=1, source_target_pairs={{0,8},{8,0},{16,24},{24,16},{1,9},{9,1},{17,25},{25,17},{2,10},{10... | collective-permute-start | bytes 6291464 | tf_op jit(solution)/shard_map/ppermute | solution.py:377
  160.3 3.8 %collective-permute-done.4.got_ref = bf16[2,2,256,1024]{3,2,1,0:T(8,128)(2,1)S(1)} collective-permute-done((bf16[2,2,256,1024]{3,2,1,0:T(8,128)(2,1)S(1)}, bf16[2,2,256,1024]{3,2,1,0:T(8,128)(2,1)S(1)}, u32[]{:S(2)}, u32[]{:S(2)}) %collective-permute-start.4) | collective-permute-done | bytes 2097184 | tf_op jit(solution)/shard_map/ppermute | solution.py:377
  167.1 4.5 %all-to-all-start.3 = ((bf16[4,2,128,1024]{3,2,1,0:T(8,128)(2,1)}), bf16[4,2,128,1024]{3,2,1,0:T(8,128)(2,1)}, u32[]{:S(2)}, u32[]{:S(2)}) async-start(bf16[4,2,128,1024]{3,2,1,0:T(8,128)(2,1)} %copy-done.5), calls=%async_computation.3 | async-start | bytes 4194304 | tf_op jit(solution)/shard_map/all_to_all | solution.py:362
  179.5 10.7 %collective-permute-done.8 = bf16[1,1,256,1024]{3,2,1,0:T(8,128)(2,1)S(1)} collective-permute-done((bf16[1,1,256,1024]{3,2,1,0:T(8,128)(2,1)S(1)}, bf16[1,1,256,1024]{3,2,1,0:T(8,128)(2,1)S(1)}, u32[]{:S(2)}, u32[]{:S(2)}) %collective-permute-start.8) | collective-permute-done | bytes 524320 | tf_op jit(solution)/shard_map/ppermute | solution.py:377
  191.1 3.5 %collective-permute-start.9 = (bf16[1,256,1024]{2,1,0:T(8,128)(2,1)}, bf16[1,256,1024]{2,1,0:T(8,128)(2,1)}, u32[]{:S(2)}, u32[]{:S(2)}) collective-permute-start(bf16[1,256,1024]{2,1,0:T(8,128)(2,1)} %fusion.1), channel_id=1, source_target_pairs={{0,4},{1,5},{2,6},{3,7},{4,0},{5,1},{6,2},{7,3},{8,12},{9,13},{10,... | collective-permute-start | bytes 1572872 | tf_op jit(solution)/shard_map/ppermute | solution.py:368
  194.6 6.8 %collective-permute-done.6 = bf16[1,1,256,1024]{3,2,1,0:T(8,128)(2,1)S(1)} collective-permute-done((bf16[1,1,256,1024]{3,2,1,0:T(8,128)(2,1)S(1)}, bf16[1,1,256,1024]{3,2,1,0:T(8,128)(2,1)S(1)}, u32[]{:S(2)}, u32[]{:S(2)}) %collective-permute-start.6) | collective-permute-done | bytes 524320 | tf_op jit(solution)/shard_map/ppermute | solution.py:377
  202.4 3.5 %collective-permute-start.7 = (bf16[1,256,1024]{2,1,0:T(8,128)(2,1)}, bf16[1,256,1024]{2,1,0:T(8,128)(2,1)}, u32[]{:S(2)}, u32[]{:S(2)}) collective-permute-start(bf16[1,256,1024]{2,1,0:T(8,128)(2,1)} %fusion), channel_id=1, source_target_pairs={{0,4},{1,5},{2,6},{3,7},{4,0},{5,1},{6,2},{7,3},{8,12},{9,13},{10,... | collective-permute-start | bytes 1572872 | tf_op jit(solution)/shard_map/ppermute | solution.py:368
  205.9 6.0 %place_rows.1 = bf16[8,128,1024]{2,1,0:T(8,128)(2,1)} custom-call(s32[1,9]{1,0:T(1,128)S(1)} %pad_add_fusion.info_ref, bf16[4,2,128,1024]{3,2,1,0:T(8,128)(2,1)S(1)} %all-to-all-done.1.own_ref, bf16[4,2,128,1024]{3,2,1,0:T(8,128)(2,1)} %all-to-all-done.3.mirror_ref), custom_call_target="tpu_custom_call" | custom-call | tf_op jit(solution)/shard_map/place_rows/pallas_call | solution.py:334
  211.9 18.4 %collective-permute-done.9.refs_3_ = bf16[1,256,1024]{2,1,0:T(8,128)(2,1)} collective-permute-done((bf16[1,256,1024]{2,1,0:T(8,128)(2,1)}, bf16[1,256,1024]{2,1,0:T(8,128)(2,1)}, u32[]{:S(2)}, u32[]{:S(2)}) %collective-permute-start.9) | collective-permute-done | bytes 524320 | tf_op jit(solution)/shard_map/ppermute | solution.py:368
  230.2 9.6 %collective-permute-done.7.refs_2_ = bf16[1,256,1024]{2,1,0:T(8,128)(2,1)} collective-permute-done((bf16[1,256,1024]{2,1,0:T(8,128)(2,1)}, bf16[1,256,1024]{2,1,0:T(8,128)(2,1)}, u32[]{:S(2)}, u32[]{:S(2)}) %collective-permute-start.7) | collective-permute-done | bytes 524320 | tf_op jit(solution)/shard_map/ppermute | solution.py:368
  239.9 3.2 %total_shares.1 = f32[2,256,1024]{2,1,0:T(8,128)} custom-call(bf16[2,256,1024]{2,1,0:T(8,128)(2,1)S(1)} %bitcast.27, bf16[2,256,1024]{2,1,0:T(8,128)(2,1)} %bitcast.13.refs_1_, bf16[1,256,1024]{2,1,0:T(8,128)(2,1)} %collective-permute-done.7.refs_2_, bf16[1,256,1024]{2,1,0:T(8,128)(2,1)} %collective-permute-done.9.refs_3_), custom_call_target="tpu_custom_call" | custom-call | tf_op jit(solution)/shard_map/total_shares/pallas_call | solution.py:433
  (65 shorter events, 30.7 us)
Async XLA Ops:
  7.2 13.1 %copy-start.4 = (bf16[1,1024,1024]{2,1,0:T(8,128)(2,1)S(1)}, bf16[1,1024,1024]{2,1,0:T(8,128)(2,1)}, u32[]{:S(2)}) copy-start(bf16[1,1024,1024]{2,1,0:T(8,128)(2,1)} %param.8) | copy-start | bytes 6291460
  7.2 8.7 %copy-start.16 = (s32[1,4,1024]{2,1,0:T(4,128)S(1)}, s32[1,4,1024]{2,1,0:T(4,128)}, u32[]{:S(2)}) copy-start(s32[1,4,1024]{2,1,0:T(4,128)} %param.9) | copy-start | bytes 49156
  7.2 8.9 %copy-start.17 = (s32[1,4,1024]{2,1,0:T(4,128)S(1)}, s32[1,4,1024]{2,1,0:T(4,128)}, u32[]{:S(2)}) copy-start(s32[1,4,1024]{2,1,0:T(4,128)} %param.10) | copy-start | bytes 49156
  7.2 8.9 %copy-start.18 = (s32[1,8]{1,0:T(1,128)S(1)}, s32[1,8]{1,0:T(1,128)}, u32[]{:S(2)}) copy-start(s32[1,8]{1,0:T(1,128)} %param.12) | copy-start | bytes 100
  7.2 13.1 %copy-start.14 = (f32[1024]{0:T(1024)S(1)}, f32[1024]{0:T(1024)}, u32[]{:S(2)}) copy-start(f32[1024]{0:T(1024)} %param.14) | copy-start | bytes 12292
  7.2 97.5 %all-gather.3.cloned.1.call-start = ((), (), s32[]{:S(2)}) async-start(), calls=%async_computation.4 | async-start | bytes 5242880 | tf_op jit(solution)/shard_map/all_gather | solution.py:450
  12.2 4.0 %collective-permute-start = (bf16[128,1024]{1,0:T(8,128)(2,1)}, bf16[128,1024]{1,0:T(8,128)(2,1)S(1)}, u32[]{:S(2)}, u32[]{:S(2)}) collective-permute-start(bf16[128,1024]{1,0:T(8,128)(2,1)} %pick_rows.1), channel_id=1, source_target_pairs={{0,8},{8,16},{16,24},{1,9},{9,17},{17,25},{2,10},{10,18},{18,26},{... | collective-permute-start | bytes 786440 | tf_op jit(solution)/shard_map/ppermute | solution.py:355
  14.5 5.8 %collective-permute-start.1 = (bf16[128,1024]{1,0:T(8,128)(2,1)}, bf16[128,1024]{1,0:T(8,128)(2,1)S(1)}, u32[]{:S(2)}, u32[]{:S(2)}) collective-permute-start(bf16[128,1024]{1,0:T(8,128)(2,1)} %pick_rows.1), channel_id=1, source_target_pairs={{8,0},{16,8},{24,16},{9,1},{17,9},{25,17},{10,2},{18,10},{26,18},{... | collective-permute-start | bytes 786440 | tf_op jit(solution)/shard_map/ppermute | solution.py:356
  48.5 3.8 %copy-start.15 = (bf16[1,2,256,1024]{3,2,1,0:T(8,128)(2,1)S(1)}, bf16[1,2,256,1024]{3,2,1,0:T(8,128)(2,1)}, u32[]{:S(2)}) copy-start(bf16[1,2,256,1024]{3,2,1,0:T(8,128)(2,1)} %param.15) | copy-start | bytes 3145732
  48.5 51.6 %all-to-all-start = ((bf16[4,2,128,1024]{3,2,1,0:T(8,128)(2,1)}), bf16[4,2,128,1024]{3,2,1,0:T(8,128)(2,1)S(1)}, u32[]{:S(2)}, u32[]{:S(2)}) async-start(bf16[4,2,128,1024]{3,2,1,0:T(8,128)(2,1)} %bitcast.33), calls=%async_computation | async-start | bytes 4194304 | tf_op jit(solution)/shard_map/all_to_all | solution.py:362
  52.3 84.8 %all-gather.5.cloned.1.call-start = ((), (), s32[]{:S(2)}) async-start(), calls=%async_computation.5 | async-start | bytes 5242880 | tf_op jit(solution)/shard_map/all_gather | solution.py:461
  52.3 37.3 %collective-permute-start.3 = (bf16[1,2,256,1024]{3,2,1,0:T(8,128)(2,1)S(1)}, bf16[1,2,256,1024]{3,2,1,0:T(8,128)(2,1)}, u32[]{:S(2)}, u32[]{:S(2)}) collective-permute-start(bf16[1,2,256,1024]{3,2,1,0:T(8,128)(2,1)S(1)} %copy-done.15), channel_id=1, source_target_pairs={{0,4},{1,5},{2,6},{3,7},{4,0},{5,1},{6,2},{7,3},{8,12},{9,13},{10,... | collective-permute-start | bytes 3145736 | tf_op jit(solution)/shard_map/ppermute | solution.py:368
  100.1 30.6 %all-to-all-start.2 = ((bf16[4,2,128,1024]{3,2,1,0:T(8,128)(2,1)}), bf16[4,2,128,1024]{3,2,1,0:T(8,128)(2,1)}, u32[]{:S(2)}, u32[]{:S(2)}) async-start(bf16[4,2,128,1024]{3,2,1,0:T(8,128)(2,1)} %bitcast.32), calls=%async_computation.2 | async-start | bytes 4194304 | tf_op jit(solution)/shard_map/all_to_all | solution.py:362
  121.1 5.0 %collective-permute-start.2 = (bf16[2,2,256,1024]{3,2,1,0:T(8,128)(2,1)}, bf16[2,2,256,1024]{3,2,1,0:T(8,128)(2,1)S(1)}, u32[]{:S(2)}, u32[]{:S(2)}) collective-permute-start(bf16[2,2,256,1024]{3,2,1,0:T(8,128)(2,1)} %get-tuple-element.23), channel_id=1, source_target_pairs={{0,8},{8,0},{16,24},{24,16},{1,9},{9,1},{17,25},{25,17},{2,10},{10... | collective-permute-start | bytes 6291464 | tf_op jit(solution)/shard_map/ppermute | solution.py:377
  130.7 36.4 %all-to-all-start.1 = ((bf16[4,2,128,1024]{3,2,1,0:T(8,128)(2,1)}), bf16[4,2,128,1024]{3,2,1,0:T(8,128)(2,1)S(1)}, u32[]{:S(2)}, u32[]{:S(2)}) async-start(bf16[4,2,128,1024]{3,2,1,0:T(8,128)(2,1)} %copy-done.6), calls=%async_computation.1 | async-start | bytes 4194304 | tf_op jit(solution)/shard_map/all_to_all | solution.py:362
  151.8 12.6 %copy-start = (bf16[2,2,256,1024]{3,2,1,0:T(8,128)(2,1)}, bf16[2,2,256,1024]{3,2,1,0:T(8,128)(2,1)S(1)}, u32[]{:S(2)}) copy-start(bf16[2,2,256,1024]{3,2,1,0:T(8,128)(2,1)S(1)} %get-tuple-element.27.keep_ref) | copy-start | bytes 6291460
  151.8 12.3 %collective-permute-start.4 = (bf16[2,2,256,1024]{3,2,1,0:T(8,128)(2,1)S(1)}, bf16[2,2,256,1024]{3,2,1,0:T(8,128)(2,1)S(1)}, u32[]{:S(2)}, u32[]{:S(2)}) collective-permute-start(bf16[2,2,256,1024]{3,2,1,0:T(8,128)(2,1)S(1)} %get-tuple-element.28), channel_id=1, source_target_pairs={{0,8},{8,0},{16,24},{24,16},{1,9},{9,1},{17,25},{25,17},{2,10},{10... | collective-permute-start | bytes 6291464 | tf_op jit(solution)/shard_map/ppermute | solution.py:377
  167.1 38.8 %all-to-all-start.3 = ((bf16[4,2,128,1024]{3,2,1,0:T(8,128)(2,1)}), bf16[4,2,128,1024]{3,2,1,0:T(8,128)(2,1)}, u32[]{:S(2)}, u32[]{:S(2)}) async-start(bf16[4,2,128,1024]{3,2,1,0:T(8,128)(2,1)} %copy-done.5), calls=%async_computation.3 | async-start | bytes 4194304 | tf_op jit(solution)/shard_map/all_to_all | solution.py:362
  174.8 26.6 %copy-start.10 = (bf16[1,1,256,1024]{3,2,1,0:T(8,128)(2,1)S(1)}, bf16[1,1,256,1024]{3,2,1,0:T(8,128)(2,1)}, u32[]{:S(2)}) copy-start(bf16[1,1,256,1024]{3,2,1,0:T(8,128)(2,1)} %copy-done.9) | copy-start | bytes 1572868
  175.0 15.1 %collective-permute-start.8 = (bf16[1,1,256,1024]{3,2,1,0:T(8,128)(2,1)S(1)}, bf16[1,1,256,1024]{3,2,1,0:T(8,128)(2,1)S(1)}, u32[]{:S(2)}, u32[]{:S(2)}) collective-permute-start(bf16[1,1,256,1024]{3,2,1,0:T(8,128)(2,1)S(1)} %get-tuple-element.34), channel_id=1, source_target_pairs={{0,16},{8,24},{16,0},{24,8},{1,17},{9,25},{17,1},{25,9},{2,18},{10... | collective-permute-start | bytes 1572872 | tf_op jit(solution)/shard_map/ppermute | solution.py:377
  177.4 23.9 %collective-permute-start.6 = (bf16[1,1,256,1024]{3,2,1,0:T(8,128)(2,1)S(1)}, bf16[1,1,256,1024]{3,2,1,0:T(8,128)(2,1)S(1)}, u32[]{:S(2)}, u32[]{:S(2)}) collective-permute-start(bf16[1,1,256,1024]{3,2,1,0:T(8,128)(2,1)S(1)} %copy-done.13), channel_id=1, source_target_pairs={{0,16},{8,24},{16,0},{24,8},{1,17},{9,25},{17,1},{25,9},{2,18},{10... | collective-permute-start | bytes 1572872 | tf_op jit(solution)/shard_map/ppermute | solution.py:377
  178.2 52.1 %collective-permute-start.5 = (bf16[2,1,256,1024]{3,2,0,1:T(8,128)(2,1)}, bf16[2,1,256,1024]{3,2,0,1:T(8,128)(2,1)}, u32[]{:S(2)}, u32[]{:S(2)}) collective-permute-start(bf16[2,1,256,1024]{3,2,0,1:T(8,128)(2,1)} %bitcast.12), channel_id=1, source_target_pairs={{0,16},{8,24},{16,0},{24,8},{1,17},{9,25},{17,1},{25,9},{2,18},{10... | collective-permute-start | bytes 3145736 | tf_op jit(solution)/shard_map/ppermute | solution.py:377
  191.1 39.1 %collective-permute-start.9 = (bf16[1,256,1024]{2,1,0:T(8,128)(2,1)}, bf16[1,256,1024]{2,1,0:T(8,128)(2,1)}, u32[]{:S(2)}, u32[]{:S(2)}) collective-permute-start(bf16[1,256,1024]{2,1,0:T(8,128)(2,1)} %fusion.1), channel_id=1, source_target_pairs={{0,4},{1,5},{2,6},{3,7},{4,0},{5,1},{6,2},{7,3},{8,12},{9,13},{10,... | collective-permute-start | bytes 1572872 | tf_op jit(solution)/shard_map/ppermute | solution.py:368
  202.4 37.5 %collective-permute-start.7 = (bf16[1,256,1024]{2,1,0:T(8,128)(2,1)}, bf16[1,256,1024]{2,1,0:T(8,128)(2,1)}, u32[]{:S(2)}, u32[]{:S(2)}) collective-permute-start(bf16[1,256,1024]{2,1,0:T(8,128)(2,1)} %fusion), channel_id=1, source_target_pairs={{0,4},{1,5},{2,6},{3,7},{4,0},{5,1},{6,2},{7,3},{8,12},{9,13},{10,... | collective-permute-start | bytes 1572872 | tf_op jit(solution)/shard_map/ppermute | solution.py:368
  (11 other events, 16.6 us)
Sparse Core Ops, SparseCore 0:
  9.6 39.6 all-gather.2
  89.7 47.2 all-gather.4

commit v6 on v5

--- a/solution.py
+++ b/solution.py
@@ -17,7 +17,7 @@
 
 
 def sigmoid(x):
-    return 1.0 / (1.0 + jnp.exp(-x))
+    return 0.5 + 0.5 * jnp.tanh(0.5 * x)
 
 
 def resident(shape):
@@ -26,18 +26,20 @@
 
 def pick_kernel(ids_ref, rows_ref, out_ref):
     count, total = out_ref.shape[0], rows_ref.shape[0]
-    places = lax.broadcasted_iota(jnp.int32, (count, total), 1)
+    places = lax.broadcasted_iota(jnp.int32, (total, count), 0)
     ones = jnp.where(places == ids_ref[...], 1.0, 0.0).astype(BF16)
-    out_ref[...] = jnp.dot(ones, rows_ref[...], preferred_element_type=F32).astype(BF16)
+    out_ref[...] = lax.dot_general(
+        ones, rows_ref[...], (((0,), (0,)), ((), ())), preferred_element_type=F32
+    ).astype(BF16)
 
 
 def pick_rows(rows, ids):
     return pl.pallas_call(
         pick_kernel,
-        out_shape=jax.ShapeDtypeStruct((ids.shape[0], rows.shape[1]), rows.dtype),
-        compiler_params=pltpu.CompilerParams(vmem_limit_bytes=VMEM),
+        out_shape=jax.ShapeDtypeStruct((ids.shape[1], rows.shape[1]), rows.dtype),
+        compiler_params=pltpu.CompilerParams(vmem_limit_bytes=16 * MB),
         name="pick_rows",
-    )(ids[:, None], rows)
+    )(ids, rows)
 
 
 def block_source(info_ref, dataset, rank):
@@ -60,6 +62,19 @@
             for a, b in zip(arrays[::2], arrays[1::2])
         ]
     return arrays[0]
+
+
+def turn(arrays):
+    rows = lax.broadcasted_iota(jnp.int32, arrays[0].shape, 0)
+    arrays = list(arrays)
+    for shift in (1, 2, 4):
+        low = (rows & shift) == 0
+        for at in range(8):
+            if at & shift == 0:
+                a, b = arrays[at], arrays[at + shift]
+                arrays[at] = jnp.where(low, a, pltpu.roll(b, shift, 0))
+                arrays[at + shift] = jnp.where(low, pltpu.roll(a, 8 - shift, 0), b)
+    return arrays
 
 
 def encode_kernel(
@@ -80,19 +95,27 @@
         pl.when(slot < sets)(lambda: one(own_ref, slot))
         pl.when(slot >= sets)(lambda: one(mirror_ref, slot - sets))
 
-    def spread(ref, at, base):
-        for k in range(tall):
-            lanes = slice(k * LANES, (k + 1) * LANES)
-            value = ref[pl.ds(at, BLOCK), lanes].astype(F32)
-            place = pl.ds(base * tall + k, BLOCK, stride=tall)
-            plain[place, :] = value
-            gained[place, :] = value * gain_ref[:, lanes]
-
-    for at in range(0, rows, BLOCK):
-        spread(atoms_ref, at, at)
-    for at in range(0, depth, BLOCK):
-        spread(low_ref, at, rows + at)
-        spread(high_ref, at, rows + depth + at)
+    def spread(ref, base):
+        def one(group, carry):
+            at = pl.multiple_of(group * 16, 16)
+            for k in range(0, tall, 8):
+                gains = gain_ref[k : k + 8, :]
+                parts = [
+                    ref[pl.ds(at, 16), (k + j) * LANES : (k + j + 1) * LANES].astype(F32)
+                    for j in range(8)
+                ]
+                for side in (0, 8):
+                    for i, row in enumerate(turn([part[side : side + 8] for part in parts])):
+                        place = pl.multiple_of((base + at + side + i) * tall + k, 8)
+                        plain[pl.ds(place, 8), :] = row
+                        gained[pl.ds(place, 8), :] = row * gains
+            return carry
+
+        lax.fori_loop(0, ref.shape[0] // 16, one, 0)
+
+    spread(atoms_ref, 0)
+    spread(low_ref, rows)
+    spread(high_ref, rows + depth)
 
     def row_of(ref, place):
         return ref[pl.ds(pl.multiple_of(place, tall), tall), :]
@@ -168,7 +191,7 @@
                 resident((depth, width)),
                 resident((depth, width)),
                 resident((width, width)),
-                resident((1, width)),
+                resident((tall, LANES)),
                 resident((rows, bond_count)),
             ],
             out_specs=[pl.BlockSpec(memory_space=pltpu.HBM)] * 2,
@@ -193,115 +216,163 @@
     return [rows.reshape(half, 2, BLOCK, width) for rows in blocks]
 
 
-def head_kernel(sizes, scale, table_ref, rows_ref, *refs):
-    pieces = refs[: len(sizes)]
-    back_ref, send_ref, keep_ref, weights, totals, sems = refs[len(sizes) :]
-    width = rows_ref.shape[-1]
-    shape = rows_ref.shape
+def head_kernel(
+    scale, bit_ref, rows_ref, weights_ref, back_ref, send_ref, keep_ref,
+    x, weights, act, slope, err, grad, back, shares, in_sems, weight_sems, back_sems, share_sems,
+):
+    width = x.shape[-1]
+    tile = x.shape[1] * x.shape[2]
     count = weights.shape[1]
-    first = jnp.logical_and(pl.program_id(0) == 0, pl.program_id(1) == 0)
-    last = jnp.logical_and(
-        pl.program_id(0) == pl.num_programs(0) - 1, pl.program_id(1) == pl.num_programs(1) - 1
-    )
-
-    def loads(act):
-        shard = 0
-        for ref, size in zip(pieces, sizes):
-            for i in range(size):
-                for layer in range(2):
-                    place = weights.at[layer, table_ref[shard]]
-                    act(pltpu.make_async_copy(ref.at[i, layer], place, sems.at[layer, shard]))
-                shard += 1
-
-    @pl.when(first)
+    chunk = width // 4
+    chunks = [slice(at, at + chunk) for at in range(0, width, chunk)]
+    transposed = (((1,), (1,)), ((), ()))
+    over_rows = (((0,), (0,)), ((), ()))
+    bit = bit_ref[0]
+
+    def rows_in(rank):
+        return pltpu.make_async_copy(rows_ref.at[:, rank], x.at[rank], in_sems.at[rank])
+
+    def weights_in(layer):
+        return [
+            pltpu.make_async_copy(
+                weights_ref.at[i, layer], weights.at[layer, i], weight_sems.at[layer, i]
+            )
+            for i in range(count)
+        ]
+
+    def back_out(rank):
+        return pltpu.make_async_copy(back.at[rank], back_ref.at[:, rank], back_sems.at[rank])
+
+    def shares_out(layer):
+        copies = []
+        for j in range(count // 2):
+            for ref, at in ((keep_ref, 2 * j + bit), (send_ref, 2 * j + 1 - bit)):
+                copies.append(
+                    pltpu.make_async_copy(
+                        shares.at[layer, at], ref.at[layer, j],
+                        share_sems.at[layer, len(copies)],
+                    )
+                )
+        return copies
+
+    def matrix(layer):
+        return weights[layer].reshape(width, width)
+
+    def forward(rank, wait):
+        inputs = x[rank].reshape(tile, width)
+        low = matrix(0)
+        for at in chunks:
+            z = jnp.dot(inputs, low[:, at], preferred_element_type=F32)
+            s = sigmoid(z)
+            act[rank * tile : (rank + 1) * tile, at] = (z * s).astype(BF16)
+            slope[rank, :, at] = s * (1.0 + z * (1.0 - s))
+        if wait:
+            for copy in weights_in(1):
+                copy.wait()
+        acts = act[rank * tile : (rank + 1) * tile, :]
+        high = matrix(1)
+        for at in chunks:
+            value = jnp.dot(acts, high[:, at], preferred_element_type=F32)
+            value = value - inputs[:, at].astype(F32)
+            err[rank, :, at] = value
+            grad[1, rank * tile : (rank + 1) * tile, at] = value.astype(BF16)
+
+    def backward(rank):
+        rows = slice(rank * tile, (rank + 1) * tile)
+        grads = grad[1, rows, :]
+        high = matrix(1)
+        for at in chunks:
+            up = lax.dot_general(grads, high[at, :], transposed, preferred_element_type=F32)
+            grad[0, rows, at] = (up * slope[rank, :, at]).astype(BF16)
+        grads = grad[0, rows, :]
+        low = matrix(0)
+        shape = x.shape[1:3] + (chunk,)
+        for at in chunks:
+            up = lax.dot_general(grads, low[at, :], transposed, preferred_element_type=F32)
+            back[rank, :, :, at] = (up - err[rank, :, at]).astype(BF16).reshape(shape)
+
+    def share(layer, acts, rows):
+        value = lax.dot_general(
+            acts, grad[layer, :rows, :], over_rows, preferred_element_type=F32
+        )
+        shares[layer] = (value * scale).astype(BF16).reshape(shares.shape[1:])
+
+    for rank in range(2):
+        rows_in(rank).start()
+    for layer in range(2):
+        for copy in weights_in(layer):
+            copy.start()
+    rows_in(0).wait()
+    for copy in weights_in(0):
+        copy.wait()
+    forward(0, True)
+    rows_in(1).wait()
+    some = jnp.max(jnp.abs(x[1].reshape(tile, width).astype(F32))) > 0
+    none = jnp.logical_not(some)
+    pl.when(some)(lambda: forward(1, False))
+    pl.when(some)(lambda: share(1, act[...], 2 * tile))
+    pl.when(none)(lambda: share(1, act[:tile, :], tile))
+    for copy in shares_out(1):
+        copy.start()
+    backward(0)
+    back_out(0).start()
+    pl.when(some)(lambda: backward(1))
+
+    @pl.when(none)
     def _():
-        loads(lambda copy: copy.start())
-        loads(lambda copy: copy.wait())
-
-    x = rows_ref[...].reshape(-1, width)
-    some = jnp.logical_or(first, jnp.max(jnp.abs(x.astype(F32))) > 0)
-
-    @pl.when(some)
-    def _():
-        low = weights[0].reshape(width, width)
-        high = weights[1].reshape(width, width)
-        transposed = (((1,), (1,)), ((), ()))
-        over_rows = (((0,), (0,)), ((), ()))
-
-        def add(layer, acts, grads):
-            value = lax.dot_general(acts, grads, over_rows, preferred_element_type=F32)
-            value = value.reshape(totals.shape[1:])
-
-            @pl.when(first)
-            def _():
-                totals[layer] = value
-
-            @pl.when(jnp.logical_not(first))
-            def _():
-                totals[layer] += value
-
-        z = jnp.dot(x, low, preferred_element_type=F32)
-        s = sigmoid(z)
-        act = (z * s).astype(BF16)
-        slope = s * (1.0 + z * (1.0 - s))
-        err = jnp.dot(act, high, preferred_element_type=F32) - x.astype(F32)
-        grad = err.astype(BF16)
-        add(1, act, grad)
-        up = lax.dot_general(grad, high, transposed, preferred_element_type=F32)
-        grad = (up * slope).astype(BF16)
-        add(0, x, grad)
-        up = lax.dot_general(grad, low, transposed, preferred_element_type=F32)
-        back_ref[...] = (up - err).astype(BF16).reshape(shape)
-
-    @pl.when(jnp.logical_not(some))
-    def _():
-        back_ref[...] = jnp.zeros_like(back_ref)
-
-    @pl.when(last)
-    def _():
-        bit = table_ref[count]
-        for layer in range(2):
-            for j in range(count // 2):
-                keep_ref[layer, j] = (totals[layer, 2 * j + bit] * scale).astype(BF16)
-                send_ref[layer, j] = (totals[layer, 2 * j + 1 - bit] * scale).astype(BF16)
-
-
-def run_head(rows, pieces, places, scale, name):
+        back[1] = jnp.zeros(back.shape[1:], BF16)
+
+    back_out(1).start()
+    pl.when(some)(lambda: share(0, x[...].reshape(2 * tile, width), 2 * tile))
+    pl.when(none)(lambda: share(0, x[0].reshape(tile, width), tile))
+    for copy in shares_out(0):
+        copy.start()
+    for rank in range(2):
+        back_out(rank).wait()
+    for layer in range(2):
+        for copy in shares_out(layer):
+            copy.wait()
+
+
+def run_head(rows, weights, scale, name):
     sources, ranks, _, width = rows.shape
-    count = lax.axis_size("dom")
-    depth = width // count
-    tile = 4 if sources % 4 == 0 else 1
-    block = pl.BlockSpec((tile, 1, BLOCK, width), lambda r, t, *_: (t, r, 0, 0))
-    total = sources * ranks * BLOCK
-    sizes = [piece.shape[0] for piece in pieces]
-    part = (2, count // 2, depth, width)
+    count, layers, depth, _ = weights.shape
+    tile = sources * BLOCK
+    total = ranks * tile
+    part = (layers, count // 2, depth, width)
     bit = lax.axis_index("dom").astype(jnp.int32) & 1
+    in_hbm = pl.BlockSpec(memory_space=pltpu.HBM)
     return pl.pallas_call(
-        functools.partial(head_kernel, sizes, scale),
+        functools.partial(head_kernel, scale),
         grid_spec=pltpu.PrefetchScalarGridSpec(
             num_scalar_prefetch=1,
-            grid=(ranks, sources // tile),
-            in_specs=[block] + [pl.BlockSpec(memory_space=pltpu.HBM)] * len(pieces),
-            out_specs=[block, resident(part), resident(part)],
+            grid=(1,),
+            in_specs=[in_hbm] * 2,
+            out_specs=[in_hbm] * 3,
             scratch_shapes=[
-                pltpu.VMEM((2, count, depth, width), BF16),
-                pltpu.VMEM((2, count, depth, width), F32),
-                pltpu.SemaphoreType.DMA((2, count)),
+                pltpu.VMEM((ranks, sources, BLOCK, width), BF16),
+                pltpu.VMEM((layers, count, depth, width), BF16),
+                pltpu.VMEM((total, width), BF16),
+                pltpu.VMEM((ranks, tile, width), F32),
+                pltpu.VMEM((ranks, tile, width), F32),
+                pltpu.VMEM((layers, total, width), BF16),
+                pltpu.VMEM((ranks, sources, BLOCK, width), BF16),
+                pltpu.VMEM((layers, count, depth, width), BF16),
+                pltpu.SemaphoreType.DMA((ranks,)),
+                pltpu.SemaphoreType.DMA((layers, count)),
+                pltpu.SemaphoreType.DMA((ranks,)),
+                pltpu.SemaphoreType.DMA((layers, count)),
             ],
         ),
-        out_shape=[
-            jax.ShapeDtypeStruct(rows.shape, BF16),
-            jax.ShapeDtypeStruct(part, BF16),
-            jax.ShapeDtypeStruct(part, BF16),
-        ],
-        compiler_params=pltpu.CompilerParams(vmem_limit_bytes=44 * MB),
+        out_shape=[pltpu.HBM(rows.shape, BF16), pltpu.HBM(part, BF16), pltpu.HBM(part, BF16)],
+        compiler_params=pltpu.CompilerParams(vmem_limit_bytes=VMEM),
         cost_estimate=pl.CostEstimate(
             flops=24 * total * width * width,
             bytes_accessed=5 * total * width * 2 + width * width * 4,
             transcendentals=total * width,
         ),
         name=name,
-    )(jnp.stack(places + [bit]).astype(jnp.int32), rows, *pieces)
+    )(bit.reshape(1), rows, weights)
 
 
 def block_place(info_ref, block):
@@ -400,7 +471,7 @@
             out_specs=[resident(shape)] * 2,
         ),
         out_shape=[jax.ShapeDtypeStruct(shape, BF16)] * 2,
-        compiler_params=pltpu.CompilerParams(vmem_limit_bytes=20 * MB),
+        compiler_params=pltpu.CompilerParams(vmem_limit_bytes=VMEM),
         name="merge_shares",
     )(mine.reshape(1), keep, got)
 
@@ -414,28 +485,33 @@
     return keep[:, 0], got[:, 0], send
 
 
-def total_kernel(*refs):
-    *terms, out_ref = refs
-    for layer in range(out_ref.shape[0]):
-        acc = None
-        for ref, at in terms_of(terms, layer):
-            value = ref[at].astype(F32)
-            acc = value if acc is None else acc + value
-        out_ref[layer] = acc
-
-
-def terms_of(terms, layer):
-    keep, got, low, high = terms
-    return [(keep, layer), (got, layer), ((low, high)[layer], 0)]
-
-
-def total(keep, got, low, high):
+def total_kernel(layer, keep_ref, got_ref, far_ref, out_ref):
+    total = keep_ref[0].astype(F32) + got_ref[0].astype(F32) + far_ref[0].astype(F32)
+    out_ref[0] = total
+
+
+def total(keep, got, far, layer, out=None):
+    layers, depth, width = keep.shape
+    tile = depth // 4
+    mine = pl.BlockSpec((1, tile, width), lambda t: (layer, t, 0))
+    came = pl.BlockSpec((1, tile, width), lambda t: (0, t, 0))
+    operands = [keep, got, far]
+    specs = [mine, mine, came]
+    kernel = functools.partial(total_kernel, layer)
+    if out is not None:
+        operands.append(out)
+        specs.append(pl.BlockSpec(memory_space=pl.ANY))
+        kernel = lambda a, b, c, _, o: total_kernel(layer, a, b, c, o)
     return pl.pallas_call(
-        total_kernel,
+        kernel,
+        grid=(4,),
+        in_specs=specs,
+        out_specs=mine,
         out_shape=jax.ShapeDtypeStruct(keep.shape, F32),
-        compiler_params=pltpu.CompilerParams(vmem_limit_bytes=20 * MB),
-        name="total_shares",
-    )(keep, got, low, high)
+        input_output_aliases={} if out is None else {3: 0},
+        compiler_params=pltpu.CompilerParams(vmem_limit_bytes=VMEM),
+        name="total_share",
+    )(*operands)
 
 
 def body(atoms, bonds, triplets, halo_ids, counts, enc_weight, gate_gain, head_weight):
@@ -449,33 +525,34 @@
     count = lax.axis_size("dom")
     own_weights = lax.all_gather(shard, "dom", axis=0, tiled=False)
     far = across(head_weight, half)
-    low, high = halo(pick_rows(atom_rows, halo_ids[0]))
+    low, high = halo(pick_rows(atom_rows, halo_ids))
     codes = ((bonds[0] * tall) * 65536 + triplets[0] * tall).reshape(-1)
     place = lax.axis_index("head").astype(jnp.int32).reshape(1, 1)
     info = jnp.concatenate([counts, place], axis=1)
     own_blocks, mirror_blocks = encode(
-        info, codes, atom_rows, low, high, enc_weight, gate_gain[None, :], bonds[0].T, half
+        info, codes, atom_rows, low, high, enc_weight, gate_gain.reshape(tall, LANES),
+        bonds[0].T, half
     )
-    own_rows = exchange(own_blocks, half)
+    own_rows = exchange(after(own_blocks, far), half)
     mirror_rows = exchange(mirror_blocks, half)
     mirror_weights = lax.all_gather(far[0], "dom", axis=0, tiled=False)
 
     scale = 1.0 / math.sqrt(count * row_count)
-    orders = [jnp.int32(i) for i in range(count)]
-    back, send, keep = run_head(own_rows, [own_weights], orders, scale, "head_own")
+    back, own_send, own_keep = run_head(own_rows, own_weights, scale, "head_own")
     own_back = exchange(back, half)
-    own_keep, own_got, own_sent = sum_over_dom(send, keep, swap(send, 0), 0, 2)
-
-    mirror_rows = after(mirror_rows, own_sent)
-    back, send, keep = run_head(mirror_rows, [mirror_weights], orders, scale, "head_mirror")
+    own_got = swap(own_send, 0)
+
+    back, send, keep = run_head(mirror_rows, mirror_weights, scale, "head_mirror")
     got = swap(send, 0)
     high_keep, high_got, high_sent = sum_over_dom(send, keep, got, 1, 1)
     low_keep, low_got, low_sent = sum_over_dom(send, keep, got, 0, 1)
-    mirror_back = exchange(after(back, high_got, low_sent), half)
+    mirror_back = exchange(after(back, low_got), half)
     high_part = across((high_keep.astype(F32) + high_got.astype(F32)).astype(BF16), half)
     low_part = across((low_keep.astype(F32) + low_got.astype(F32)).astype(BF16), half)
+    own_keep, own_got, _ = sum_over_dom(own_send, after(own_keep, low_got), own_got, 0, 2)
     row_part = place_rows(info, own_back, mirror_back, row_blocks)
-    head_part = total(own_keep, own_got, low_part, after(high_part, row_part))
+    head_part = total(own_keep, own_got, after(high_part, row_part), 1)
+    head_part = total(own_keep, own_got, after(low_part, head_part), 0, head_part)
     return row_part.reshape(1, row_count, width), head_part[None]
 
 

time: 252 us -> 250 us (level)
  Pallas kernels: 66.9 us -> 79.2 us
  local copies, waits for them, and re-layouts: 15.4 us -> 8.56 us
  starting transfers between devices: 44 us -> 37.2 us
    all_to_all x4, waiting for transfers between devices: 12 us -> 40.5 us  [exchange(): lax.all_to_all(blocks, 'head', split_axis=0, concat_axis=0, axis_index_gr...]
    ppermute x3, waiting for transfers between devices: 62.6 us -> 39.4 us  [across(): lax.ppermute(array, 'head', [(i, (i + half) % (2 * half)) for i in range(...]
    ppermute x5, starting transfers between devices: 13.9 us -> 3.55 us  [swap(): return lax.ppermute(array, 'dom', [(i, i ^ 1 << bit) for i in range(count)])]
    pallas_call x3, Pallas kernels: 1.86 us -> 9.38 us  [merge(): pl.pallas_call(merge_kernel, grid_spec=pltpu.PrefetchScalarGridSpec(num_s...]
    pallas_call x4 -> x5, Pallas kernels: 32.9 us -> 38.9 us  [the longest x2 31.3 us: run_head(): pl.pallas_call(functools.partial(head_kernel, scale), grid_spec=pltpu.Pre...]
    unnamed x40 -> x30, local copies, waits for them, and re-layouts: 13.9 us -> 8.56 us
    all_to_all x4, starting transfers between devices: 16.7 us -> 21.8 us  [exchange(): lax.all_to_all(blocks, 'head', split_axis=0, concat_axis=0, axis_index_gr...]
    ppermute x1, waiting for transfers between devices: 4.09 us -> 0.41 us  [halo(): high = lax.ppermute(cut_rows, 'dom', backward)]
  transfers between devices with their start and end apart: 16 -> 16, of which waited for: 11 -> 10; matrix products, arithmetic and copies ran while one was open for 2% -> 1% of each run, Pallas kernels for 25% -> 30%
where the time goes in v6:
time: 250 us; the launch traced here: 249 us
  waiting for transfers between devices  108 us (43%)
  Pallas kernels  79.2 us (32%)
  starting transfers between devices  37.2 us (15%)
  between operations  14.2 us (6%)
  local copies, waits for them, and re-layouts  8.56 us (3%)
    all_to_all x4, waiting for transfers between devices, exchange(): lax.all_to_all(blocks, 'head', split_axis=0, concat_axis=0, axis_index_gr...  40.5 us
    ppermute x3, waiting for transfers between devices, across(): lax.ppermute(array, 'head', [(i, (i + half) % (2 * half)) for i in range(...  39.4 us
    pallas_call x2, Pallas kernels, run_head(): pl.pallas_call(functools.partial(head_kernel, scale), grid_spec=pltpu.Pre...  31.3 us
    ppermute x5, waiting for transfers between devices, swap(): return lax.ppermute(array, 'dom', [(i, i ^ 1 << bit) for i in range(count)])  26.2 us
    pallas_call x1, Pallas kernels, encode(): pl.pallas_call(functools.partial(encode_kernel, half), grid_spec=pltpu.Pr...  25 us
    all_to_all x4, starting transfers between devices, exchange(): lax.all_to_all(blocks, 'head', split_axis=0, concat_axis=0, axis_index_gr...  21.8 us
    pallas_call x3, Pallas kernels, merge(): pl.pallas_call(merge_kernel, grid_spec=pltpu.PrefetchScalarGridSpec(num_s...  9.38 us
    unnamed x30, local copies, waits for them, and re-layouts  8.56 us
  transfers between devices with their start and end apart: 16, of which 10 were waited for; matrix products, arithmetic and copies ran while one was open for 1% of the time, Pallas kernels for 30%

profile of v6, /device:TPU:0, one launch (start us, length us, event | category | flops | bytes accessed | tf_op | source)
XLA Modules:
  0.0 249.2 jit_solution(6969353418088677077)
XLA Ops:
  14.5 3.5 %collective-permute-start.2 = (bf16[1,2,256,1024]{3,2,1,0:T(8,128)(2,1)}, bf16[1,2,256,1024]{3,2,1,0:T(8,128)(2,1)}, u32[]{:S(2)}, u32[]{:S(2)}) collective-permute-start(bf16[1,2,256,1024]{3,2,1,0:T(8,128)(2,1)} %param.15), channel_id=1, source_target_pairs={{0,4},{1,5},{2,6},{3,7},{4,0},{5,1},{6,2},{7,3},{8,12},{9,13},{10,... | collective-permute-start | bytes 3145736 | tf_op jit(solution)/shard_map/ppermute | solution.py:439
  20.6 25.0 %encode_rows.1 = (bf16[8,128,1024]{2,1,0:T(8,128)(2,1)}, bf16[8,128,1024]{2,1,0:T(8,128)(2,1)}) custom-call(s32[1,9]{1,0:T(1,128)S(1)} %pad_add_fusion.info_ref, s32[4096]{0:T(1024)S(1)} %bitcast.30, bf16[1024,1024]{1,0:T(8,128)(2,1)S(1)} %bitcast.28, bf16[128,1024]{1,0:T(8,128)(2,1)S(1)} %collective-permute-done.low_ref, ...), custom_call_target="tpu_custom_call" | custom-call | flops 42949672960 | bytes 31457280 | tf_op jit(solution)/shard_map/encode_rows/pallas_call | solution.py:184
  45.5 17.7 %collective-permute-done.2 = bf16[1,2,256,1024]{3,2,1,0:T(8,128)(2,1)} collective-permute-done((bf16[1,2,256,1024]{3,2,1,0:T(8,128)(2,1)}, bf16[1,2,256,1024]{3,2,1,0:T(8,128)(2,1)}, u32[]{:S(2)}, u32[]{:S(2)}) %collective-permute-start.2) | collective-permute-done | bytes 1048608 | tf_op jit(solution)/shard_map/ppermute | solution.py:439
  63.2 4.6 %all-to-all-start = ((bf16[4,2,128,1024]{3,2,1,0:T(8,128)(2,1)}), bf16[4,2,128,1024]{3,2,1,0:T(8,128)(2,1)S(1)}, u32[]{:S(2)}, u32[]{:S(2)}) async-start(bf16[4,2,128,1024]{3,2,1,0:T(8,128)(2,1)} %bitcast.36), calls=%async_computation | async-start | bytes 4194304 | tf_op jit(solution)/shard_map/all_to_all | solution.py:433
  68.6 24.9 %all-to-all-done.rows_ref = bf16[4,2,128,1024]{3,2,1,0:T(8,128)(2,1)S(1)} async-done(((bf16[4,2,128,1024]{3,2,1,0:T(8,128)(2,1)}), bf16[4,2,128,1024]{3,2,1,0:T(8,128)(2,1)S(1)}, u32[]{:S(2)}, u32[]{:S(2)}) %all-to-all-start) | async-done | bytes 2097184 | tf_op jit(solution)/shard_map/all_to_all | solution.py:433
  94.8 3.6 %all-to-all-start.2 = ((bf16[4,2,128,1024]{3,2,1,0:T(8,128)(2,1)}), bf16[4,2,128,1024]{3,2,1,0:T(8,128)(2,1)S(1)}, u32[]{:S(2)}, u32[]{:S(2)}) async-start(bf16[4,2,128,1024]{3,2,1,0:T(8,128)(2,1)} %bitcast.7), calls=%async_computation.2 | async-start | bytes 4194304 | tf_op jit(solution)/shard_map/all_to_all | solution.py:433
  98.5 19.1 %head_own.1 = (bf16[4,2,128,1024]{3,2,1,0:T(8,128)(2,1)}, bf16[2,2,256,1024]{3,2,1,0:T(8,128)(2,1)}, bf16[2,2,256,1024]{3,2,1,0:T(8,128)(2,1)}) custom-call(s32[1]{0:T(128)} %bitcast.1.bit_ref, bf16[4,2,128,1024]{3,2,1,0:T(8,128)(2,1)} %copy-done.6, bf16[4,2,256,1024]{3,2,1,0:T(8,128)(2,1)} %all-gather.3.cloned.1.call-done.weights_ref), custom_call_target="tpu_custom_call" | custom-call | flops 25769803776 | bytes 14680064 | tf_op jit(solution)/shard_map/head_own/pallas_call | solution.py:345
  117.6 5.9 %all-to-all-done.2.rows_ref = bf16[4,2,128,1024]{3,2,1,0:T(8,128)(2,1)S(1)} async-done(((bf16[4,2,128,1024]{3,2,1,0:T(8,128)(2,1)}), bf16[4,2,128,1024]{3,2,1,0:T(8,128)(2,1)S(1)}, u32[]{:S(2)}, u32[]{:S(2)}) %all-to-all-start.2) | async-done | bytes 2097184 | tf_op jit(solution)/shard_map/all_to_all | solution.py:433
  124.8 3.6 %all-to-all-start.1 = ((bf16[4,2,128,1024]{3,2,1,0:T(8,128)(2,1)}), bf16[4,2,128,1024]{3,2,1,0:T(8,128)(2,1)S(1)}, u32[]{:S(2)}, u32[]{:S(2)}) async-start(bf16[4,2,128,1024]{3,2,1,0:T(8,128)(2,1)} %get-tuple-element.23), calls=%async_computation.1 | async-start | bytes 4194304 | tf_op jit(solution)/shard_map/all_to_all | solution.py:433
  128.4 12.2 %head_mirror.1 = (bf16[4,2,128,1024]{3,2,1,0:T(8,128)(2,1)}, bf16[2,2,256,1024]{3,2,1,0:T(8,128)(2,1)}, bf16[2,2,256,1024]{3,2,1,0:T(8,128)(2,1)}) custom-call(s32[1]{0:T(128)} %bitcast.1.bit_ref, bf16[4,2,128,1024]{3,2,1,0:T(8,128)(2,1)} %copy-done.5, bf16[4,2,256,1024]{3,2,1,0:T(8,128)(2,1)} %all-gather.5.cloned.1.call-done.weights_ref), custom_call_target="tpu_custom_call" | custom-call | flops 25769803776 | bytes 14680064 | tf_op jit(solution)/shard_map/head_mirror/pallas_call | solution.py:345
  140.7 4.5 %collective-permute-done.3.got_ref = bf16[2,2,256,1024]{3,2,1,0:T(8,128)(2,1)} collective-permute-done((bf16[2,2,256,1024]{3,2,1,0:T(8,128)(2,1)}, bf16[2,2,256,1024]{3,2,1,0:T(8,128)(2,1)}, u32[]{:S(2)}, u32[]{:S(2)}) %collective-permute-start.3) | collective-permute-done | bytes 2097184 | tf_op jit(solution)/shard_map/ppermute | solution.py:448
  145.1 2.7 %merge_shares.3 = (bf16[1,1,256,1024]{3,2,1,0:T(8,128)(2,1)}, bf16[1,1,256,1024]{3,2,1,0:T(8,128)(2,1)}) custom-call(s32[1]{0:T(128)} %bitcast.8.bit_ref, bf16[2,2,256,1024]{3,2,1,0:T(8,128)(2,1)} %get-tuple-element.26.keep_ref, bf16[2,2,256,1024]{3,2,1,0:T(8,128)(2,1)} %collective-permute-done.3.got_ref), custom_call_target="tpu_custom_call" | custom-call | tf_op jit(solution)/shard_map/merge_shares/pallas_call | solution.py:465
  149.3 12.7 %collective-permute-done.4 = bf16[1,1,256,1024]{3,2,1,0:T(8,128)(2,1)S(1)} collective-permute-done((bf16[1,1,256,1024]{3,2,1,0:T(8,128)(2,1)}, bf16[1,1,256,1024]{3,2,1,0:T(8,128)(2,1)S(1)}, u32[]{:S(2)}, u32[]{:S(2)}) %collective-permute-start.4) | collective-permute-done | bytes 524320 | tf_op jit(solution)/shard_map/ppermute | solution.py:448
  162.0 10.0 %all-to-all-start.3 = ((bf16[4,2,128,1024]{3,2,1,0:T(8,128)(2,1)}), bf16[4,2,128,1024]{3,2,1,0:T(8,128)(2,1)}, u32[]{:S(2)}, u32[]{:S(2)}) async-start(bf16[4,2,128,1024]{3,2,1,0:T(8,128)(2,1)} %get-tuple-element.29), calls=%async_computation.3 | async-start | bytes 4194304 | tf_op jit(solution)/shard_map/all_to_all | solution.py:433
  172.0 2.7 %merge_shares.5 = (bf16[1,1,256,1024]{3,2,1,0:T(8,128)(2,1)}, bf16[1,1,256,1024]{3,2,1,0:T(8,128)(2,1)}) custom-call(s32[1]{0:T(128)} %bitcast.8.bit_ref, bf16[2,2,256,1024]{3,2,1,0:T(8,128)(2,1)} %get-tuple-element.26.keep_ref, bf16[2,2,256,1024]{3,2,1,0:T(8,128)(2,1)} %collective-permute-done.3.got_ref), custom_call_target="tpu_custom_call" | custom-call | tf_op jit(solution)/shard_map/merge_shares/pallas_call | solution.py:465
  176.4 4.0 %merge_shares.4 = (bf16[2,1,256,1024]{3,2,1,0:T(8,128)(2,1)}, bf16[2,1,256,1024]{3,2,1,0:T(8,128)(2,1)}) custom-call(s32[1]{0:T(128)} %bitcast.8.bit_ref, bf16[2,2,256,1024]{3,2,1,0:T(8,128)(2,1)} %get-tuple-element.31.keep_ref, bf16[2,2,256,1024]{3,2,1,0:T(8,128)(2,1)} %collective-permute-done.5.got_ref), custom_call_target="tpu_custom_call" | custom-call | tf_op jit(solution)/shard_map/merge_shares/pallas_call | solution.py:465
  180.7 9.0 %collective-permute-done.8 = bf16[1,1,256,1024]{3,2,1,0:T(8,128)(2,1)S(1)} collective-permute-done((bf16[1,1,256,1024]{3,2,1,0:T(8,128)(2,1)}, bf16[1,1,256,1024]{3,2,1,0:T(8,128)(2,1)S(1)}, u32[]{:S(2)}, u32[]{:S(2)}) %collective-permute-start.8) | collective-permute-done | bytes 524320 | tf_op jit(solution)/shard_map/ppermute | solution.py:448
  190.7 4.5 %collective-permute-start.9 = (bf16[1,256,1024]{2,1,0:T(8,128)(2,1)}, bf16[1,256,1024]{2,1,0:T(8,128)(2,1)S(1)}, u32[]{:S(2)}, u32[]{:S(2)}) collective-permute-start(bf16[1,256,1024]{2,1,0:T(8,128)(2,1)} %fusion.1), channel_id=1, source_target_pairs={{0,4},{1,5},{2,6},{3,7},{4,0},{5,1},{6,2},{7,3},{8,12},{9,13},{10,... | collective-permute-start | bytes 1572872 | tf_op jit(solution)/shard_map/ppermute | solution.py:439
  196.2 9.7 %all-to-all-done.3.mirror_ref = bf16[4,2,128,1024]{3,2,1,0:T(8,128)(2,1)} async-done(((bf16[4,2,128,1024]{3,2,1,0:T(8,128)(2,1)}), bf16[4,2,128,1024]{3,2,1,0:T(8,128)(2,1)}, u32[]{:S(2)}, u32[]{:S(2)}) %all-to-all-start.3) | async-done | bytes 2097184 | tf_op jit(solution)/shard_map/all_to_all | solution.py:433
  205.9 6.0 %place_rows.1 = bf16[8,128,1024]{2,1,0:T(8,128)(2,1)} custom-call(s32[1,9]{1,0:T(1,128)S(1)} %pad_add_fusion.info_ref, bf16[4,2,128,1024]{3,2,1,0:T(8,128)(2,1)S(1)} %all-to-all-done.1.own_ref, bf16[4,2,128,1024]{3,2,1,0:T(8,128)(2,1)} %all-to-all-done.3.mirror_ref), custom_call_target="tpu_custom_call" | custom-call | tf_op jit(solution)/shard_map/place_rows/pallas_call | solution.py:405
  211.9 18.8 %collective-permute-done.9.far_ref = bf16[1,256,1024]{2,1,0:T(8,128)(2,1)S(1)} collective-permute-done((bf16[1,256,1024]{2,1,0:T(8,128)(2,1)}, bf16[1,256,1024]{2,1,0:T(8,128)(2,1)S(1)}, u32[]{:S(2)}, u32[]{:S(2)}) %collective-permute-start.9) | collective-permute-done | bytes 524320 | tf_op jit(solution)/shard_map/ppermute | solution.py:439
  231.5 3.6 %total_share.2._ = f32[2,256,1024]{2,1,0:T(8,128)} custom-call(bf16[2,256,1024]{2,1,0:T(8,128)(2,1)} %bitcast.33, bf16[2,256,1024]{2,1,0:T(8,128)(2,1)} %bitcast.13.got_ref.b, bf16[1,256,1024]{2,1,0:T(8,128)(2,1)} %copy-done.9), custom_call_target="tpu_custom_call" | custom-call | tf_op jit(solution)/shard_map/total_share/pallas_call | solution.py:505
  235.1 2.9 %collective-permute-done.7.c = bf16[1,256,1024]{2,1,0:T(8,128)(2,1)S(1)} collective-permute-done((bf16[1,256,1024]{2,1,0:T(8,128)(2,1)}, bf16[1,256,1024]{2,1,0:T(8,128)(2,1)S(1)}, u32[]{:S(2)}, u32[]{:S(2)}) %collective-permute-start.7) | collective-permute-done | bytes 524320 | tf_op jit(solution)/shard_map/ppermute | solution.py:439
  238.8 3.6 %total_share.3 = f32[2,256,1024]{2,1,0:T(8,128)} custom-call(bf16[2,256,1024]{2,1,0:T(8,128)(2,1)} %bitcast.34, bf16[2,256,1024]{2,1,0:T(8,128)(2,1)} %bitcast.13.got_ref.b, bf16[1,256,1024]{2,1,0:T(8,128)(2,1)} %copy-done.10, f32[2,256,1024]{2,1,0:T(8,128)} %total_share.2._), custom_call_target="tpu_custom_call", output_to_operand_aliasing={{}: (3, {})} | custom-call | tf_op jit(solution)/shard_map/total_share/pallas_call | solution.py:505
  (54 shorter events, 20.4 us)
Async XLA Ops:
  7.2 10.8 %copy-start.11 = (s32[1,4,1024]{2,1,0:T(4,128)S(1)}, s32[1,4,1024]{2,1,0:T(4,128)}, u32[]{:S(2)}) copy-start(s32[1,4,1024]{2,1,0:T(4,128)} %param.9) | copy-start | bytes 49156
  7.2 11.0 %copy-start.12 = (s32[1,4,1024]{2,1,0:T(4,128)S(1)}, s32[1,4,1024]{2,1,0:T(4,128)}, u32[]{:S(2)}) copy-start(s32[1,4,1024]{2,1,0:T(4,128)} %param.10) | copy-start | bytes 49156
  7.2 11.0 %copy-start.13 = (s32[1,8]{1,0:T(1,128)S(1)}, s32[1,8]{1,0:T(1,128)}, u32[]{:S(2)}) copy-start(s32[1,8]{1,0:T(1,128)} %param.12) | copy-start | bytes 100
  7.2 11.5 %copy-start.4 = (f32[1024]{0:T(1024)S(1)}, f32[1024]{0:T(1024)}, u32[]{:S(2)}) copy-start(f32[1024]{0:T(1024)} %param.14) | copy-start | bytes 12292
  7.2 91.3 %all-gather.3.cloned.1.call-start = ((), (), s32[]{:S(2)}) async-start(), calls=%async_computation.4 | async-start | bytes 5242880 | tf_op jit(solution)/shard_map/all_gather | solution.py:526
  10.2 8.5 %copy-start.1 = (bf16[1,1024,1024]{2,1,0:T(8,128)(2,1)S(1)}, bf16[1,1024,1024]{2,1,0:T(8,128)(2,1)}, u32[]{:S(2)}) copy-start(bf16[1,1024,1024]{2,1,0:T(8,128)(2,1)} %param.8) | copy-start | bytes 6291460
  10.7 7.7 %collective-permute-start = (bf16[128,1024]{1,0:T(8,128)(2,1)S(1)}, bf16[128,1024]{1,0:T(8,128)(2,1)S(1)}, u32[]{:S(2)}, u32[]{:S(2)}) collective-permute-start(bf16[128,1024]{1,0:T(8,128)(2,1)S(1)} %pick_rows.1), channel_id=1, source_target_pairs={{0,8},{8,16},{16,24},{1,9},{9,17},{17,25},{2,10},{10,18},{18,26},{... | collective-permute-start | bytes 786440 | tf_op jit(solution)/shard_map/ppermute | solution.py:426
  13.2 5.5 %collective-permute-start.1 = (bf16[128,1024]{1,0:T(8,128)(2,1)S(1)}, bf16[128,1024]{1,0:T(8,128)(2,1)S(1)}, u32[]{:S(2)}, u32[]{:S(2)}) collective-permute-start(bf16[128,1024]{1,0:T(8,128)(2,1)S(1)} %pick_rows.1), channel_id=1, source_target_pairs={{8,0},{16,8},{24,16},{9,1},{17,9},{25,17},{10,2},{18,10},{26,18},{... | collective-permute-start | bytes 786440 | tf_op jit(solution)/shard_map/ppermute | solution.py:427
  14.5 48.8 %collective-permute-start.2 = (bf16[1,2,256,1024]{3,2,1,0:T(8,128)(2,1)}, bf16[1,2,256,1024]{3,2,1,0:T(8,128)(2,1)}, u32[]{:S(2)}, u32[]{:S(2)}) collective-permute-start(bf16[1,2,256,1024]{3,2,1,0:T(8,128)(2,1)} %param.15), channel_id=1, source_target_pairs={{0,4},{1,5},{2,6},{3,7},{4,0},{5,1},{6,2},{7,3},{8,12},{9,13},{10,... | collective-permute-start | bytes 3145736 | tf_op jit(solution)/shard_map/ppermute | solution.py:439
  18.7 1.8 copy-start.3
  63.2 30.3 %all-to-all-start = ((bf16[4,2,128,1024]{3,2,1,0:T(8,128)(2,1)}), bf16[4,2,128,1024]{3,2,1,0:T(8,128)(2,1)S(1)}, u32[]{:S(2)}, u32[]{:S(2)}) async-start(bf16[4,2,128,1024]{3,2,1,0:T(8,128)(2,1)} %bitcast.36), calls=%async_computation | async-start | bytes 4194304 | tf_op jit(solution)/shard_map/all_to_all | solution.py:433
  67.9 60.5 %all-gather.5.cloned.1.call-start = ((), (), s32[]{:S(2)}) async-start(), calls=%async_computation.5 | async-start | bytes 5242880 | tf_op jit(solution)/shard_map/all_gather | solution.py:538
  94.8 28.6 %all-to-all-start.2 = ((bf16[4,2,128,1024]{3,2,1,0:T(8,128)(2,1)}), bf16[4,2,128,1024]{3,2,1,0:T(8,128)(2,1)S(1)}, u32[]{:S(2)}, u32[]{:S(2)}) async-start(bf16[4,2,128,1024]{3,2,1,0:T(8,128)(2,1)} %bitcast.7), calls=%async_computation.2 | async-start | bytes 4194304 | tf_op jit(solution)/shard_map/all_to_all | solution.py:433
  124.8 37.2 %all-to-all-start.1 = ((bf16[4,2,128,1024]{3,2,1,0:T(8,128)(2,1)}), bf16[4,2,128,1024]{3,2,1,0:T(8,128)(2,1)S(1)}, u32[]{:S(2)}, u32[]{:S(2)}) async-start(bf16[4,2,128,1024]{3,2,1,0:T(8,128)(2,1)} %get-tuple-element.23), calls=%async_computation.1 | async-start | bytes 4194304 | tf_op jit(solution)/shard_map/all_to_all | solution.py:433
  140.6 4.6 %collective-permute-start.3 = (bf16[2,2,256,1024]{3,2,1,0:T(8,128)(2,1)}, bf16[2,2,256,1024]{3,2,1,0:T(8,128)(2,1)}, u32[]{:S(2)}, u32[]{:S(2)}) collective-permute-start(bf16[2,2,256,1024]{3,2,1,0:T(8,128)(2,1)} %get-tuple-element.27), channel_id=1, source_target_pairs={{0,8},{8,0},{16,24},{24,16},{1,9},{9,1},{17,25},{25,17},{2,10},{10... | collective-permute-start | bytes 6291464 | tf_op jit(solution)/shard_map/ppermute | solution.py:448
  147.8 14.2 %collective-permute-start.4 = (bf16[1,1,256,1024]{3,2,1,0:T(8,128)(2,1)}, bf16[1,1,256,1024]{3,2,1,0:T(8,128)(2,1)S(1)}, u32[]{:S(2)}, u32[]{:S(2)}) collective-permute-start(bf16[1,1,256,1024]{3,2,1,0:T(8,128)(2,1)} %get-tuple-element.28), channel_id=1, source_target_pairs={{0,16},{8,24},{16,0},{24,8},{1,17},{9,25},{17,1},{25,9},{2,18},{10... | collective-permute-start | bytes 1572872 | tf_op jit(solution)/shard_map/ppermute | solution.py:448
  149.3 27.1 %collective-permute-start.5 = (bf16[2,2,256,1024]{3,2,1,0:T(8,128)(2,1)}, bf16[2,2,256,1024]{3,2,1,0:T(8,128)(2,1)}, u32[]{:S(2)}, u32[]{:S(2)}) collective-permute-start(bf16[2,2,256,1024]{3,2,1,0:T(8,128)(2,1)} %get-tuple-element.32), channel_id=1, source_target_pairs={{0,8},{8,0},{16,24},{24,16},{1,9},{9,1},{17,25},{25,17},{2,10},{10... | collective-permute-start | bytes 6291464 | tf_op jit(solution)/shard_map/ppermute | solution.py:448
  162.0 43.9 %all-to-all-start.3 = ((bf16[4,2,128,1024]{3,2,1,0:T(8,128)(2,1)}), bf16[4,2,128,1024]{3,2,1,0:T(8,128)(2,1)}, u32[]{:S(2)}, u32[]{:S(2)}) async-start(bf16[4,2,128,1024]{3,2,1,0:T(8,128)(2,1)} %get-tuple-element.29), calls=%async_computation.3 | async-start | bytes 4194304 | tf_op jit(solution)/shard_map/all_to_all | solution.py:433
  174.6 15.1 %collective-permute-start.8 = (bf16[1,1,256,1024]{3,2,1,0:T(8,128)(2,1)}, bf16[1,1,256,1024]{3,2,1,0:T(8,128)(2,1)S(1)}, u32[]{:S(2)}, u32[]{:S(2)}) collective-permute-start(bf16[1,1,256,1024]{3,2,1,0:T(8,128)(2,1)} %get-tuple-element.37), channel_id=1, source_target_pairs={{0,16},{8,24},{16,0},{24,8},{1,17},{9,25},{17,1},{25,9},{2,18},{10... | collective-permute-start | bytes 1572872 | tf_op jit(solution)/shard_map/ppermute | solution.py:448
  176.4 13.3 %copy-start.8 = (bf16[1,1,256,1024]{3,2,1,0:T(8,128)(2,1)S(1)}, bf16[1,1,256,1024]{3,2,1,0:T(8,128)(2,1)}, u32[]{:S(2)}) copy-start(bf16[1,1,256,1024]{3,2,1,0:T(8,128)(2,1)} %get-tuple-element.36) | copy-start | bytes 1572868
  176.4 18.8 %copy-start.7 = (bf16[1,1,256,1024]{3,2,1,0:T(8,128)(2,1)S(1)}, bf16[1,1,256,1024]{3,2,1,0:T(8,128)(2,1)}, u32[]{:S(2)}) copy-start(bf16[1,1,256,1024]{3,2,1,0:T(8,128)(2,1)} %get-tuple-element.35) | copy-start | bytes 1572868
  180.4 50.3 %collective-permute-start.6 = (bf16[2,1,256,1024]{3,2,0,1:T(8,128)(2,1)}, bf16[2,1,256,1024]{3,2,0,1:T(8,128)(2,1)}, u32[]{:S(2)}, u32[]{:S(2)}) collective-permute-start(bf16[2,1,256,1024]{3,2,0,1:T(8,128)(2,1)} %bitcast.37), channel_id=1, source_target_pairs={{0,16},{8,24},{16,0},{24,8},{1,17},{9,25},{17,1},{25,9},{2,18},{10... | collective-permute-start | bytes 3145736 | tf_op jit(solution)/shard_map/ppermute | solution.py:448
  190.7 40.0 %collective-permute-start.9 = (bf16[1,256,1024]{2,1,0:T(8,128)(2,1)}, bf16[1,256,1024]{2,1,0:T(8,128)(2,1)S(1)}, u32[]{:S(2)}, u32[]{:S(2)}) collective-permute-start(bf16[1,256,1024]{2,1,0:T(8,128)(2,1)} %fusion.1), channel_id=1, source_target_pairs={{0,4},{1,5},{2,6},{3,7},{4,0},{5,1},{6,2},{7,3},{8,12},{9,13},{10,... | collective-permute-start | bytes 1572872 | tf_op jit(solution)/shard_map/ppermute | solution.py:439
  196.2 41.8 %collective-permute-start.7 = (bf16[1,256,1024]{2,1,0:T(8,128)(2,1)}, bf16[1,256,1024]{2,1,0:T(8,128)(2,1)S(1)}, u32[]{:S(2)}, u32[]{:S(2)}) collective-permute-start(bf16[1,256,1024]{2,1,0:T(8,128)(2,1)} %fusion), channel_id=1, source_target_pairs={{0,4},{1,5},{2,6},{3,7},{4,0},{5,1},{6,2},{7,3},{8,12},{9,13},{10,... | collective-permute-start | bytes 1572872 | tf_op jit(solution)/shard_map/ppermute | solution.py:439
  (6 other events, 6.5 us)
Sparse Core Ops, SparseCore 0:
  9.6 38.1 all-gather.2
  70.3 37.3 all-gather.4
